TPU v7x, 32 devices: a whole 2x2x4 slice. The times are simulated.
32 devices in a mesh: groups: 2 (over y), dp: 4 (over x, core), tensor: 4 (over z).
Axes of the slice: x: 2, y: 2, z: 4, core: 2. Of those that a mesh axis runs over, the one named last changes fastest.
Arguments:
- hidden_in: bfloat16 [1024, 8192], P(('groups', 'dp'), 'tensor'), parts along dimension 0, may hold values from -48 to 48
- queries: bfloat16 [1024, 4096], P(('groups', 'dp'), 'tensor'), parts along dimension 0, may hold values from -9 to 9
- keys_values: bfloat16 [1024, 2, 512], P(('groups', 'dp')), parts along dimension 0, may hold values from -6 to 6
- out_weight: bfloat16 [4096, 8192], P('tensor'), may hold values from -0.125 to 0.125
- send_rows: int32 [8, 128], P(('groups', 'dp')), parts along dimension 0, may hold values from 0 to 127, each once within a row
- lengths: int32 [8, 8], P(('groups', 'dp')), parts along dimension 0, may hold values from 1 to 32, 128 in all within a row
- block_scales: bfloat16 [1024, 64], P(('groups', 'dp'), 'tensor'), parts along dimension 0, may hold values from 0.0009994507 to 0.019897461
- value_head: bfloat16 [8192], replicated, may hold values from -0.0625 to 0.0625
Outputs:
- restored: float32 [1024, 8192], P(('groups', 'dp'), 'tensor'), parts along dimension 0
- values: float32 [1024], P(('groups', 'dp')), parts along dimension 0
There are 2 independent parts, one for each index of `groups`. A program takes and returns all parts, laid end to end along the dimension named above; an argument that names none is the same for every part. Nothing has to cross between parts.
Inputs may be any that keep to these rules, and one draw needn't show every extreme that they name: `send_rows`: each row names each of 0 to 127 once. Each dp index's 8 lengths sum to 128; the largest is 32.
All inputs are finite; a program needn't handle non-finite values.
Results may differ from a plain program's by a relative error of at most 0.0085.
Values may be sent and summed in bfloat16 or wider, within the bound.
No kernel may reach another device: no remote copies, remote signals or barrier semaphores. Data moves between devices by JAX's collectives and lax.ppermute only.
A program may use at most 64 MiB of HBM per device.

v0:
```python
import jax
import jax.numpy as jnp
from jax import lax
from jax.sharding import PartitionSpec as P

D = 8192
HEADS = 32
KV_HEADS = 4
HD = 128
BLOCK = 128


CLIP_CODE = 448.0
EPS = 1e-06


def segment_of(lengths_here, row_total):
    ends_at = jnp.cumsum(lengths_here)
    position = jnp.arange(row_total, dtype=jnp.int32)
    return jnp.sum((position[:, None] >= ends_at[None, :]).astype(jnp.int32), axis=1)


def attend(moved_query, moved_kv, segment, heads_here):
    row_total = moved_query.shape[0]
    query_heads = moved_query.reshape(row_total, heads_here, HD)
    kv_pair = moved_kv.reshape(row_total, 2, HD)
    scores = jnp.einsum(
        "qhd,kd->hqk", query_heads, kv_pair[:, 0], preferred_element_type=jnp.float32
    ) * HD ** (-0.5)
    position = jnp.arange(row_total, dtype=jnp.int32)
    allowed = (segment[:, None] == segment[None, :]) & (position[:, None] >= position[None, :])
    scores = jnp.where(allowed[None], scores, -jnp.inf)
    peak_score = jnp.max(scores, axis=2, keepdims=True)
    weights = jnp.exp(scores - peak_score)
    weights_low = (weights / jnp.sum(weights, axis=2, keepdims=True)).astype(jnp.bfloat16)
    context = jnp.einsum(
        "hqk,kd->qhd", weights_low, kv_pair[:, 1], preferred_element_type=jnp.float32
    )
    return context.astype(jnp.bfloat16).reshape(row_total, heads_here * HD)


def per_device(
    hidden_in, queries, keys_values, out_weight, send_rows, lengths, block_scales, value_head
):
    row_total = hidden_in.shape[0]
    col_width = hidden_in.shape[1]
    heads_here = queries.shape[1] // HD
    group_size = HEADS // KV_HEADS
    tensor_index = lax.axis_index("tensor")
    kv_head = tensor_index * heads_here // group_size
    kv_local = lax.dynamic_slice_in_dim(keys_values, kv_head * HD, HD, 2).reshape(row_total, 2 * HD)
    send_order = send_rows[0]
    query_out = jnp.take(queries, send_order, axis=0)
    kv_out = jnp.take(kv_local, send_order, axis=0)
    hidden_out = jnp.take(hidden_in, send_order, axis=0)
    segment = segment_of(lengths[0], row_total)
    moved_query, moved_kv, moved_hidden = (
        lax.all_to_all(query_out, "dp", split_axis=0, concat_axis=0, tiled=True),
        lax.all_to_all(kv_out, "dp", split_axis=0, concat_axis=0, tiled=True),
        lax.all_to_all(hidden_out, "dp", split_axis=0, concat_axis=0, tiled=True),
    )
    context = attend(moved_query, moved_kv, segment, heads_here)
    partial_term = jnp.dot(context, out_weight, preferred_element_type=jnp.float32)
    summed = lax.psum_scatter(
        partial_term.astype(jnp.bfloat16), "tensor", scatter_dimension=1, tiled=True
    ).astype(jnp.float32)
    residual = moved_hidden.astype(jnp.float32) + summed
    blocks_here = col_width // BLOCK
    scale_wide = block_scales.astype(jnp.float32)[:, :, None]
    code_block = jnp.clip(
        residual.reshape(row_total, blocks_here, BLOCK) / scale_wide, -CLIP_CODE, CLIP_CODE
    ).astype(jnp.bfloat16)
    restored = code_block.astype(jnp.float32) * scale_wide
    head_table = value_head.astype(jnp.float32).reshape(D // BLOCK, BLOCK)
    piece_codes = lax.all_gather(code_block, "tensor", axis=1, tiled=True)
    piece_scales = lax.all_gather(block_scales, "tensor", axis=1, tiled=True)
    piece_values = piece_codes.astype(jnp.float32) * piece_scales.astype(jnp.float32)[:, :, None]
    power_part = jnp.sum(piece_values * piece_values, axis=(1, 2))
    head_part = jnp.sum(piece_values * head_table[None], axis=(1, 2))
    values = head_part / jnp.sqrt(power_part / D + EPS)
    return (restored.reshape(row_total, col_width), values)


def solution(mesh):
    in_specs = (
        P(("groups", "dp"), "tensor"),
        P(("groups", "dp"), "tensor"),
        P(("groups", "dp"), None, None),
        P("tensor", None),
        P(("groups", "dp"), None),
        P(("groups", "dp"), None),
        P(("groups", "dp"), "tensor"),
        P(),
    )
    out_specs = (P(("groups", "dp"), "tensor"), P(("groups", "dp")))
    return jax.shard_map(
        per_device, mesh=mesh, in_specs=in_specs, out_specs=out_specs, check_vma=False
    )
```

profile of v0, /device:TPU:0, one launch (start us, length us, event | category | flops | bytes accessed | tf_op | source)
XLA Modules:
  0.0 148.6 jit_solution(7662302804834954742)
XLA Ops:
  7.2 0.0 copy-start
  7.2 0.9 constant_dynamic-slice_fusion
  8.2 0.7 fusion.15
  8.8 0.5 broadcast.84
  9.3 1.3 reduce.3
  10.7 0.1 squeeze.12
  10.8 0.8 gather_fusion.1
  11.6 0.7 broadcast_select_fusion.2
  12.3 4.2 %all-to-all-start.1 = ((bf16[4,32,256]{2,1,0:T(8,128)(2,1)}), bf16[4,32,256]{2,1,0:T(8,128)(2,1)S(1)}, u32[]{:S(2)}, u32[]{:S(2)}) async-start(bf16[4,32,256]{2,1,0:T(8,128)(2,1)} %broadcast_select_fusion.2), calls=%async_computation.1 | async-start | bytes 131072 | tf_op jit(solution)/shard_map/all_to_all | solution.py:59
  16.5 2.0 %gather_fusion.2 = bf16[128,1024]{1,0:T(8,128)(2,1)S(1)} fusion(bf16[128,1024]{1,0:T(8,128)(2,1)} %param.9, s32[1024]{0:T(1024)S(1)} %pad_clamp_fusion), kind=kCustom, calls=%fused_computation.2 | custom fusion | bytes 524800 | tf_op jit(solution)/shard_map/jit(_take)/gather | solution.py:53
  18.6 0.8 broadcast_select_fusion.1
  19.4 0.8 reduce-window.8
  20.2 0.1 convert_reduce_fusion
  20.3 0.1 fusion.11
  20.4 0.3 all-to-all-done.1
  20.6 3.4 %all-to-all-start.2 = ((bf16[4,32,1024]{2,1,0:T(8,128)(2,1)}), bf16[4,32,1024]{2,1,0:T(8,128)(2,1)S(1)}, u32[]{:S(2)}, u32[]{:S(2)}) async-start(bf16[4,32,1024]{2,1,0:T(8,128)(2,1)} %broadcast_select_fusion.1), calls=%async_computation.2 | async-start | bytes 524288 | tf_op jit(solution)/shard_map/all_to_all | solution.py:58
  24.1 0.0 reduce-scatter.2.cloned.1.call-start
  24.1 0.1 fusion.19
  24.2 0.1 copy.27
  24.4 5.7 %all-to-all-done.2 = bf16[4,32,1024]{2,1,0:T(8,128)(2,1)S(1)} async-done(((bf16[4,32,1024]{2,1,0:T(8,128)(2,1)}), bf16[4,32,1024]{2,1,0:T(8,128)(2,1)S(1)}, u32[]{:S(2)}, u32[]{:S(2)}) %all-to-all-start.2) | async-done | bytes 262176 | tf_op jit(solution)/shard_map/all_to_all | solution.py:58
  30.1 0.2 fusion.4
  30.4 0.3 fusion.20
  30.7 0.3 convolution_convert_fusion.1
  31.0 9.6 %convolution_convert_fusion = bf16[128,8192]{1,0:T(8,128)(2,1)} fusion(bf16[128,1024]{0,1:T(8,128)(2,1)S(1)} %bitcast.74, bf16[1024,8192]{1,0:T(8,128)(2,1)} %param.11), kind=kOutput, calls=%fused_computation.4 | convolution fusion | flops 2148532224 | bytes 19136512 | tf_op jit(solution)/shard_map/dot_general | solution.py:63
  40.6 0.0 copy-start.2
  40.6 0.0 reduce-scatter.2.cloned.1.call-update
  40.6 0.0 copy-done
  40.6 0.9 gather_fusion
  41.6 0.9 broadcast_select_fusion
  42.5 3.5 %all-to-all-start = ((bf16[4,32,2048]{2,1,0:T(8,128)(2,1)}), bf16[4,32,2048]{2,1,0:T(8,128)(2,1)S(1)}, u32[]{:S(2)}, u32[]{:S(2)}) async-start(bf16[4,32,2048]{2,1,0:T(8,128)(2,1)} %broadcast_select_fusion), calls=%async_computation | async-start | bytes 1048576 | tf_op jit(solution)/shard_map/all_to_all | solution.py:60
  45.9 0.0 all-gather.2.cloned.1.call-start
  46.0 0.0 copy-done.2
  46.0 0.1 copy.24
  46.1 8.6 %all-to-all-done = bf16[4,32,2048]{2,1,0:T(8,128)(2,1)S(1)} async-done(((bf16[4,32,2048]{2,1,0:T(8,128)(2,1)}), bf16[4,32,2048]{2,1,0:T(8,128)(2,1)S(1)}, u32[]{:S(2)}, u32[]{:S(2)}) %all-to-all-start) | async-done | bytes 524320 | tf_op jit(solution)/shard_map/all_to_all | solution.py:60
  54.8 30.8 %reduce-scatter.2.cloned.1.call-done = bf16[128,2048]{1,0:T(8,128)(2,1)} async-done(((bf16[128,8192]{1,0:T(8,128)(2,1)}), bf16[128,2048]{1,0:T(8,128)(2,1)}) %reduce-scatter.2.cloned.1.call-update) | async-done | bytes 524304 | tf_op jit(solution)/shard_map/reduce_scatter | solution.py:64
  85.5 0.3 div.43
  85.8 0.0 copy-start.1
  85.9 2.6 %fusion.9 = (f32[16,8,16,128]{3,1,2,0:T(8,128)S(1)}, f32[128,2048]{1,0:T(8,128)}) fusion(bf16[128,2048]{1,0:T(8,128)(2,1)} %reduce-scatter.2.cloned.1.call-done, bf16[4,32,2048]{2,1,0:T(8,128)(2,1)S(1)} %all-to-all-done, f32[16,8,16,128]{3,2,1,0:T(8,128)S(1)} %bitcast.68), kind=kLoop, calls=%fused_computation.22 | loop fusion | flops 2097152 | bytes 4194304
  88.5 0.2 copy.32
  88.7 1.1 fusion.6
  89.8 0.0 all-gather.2.cloned.1.call-update
  89.8 13.2 %all_gather.7 = bf16[128,64]{0,1:T(8,128)(2,1)S(1)} all-gather(bf16[128,16]{0,1:T(8,128)(2,1)S(1)} %copy-done.2), channel_id=1, replica_groups=mesh['groups'=2,'dp'=4,'tensor'=4] {'tensor'}, dimensions={1}, use_global_device_ids=true | all-gather | bytes 20480 | tf_op jit(solution)/shard_map/all_gather | solution.py:76
  103.0 0.1 copy.25
  103.1 0.0 copy-done.1
  103.1 32.4 %all-gather.2.cloned.1.call-done = bf16[128,64,128]{2,1,0:T(8,128)(2,1)} async-done(((bf16[128,16,128]{2,1,0:T(8,128)(2,1)}), bf16[128,64,128]{2,1,0:T(8,128)(2,1)}) %all-gather.2.cloned.1.call-update) | async-done | bytes 2097168 | tf_op jit(solution)/shard_map/all_gather | solution.py:75
  135.5 5.7 %multiply_reduce_fusion = (f32[128]{0:T(128)S(1)}, f32[128]{0:T(128)S(1)}) fusion(bf16[128,64,128]{2,1,0:T(8,128)(2,1)} %all-gather.2.cloned.1.call-done, f32[128,64]{1,0:T(8,128)S(1)} %copy.25, f32[64,128]{1,0:T(8,128)S(1)} %bitcast_convert_fusion), kind=kLoop, calls=%fused_computation.5 | loop fusion | flops 6291200 | bytes 2163712 | tf_op jit(solution)/shard_map/reduce_sum | solution.py:78
  141.2 0.5 rsqrt_multiply_fusion
  (6 shorter events, 0.1 us)
Async XLA Ops:
  7.2 33.4 %copy-start = (bf16[128,2048]{1,0:T(8,128)(2,1)S(1)}, bf16[128,2048]{1,0:T(8,128)(2,1)}, u32[]{:S(2)}) copy-start(bf16[128,2048]{1,0:T(8,128)(2,1)} %param.8) | copy-start | bytes 1572868
  12.3 8.3 %all-to-all-start.1 = ((bf16[4,32,256]{2,1,0:T(8,128)(2,1)}), bf16[4,32,256]{2,1,0:T(8,128)(2,1)S(1)}, u32[]{:S(2)}, u32[]{:S(2)}) async-start(bf16[4,32,256]{2,1,0:T(8,128)(2,1)} %broadcast_select_fusion.2), calls=%async_computation.1 | async-start | bytes 131072 | tf_op jit(solution)/shard_map/all_to_all | solution.py:59
  20.6 9.4 %all-to-all-start.2 = ((bf16[4,32,1024]{2,1,0:T(8,128)(2,1)}), bf16[4,32,1024]{2,1,0:T(8,128)(2,1)S(1)}, u32[]{:S(2)}, u32[]{:S(2)}) async-start(bf16[4,32,1024]{2,1,0:T(8,128)(2,1)} %broadcast_select_fusion.1), calls=%async_computation.2 | async-start | bytes 524288 | tf_op jit(solution)/shard_map/all_to_all | solution.py:58
  24.1 61.4 %reduce-scatter.2.cloned.1.call-start = ((), (), s32[]{:S(2)}) async-start(), calls=%async_computation.4 | async-start | bytes 2621440 | tf_op jit(solution)/shard_map/reduce_scatter | solution.py:64
  40.6 5.4 %copy-start.2 = (bf16[128,16]{0,1:T(8,128)(2,1)S(1)}, bf16[128,16]{0,1:T(8,128)(2,1)}, u32[]{:S(2)}) copy-start(bf16[128,16]{0,1:T(8,128)(2,1)} %param.14) | copy-start | bytes 12292
  42.5 12.3 %all-to-all-start = ((bf16[4,32,2048]{2,1,0:T(8,128)(2,1)}), bf16[4,32,2048]{2,1,0:T(8,128)(2,1)S(1)}, u32[]{:S(2)}, u32[]{:S(2)}) async-start(bf16[4,32,2048]{2,1,0:T(8,128)(2,1)} %broadcast_select_fusion), calls=%async_computation | async-start | bytes 1048576 | tf_op jit(solution)/shard_map/all_to_all | solution.py:60
  45.9 89.6 %all-gather.2.cloned.1.call-start = ((), (), s32[]{:S(2)}) async-start(), calls=%async_computation.5 | async-start | bytes 2621440 | tf_op jit(solution)/shard_map/all_gather | solution.py:75
  85.8 17.3 %copy-start.1 = (bf16[8192]{0:T(1024)(128)(2,1)S(1)}, bf16[8192]{0:T(1024)(128)(2,1)}, u32[]{:S(2)}) copy-start(bf16[8192]{0:T(1024)(128)(2,1)} %param.15) | copy-start | bytes 49156
Sparse Core Ops, SparseCore 0:
  40.7 44.7 reduce-scatter.1
  90.0 45.5 all-gather.1
where the time goes:
time: 149 us
  waiting for transfers between devices  77.8 us (52%)
  other arithmetic  15.4 us (10%)
  between operations  14.2 us (10%)
  blocking collectives  13.2 us (9%)
  starting transfers between devices  11.2 us (8%)
  matrix products  10.4 us (7%)
  local copies, waits for them, and re-layouts  6.37 us (4%)
    all_gather x1, waiting for transfers between devices, per_device(): piece_codes = lax.all_gather(code_block, 'tensor', axis=1, tiled=True)  32.4 us
    reduce_scatter x1, waiting for transfers between devices, per_device(): lax.psum_scatter(partial_term.astype(jnp.bfloat16), 'tensor', scatter_dim...  30.8 us
    all_gather x1, blocking collectives, per_device(): piece_scales = lax.all_gather(block_scales, 'tensor', axis=1, tiled=True)  13.2 us
    dot_general x1, matrix products, per_device(): jnp.dot(context, out_weight, preferred_element_type=jnp.float32)  9.59 us
    all_to_all x1, waiting for transfers between devices, per_device(): lax.all_to_all(hidden_out, 'dp', split_axis=0, concat_axis=0, tiled=True)  8.64 us
    all_to_all x1, waiting for transfers between devices, per_device(): lax.all_to_all(query_out, 'dp', split_axis=0, concat_axis=0, tiled=True)  5.71 us
    reduce_sum x1, other arithmetic, per_device(): power_part = jnp.sum(piece_values * piece_values, axis=(1, 2))  5.67 us
    all_to_all x1, starting transfers between devices, per_device(): lax.all_to_all(kv_out, 'dp', split_axis=0, concat_axis=0, tiled=True)  4.21 us
  transfers between devices with their start and end apart: 5, of which 5 were waited for; matrix products, arithmetic and copies ran while one was open for 4% of the time, Pallas kernels for 0%

commit v1 on v0

v1 whole, which is shorter than its diff:
```python
import functools

import jax
import jax.numpy as jnp
from jax import lax
from jax.experimental import pallas as pl
from jax.experimental.pallas import tpu as pltpu
from jax.sharding import PartitionSpec as P

D = 8192
HEADS = 32
KV_HEADS = 4
HD = 128
BLOCK = 128
GROUP = HEADS // KV_HEADS

CLIP_CODE = 448.0
EPS = 1e-06
F32 = jnp.float32
BF16 = jnp.bfloat16
VMEM = pl.BlockSpec(memory_space=pltpu.VMEM)
SMEM = pl.BlockSpec(memory_space=pltpu.SMEM)
ANY = pl.BlockSpec(memory_space=pl.ANY)


def params(mib):
    return pltpu.CompilerParams(vmem_limit_bytes=mib << 20)


def one_hot_columns(send_ref):
    rows = send_ref.shape[1]
    row_id = lax.broadcasted_iota(jnp.int32, (rows, rows), 0)
    return (row_id == send_ref[...]).astype(F32).astype(BF16)


def reorder(one_hot, values):
    return lax.dot_general(
        one_hot, values, (((0,), (0,)), ((), ())), preferred_element_type=F32
    ).astype(BF16)


def pack_qkv_kernel(heads_here, send_ref, q_ref, kv_ref, *refs):
    outs, buf = refs[:-1], refs[-1]
    me = lax.axis_index("dp")
    kv_head = lax.axis_index("tensor") * heads_here // GROUP
    one_hot = one_hot_columns(send_ref)
    width = q_ref.shape[1]
    buf[:, :width] = reorder(one_hot, q_ref[...])
    for pair in range(2):
        start = pl.multiple_of(kv_head * HD, HD)
        part = kv_ref[:, pair, pl.ds(start, HD)]
        buf[:, width + pair * HD : width + (pair + 1) * HD] = reorder(one_hot, part)
    share = outs[0].shape[0]
    for k, out in enumerate(outs):
        start = pl.multiple_of((me ^ k) * share, share)
        out[...] = buf[pl.ds(start, share), :]


def pack_qkv(send_rows, queries, keys_values, n_dp):
    rows, width = queries.shape
    out = jax.ShapeDtypeStruct((rows // n_dp, width + 2 * HD), BF16)
    return pl.pallas_call(
        functools.partial(pack_qkv_kernel, width // HD),
        out_shape=[out] * n_dp,
        in_specs=[VMEM] * 3,
        out_specs=[VMEM] * n_dp,
        scratch_shapes=[pltpu.VMEM((rows, width + 2 * HD), BF16)],
        name="pack_qkv",
    )(send_rows, queries, keys_values)


def pack_hidden_kernel(send_ref, h_ref, *refs):
    outs, buf = refs[:-1], refs[-1]
    me = lax.axis_index("dp")
    buf[...] = reorder(one_hot_columns(send_ref), h_ref[...])
    share = outs[0].shape[0]
    for k, out in enumerate(outs):
        start = pl.multiple_of((me ^ k) * share, share)
        out[...] = buf[pl.ds(start, share), :]


def pack_hidden(send_rows, hidden, n_dp):
    rows, width = hidden.shape
    out = jax.ShapeDtypeStruct((rows // n_dp, width), BF16)
    return pl.pallas_call(
        pack_hidden_kernel,
        out_shape=[out] * n_dp,
        in_specs=[VMEM] * 2,
        out_specs=[VMEM] * n_dp,
        scratch_shapes=[pltpu.VMEM((rows, width), BF16)],
        name="pack_hidden",
    )(send_rows, hidden)


def attend_kernel(len_ref, *refs):
    pieces, out, buf = refs[:-2], refs[-2], refs[-1]
    me = lax.axis_index("dp")
    share = pieces[0].shape[0]
    for k, piece in enumerate(pieces):
        start = pl.multiple_of((me ^ k) * share, share)
        buf[pl.ds(start, share), :] = piece[...]
    rows, width = out.shape
    row_id = lax.broadcasted_iota(jnp.int32, (rows, rows), 0)
    col_id = lax.broadcasted_iota(jnp.int32, (rows, rows), 1)
    row_seg = jnp.zeros((rows, rows), jnp.int32)
    col_seg = jnp.zeros((rows, rows), jnp.int32)
    end = jnp.int32(0)
    for r in range(len_ref.shape[1]):
        end = end + len_ref[0, r]
        row_seg += (row_id >= end).astype(jnp.int32)
        col_seg += (col_id >= end).astype(jnp.int32)
    allowed = (row_seg == col_seg) & (row_id >= col_id)
    keys = buf[:, width : width + HD]
    values = buf[:, width + HD : width + 2 * HD]
    for h in range(width // HD):
        cols = slice(h * HD, (h + 1) * HD)
        scores = lax.dot_general(
            buf[:, cols], keys, (((1,), (1,)), ((), ())), preferred_element_type=F32
        ) * HD ** (-0.5)
        scores = jnp.where(allowed, scores, -jnp.inf)
        peak = jnp.max(scores, axis=1, keepdims=True)
        weights = jnp.exp(scores - peak)
        low = (weights / jnp.sum(weights, axis=1, keepdims=True)).astype(BF16)
        out[:, cols] = jnp.dot(low, values, preferred_element_type=F32).astype(BF16)


def attend(lengths, pieces):
    n_dp = len(pieces)
    share, wide = pieces[0].shape
    rows, width = share * n_dp, wide - 2 * HD
    return pl.pallas_call(
        attend_kernel,
        out_shape=jax.ShapeDtypeStruct((rows, width), BF16),
        in_specs=[SMEM] + [VMEM] * n_dp,
        out_specs=VMEM,
        scratch_shapes=[pltpu.VMEM((rows, wide), BF16)],
        name="attend",
    )(lengths, *pieces)


def step_kernel(n, chunks, step, with_recv, ctx_ref, w_ref, *refs):
    if with_recv:
        recv_r, recv_l, out_r, out_l, w_buf, sem = refs
    else:
        out_r, out_l, w_buf, sem = refs
    width = out_r.shape[1]
    i = lax.axis_index("tensor")
    turn, part = step // chunks, step % chunks
    right = jnp.minimum(n - 1 - turn + i, n - 1) * chunks + part
    left = jnp.maximum(turn - (n - 1 - i), 0) * chunks + part
    copies = []
    for side, block in enumerate((right, left)):
        start = pl.multiple_of(block * width, width)
        copies.append(
            pltpu.make_async_copy(w_ref.at[:, pl.ds(start, width)], w_buf.at[side], sem.at[side])
        )
        copies[-1].start()
    for side, out in enumerate((out_r, out_l)):
        copies[side].wait()
        term = jnp.dot(ctx_ref[...], w_buf[side], preferred_element_type=F32)
        if with_recv:
            term = term + (recv_r, recv_l)[side][...].astype(F32)
        out[...] = term.astype(BF16)


def chain_step(n, chunks, step, context, weight, recv):
    rows, depth = context.shape
    width = weight.shape[1] // (n * chunks)
    out = jax.ShapeDtypeStruct((rows, width), BF16)
    return pl.pallas_call(
        functools.partial(step_kernel, n, chunks, step, recv is not None),
        out_shape=[out] * 2,
        in_specs=[VMEM, ANY] + [VMEM] * (2 if recv is not None else 0),
        out_specs=[VMEM] * 2,
        scratch_shapes=[pltpu.VMEM((2, depth, width), BF16), pltpu.SemaphoreType.DMA((2,))],
        compiler_params=params(16),
        cost_estimate=pl.CostEstimate(
            flops=4 * rows * depth * width, bytes_accessed=4 * depth * width, transcendentals=0
        ),
        name="chain_step",
    )(context, weight, *(recv or ()))


def own_kernel(ctx_ref, w_ref, out, w_buf, sem):
    width = out.shape[1]
    start = pl.multiple_of(lax.axis_index("tensor") * width, width)
    copy = pltpu.make_async_copy(w_ref.at[:, pl.ds(start, width)], w_buf, sem)
    copy.start()
    copy.wait()
    out[...] = jnp.dot(ctx_ref[...], w_buf[...], preferred_element_type=F32)


def own_term(n, context, weight):
    rows, depth = context.shape
    width = weight.shape[1] // n
    return pl.pallas_call(
        own_kernel,
        out_shape=jax.ShapeDtypeStruct((rows, width), F32),
        in_specs=[VMEM, ANY],
        out_specs=VMEM,
        scratch_shapes=[pltpu.VMEM((depth, width), BF16), pltpu.SemaphoreType.DMA],
        compiler_params=params(16),
        cost_estimate=pl.CostEstimate(
            flops=2 * rows * depth * width, bytes_accessed=2 * depth * width, transcendentals=0
        ),
        name="own_term",
    )(context, weight)


def finish_kernel(n_dp, part, width, recv_r, recv_l, own, scale_ref, head_ref, *refs):
    pieces = refs[:n_dp]
    out, sums = refs[-2:]
    earlier = refs[n_dp + 1] if part else None
    me = lax.axis_index("dp")
    i = lax.axis_index("tensor")
    share = pieces[0].shape[0]
    rows, cols = recv_r.shape
    base = part * cols
    for k, piece in enumerate(pieces):
        start = pl.multiple_of((me ^ k) * share, share)
        out[pl.ds(start, share), :] = piece[:, base : base + cols].astype(F32)
    power = jnp.zeros((rows, BLOCK), F32)
    dots = jnp.zeros((rows, BLOCK), F32)
    for b in range(cols // BLOCK):
        here = slice(b * BLOCK, (b + 1) * BLOCK)
        wide = slice(base + b * BLOCK, base + (b + 1) * BLOCK)
        block = base // BLOCK + b
        scale = scale_ref[:, block : block + 1].astype(F32)
        summed = recv_r[:, here].astype(F32) + recv_l[:, here].astype(F32) + own[:, wide]
        residual = out[:, here] + summed
        code = jnp.clip(residual / scale, -CLIP_CODE, CLIP_CODE).astype(BF16)
        restored = code.astype(F32) * scale
        out[:, here] = restored
        power += restored * restored
        start = pl.multiple_of(i * width + base + b * BLOCK, BLOCK)
        dots += restored * head_ref[:, pl.ds(start, BLOCK)].astype(F32)
    total = jnp.concatenate(
        [
            jnp.sum(jnp.transpose(power), axis=0, keepdims=True),
            jnp.sum(jnp.transpose(dots), axis=0, keepdims=True),
            jnp.zeros((6, rows), F32),
        ],
        axis=0,
    )
    if part:
        total = total + earlier[...]
    sums[...] = total


def finish(part, recv_r, recv_l, own, scales, head_row, pieces, before):
    rows, cols = recv_r.shape
    width = own.shape[1]
    n_dp = len(pieces)
    out_spec = pl.BlockSpec((rows, cols), lambda g: (0, part))
    whole = lambda x: pl.BlockSpec(x.shape, lambda g: (0,) * x.ndim)
    args = [recv_r, recv_l, own, scales, head_row, *pieces]
    specs = [whole(x) for x in args]
    aliases = {}
    if before is not None:
        aliases = {len(args): 0}
        args += list(before)
        specs += [ANY, whole(before[1])]
    return pl.pallas_call(
        functools.partial(finish_kernel, n_dp, part, width),
        grid=(1,),
        out_shape=[jax.ShapeDtypeStruct((rows, width), F32), jax.ShapeDtypeStruct((8, rows), F32)],
        in_specs=specs,
        out_specs=[out_spec, pl.BlockSpec((8, rows), lambda g: (0, 0))],
        input_output_aliases=aliases,
        compiler_params=params(32),
        name="finish",
    )(*args)


def exchange(pieces, axis, n):
    return [pieces[0]] + [
        lax.ppermute(pieces[k], axis, [(i, i ^ k) for i in range(n)]) for k in range(1, n)
    ]


def total_over(values, axis, n):
    done = 1
    while done < n:
        radix = min(4, n // done)
        got = [values] + [
            lax.ppermute(values, axis, [(i, i ^ (k * done)) for i in range(n)])
            for k in range(1, radix)
        ]
        values = got[0] + got[1] if radix == 2 else (got[0] + got[1]) + (got[2] + got[3])
        done *= radix
    return values


def per_device(
    n_dp, n, hidden_in, queries, keys_values, out_weight, send_rows, lengths, block_scales, value_head
):
    chunks = 2
    moved = exchange(pack_qkv(send_rows, queries, keys_values, n_dp), "dp", n_dp)
    hidden = exchange(pack_hidden(send_rows, hidden_in, n_dp), "dp", n_dp)
    context = attend(lengths, moved)
    recv = []
    own = None
    for step in range((n - 1) * chunks):
        pair = chain_step(n, chunks, step, context, out_weight, recv[step - chunks] if step >= chunks else None)
        turn = step // chunks
        recv.append(
            (
                lax.ppermute(pair[0], "tensor", [(i, i + 1) for i in range(n - 1) if turn >= i]),
                lax.ppermute(
                    pair[1], "tensor", [(n - 1 - i, n - 2 - i) for i in range(n - 1) if turn >= i]
                ),
            )
        )
    own = own_term(n, context, out_weight)
    head_row = value_head.reshape(1, D)
    result = None
    for part in range(chunks):
        recv_r, recv_l = recv[(n - 2) * chunks + part]
        result = finish(part, recv_r, recv_l, own, block_scales, head_row, hidden, result)
    restored, sums = result
    sums = total_over(sums, "tensor", n)
    values = sums[1] / jnp.sqrt(sums[0] / D + EPS)
    return restored, values


def solution(mesh):
    in_specs = (
        P(("groups", "dp"), "tensor"),
        P(("groups", "dp"), "tensor"),
        P(("groups", "dp"), None, None),
        P("tensor", None),
        P(("groups", "dp"), None),
        P(("groups", "dp"), None),
        P(("groups", "dp"), "tensor"),
        P(),
    )
    out_specs = (P(("groups", "dp"), "tensor"), P(("groups", "dp")))
    return jax.shard_map(
        functools.partial(per_device, mesh.shape["dp"], mesh.shape["tensor"]),
        mesh=mesh,
        in_specs=in_specs,
        out_specs=out_specs,
        check_vma=False,
    )
```

time: 149 us -> 93.9 us (0.63)
  waiting for transfers between devices: 77.8 us -> 10.2 us
  starting transfers between devices: 11.2 us -> 39.4 us
  Pallas kernels: 0 us -> 23.2 us
  other arithmetic: 15.4 us -> 0.53 us
  between operations: 14.2 us -> 0.94 us
  blocking collectives: 13.2 us -> 0 us
  local copies, waits for them, and re-layouts: 6.37 us -> 19 us
  matrix products: 10.4 us -> 0 us
    ppermute x0 -> x21, starting transfers between devices: none -> 39.4 us  [the longest x6 24.5 us: per_device(): lax.ppermute(pair[0], 'tensor', [(i, i + 1) for i in range(n - 1) if turn...]
    all_gather x1 -> x0, waiting for transfers between devices: 32.4 us -> none  [per_device(): piece_codes = lax.all_gather(code_block, 'tensor', axis=1, tiled=True)]
    reduce_scatter x1 -> x0, waiting for transfers between devices: 30.8 us -> none  [per_device(): lax.psum_scatter(partial_term.astype(jnp.bfloat16), 'tensor', scatter_dim...]
    pallas_call x0 -> x12, Pallas kernels: none -> 23.2 us  [the longest x6 10.4 us: chain_step(): pl.pallas_call(functools.partial(step_kernel, n, chunks, step, recv is no...]
    unnamed x11 -> x25, local copies, waits for them, and re-layouts: 0.88 us -> 19 us
    all_to_all x3 -> x0, waiting for transfers between devices: 14.6 us -> none  [the longest x1 8.64 us: per_device(): lax.all_to_all(hidden_out, 'dp', split_axis=0, concat_axis=0, tiled=True)]
    all_gather x1 -> x0, blocking collectives: 13.2 us -> none  [per_device(): piece_scales = lax.all_gather(block_scales, 'tensor', axis=1, tiled=True)]
    all_to_all x3 -> x0, starting transfers between devices: 11.1 us -> none  [the longest x1 4.21 us: per_device(): lax.all_to_all(kv_out, 'dp', split_axis=0, concat_axis=0, tiled=True)]
  transfers between devices with their start and end apart: 5 -> 21, of which waited for: 5 -> 5; matrix products, arithmetic and copies ran while one was open for 4% -> 0% of each run, Pallas kernels for 0% -> 15%
where the time goes in v1:
time: 93.9 us; the launch traced here: 93.3 us
  starting transfers between devices  39.4 us (42%)
  Pallas kernels  23.2 us (25%)
  local copies, waits for them, and re-layouts  19 us (20%)
  waiting for transfers between devices  10.2 us (11%)
  between operations  0.94 us (1%)
    ppermute x6, starting transfers between devices, per_device(): lax.ppermute(pair[0], 'tensor', [(i, i + 1) for i in range(n - 1) if turn...  24.5 us
    unnamed x25, local copies, waits for them, and re-layouts  19 us
    pallas_call x6, Pallas kernels, chain_step(): pl.pallas_call(functools.partial(step_kernel, n, chunks, step, recv is no...  10.4 us
    ppermute x6, starting transfers between devices, per_device(): lax.ppermute(pair[1], 'tensor', [(n - 1 - i, n - 2 - i) for i in range(n...  5.56 us
    ppermute x6, starting transfers between devices, exchange(): lax.ppermute(pieces[k], axis, [(i, i ^ k) for i in range(n)])  4.72 us
    ppermute x6, waiting for transfers between devices, exchange(): lax.ppermute(pieces[k], axis, [(i, i ^ k) for i in range(n)])  4.65 us
    ppermute x3, starting transfers between devices, total_over(): lax.ppermute(values, axis, [(i, i ^ k * done) for i in range(n)])  4.65 us
    pallas_call x1, Pallas kernels, attend(): pl.pallas_call(attend_kernel, out_shape=jax.ShapeDtypeStruct((rows, width...  4.43 us
  transfers between devices with their start and end apart: 21, of which 5 were waited for; matrix products, arithmetic and copies ran while one was open for 0% of the time, Pallas kernels for 15%

profile of v1, /device:TPU:0, one launch (start us, length us, event | category | flops | bytes accessed | tf_op | source)
XLA Modules:
  0.0 93.3 jit_solution(5560257474271375965)
XLA Ops:
  0.6 2.1 %pack_qkv.1 = (bf16[32,1280]{1,0:T(8,128)(2,1)}, bf16[32,1280]{1,0:T(8,128)(2,1)}, bf16[32,1280]{1,0:T(8,128)(2,1)}, bf16[32,1280]{1,0:T(8,128)(2,1)}) custom-call(s32[1,128]{1,0:T(1,128)} %send_ref.3, bf16[128,1024]{1,0:T(8,128)(2,1)} %q_ref.1, bf16[128,2,512]{2,1,0:T(2,128)(2,1)} %kv_ref.1), custom_call_target="tpu_custom_call" | custom-call | tf_op jit(solution)/shard_map/pack_qkv/pallas_call | solution.py:62
  2.7 0.5 collective-permute-start
  3.2 2.5 %collective-permute-start.1 = (bf16[32,1280]{1,0:T(8,128)(2,1)}, bf16[32,1280]{1,0:T(8,128)(2,1)S(1)}, u32[]{:S(2)}, u32[]{:S(2)}) collective-permute-start(bf16[32,1280]{1,0:T(8,128)(2,1)} %get-tuple-element.28), channel_id=1, source_target_pairs={{0,8},{4,12},{8,0},{12,4},{1,9},{5,13},{9,1},{13,5},{2,10},{6,14},... | collective-permute-start | bytes 245768 | tf_op jit(solution)/shard_map/ppermute | solution.py:277
  5.7 0.1 collective-permute-start.2
  5.8 0.0 collective-permute-done.refs_1_
  5.8 3.2 %collective-permute-done.1.refs_2_ = bf16[32,1280]{1,0:T(8,128)(2,1)S(1)} collective-permute-done((bf16[32,1280]{1,0:T(8,128)(2,1)}, bf16[32,1280]{1,0:T(8,128)(2,1)S(1)}, u32[]{:S(2)}, u32[]{:S(2)}) %collective-permute-start.1) | collective-permute-done | bytes 81952 | tf_op jit(solution)/shard_map/ppermute | solution.py:277
  9.1 1.4 %collective-permute-done.2.refs_3_ = bf16[32,1280]{1,0:T(8,128)(2,1)S(1)} collective-permute-done((bf16[32,1280]{1,0:T(8,128)(2,1)}, bf16[32,1280]{1,0:T(8,128)(2,1)S(1)}, u32[]{:S(2)}, u32[]{:S(2)}) %collective-permute-start.2) | collective-permute-done | bytes 81952 | tf_op jit(solution)/shard_map/ppermute | solution.py:277
  10.5 0.6 copy-done.8
  11.1 4.4 %attend.1.ctx_ref = bf16[128,1024]{1,0:T(8,128)(2,1)} custom-call(s32[1,8]{1,0:T(1,128)} %len_ref.1, bf16[32,1280]{1,0:T(8,128)(2,1)} %get-tuple-element.26.refs_0_, bf16[32,1280]{1,0:T(8,128)(2,1)} %copy-done.6, bf16[32,1280]{1,0:T(8,128)(2,1)} %copy-done.7, bf16[32,1280]{1,0:T(8,128)(2,1)} %copy-done.8), custom_call_target="tpu_custom_call" | custom-call | tf_op jit(solution)/shard_map/attend/pallas_call | solution.py:131
  15.5 5.8 %copy-done = bf16[1024,8192]{1,0:T(8,128)(2,1)S(1)} copy-done((bf16[1024,8192]{1,0:T(8,128)(2,1)S(1)}, bf16[1024,8192]{1,0:T(8,128)(2,1)}, u32[]{:S(2)}) %copy-start) | copy-done | bytes 16777240
  21.3 0.9 %copy-done.3 = bf16[128,1024]{1,0:T(8,128)(2,1)S(1)} copy-done((bf16[128,1024]{1,0:T(8,128)(2,1)S(1)}, bf16[128,1024]{1,0:T(8,128)(2,1)}, u32[]{:S(2)}) %copy-start.3) | copy-done | bytes 262168
  22.3 1.7 %chain_step.9 = (bf16[128,1024]{1,0:T(8,128)(2,1)S(1)}, bf16[128,1024]{1,0:T(8,128)(2,1)S(1)}) custom-call(bf16[128,1024]{1,0:T(8,128)(2,1)S(1)} %copy-done.3, bf16[1024,8192]{1,0:T(8,128)(2,1)S(1)} %copy-done), custom_call_target="tpu_custom_call" | custom-call | flops 536870912 | bytes 4194304 | tf_op jit(solution)/shard_map/chain_step/pallas_call | solution.py:170
  24.0 3.6 %collective-permute-start.12 = (bf16[128,1024]{1,0:T(8,128)(2,1)S(1)}, bf16[128,1024]{1,0:T(8,128)(2,1)S(1)}, u32[]{:S(2)}, u32[]{:S(2)}) collective-permute-start(bf16[128,1024]{1,0:T(8,128)(2,1)S(1)} %get-tuple-element.40), channel_id=1, source_target_pairs={{0,1},{4,5},{8,9},{12,13},{16,17},{20,21},{24,25},{28,29}} | collective-permute-start | bytes 786440 | tf_op jit(solution)/shard_map/ppermute | solution.py:308
  27.6 0.7 collective-permute-start.13
  28.3 1.7 %chain_step.6 = (bf16[128,1024]{1,0:T(8,128)(2,1)S(1)}, bf16[128,1024]{1,0:T(8,128)(2,1)S(1)}) custom-call(bf16[128,1024]{1,0:T(8,128)(2,1)S(1)} %copy-done.3, bf16[1024,8192]{1,0:T(8,128)(2,1)S(1)} %copy-done), custom_call_target="tpu_custom_call" | custom-call | flops 536870912 | bytes 4194304 | tf_op jit(solution)/shard_map/chain_step/pallas_call | solution.py:170
  30.1 1.3 %collective-permute-start.3 = (bf16[128,1024]{1,0:T(8,128)(2,1)S(1)}, bf16[128,1024]{1,0:T(8,128)(2,1)S(1)}, u32[]{:S(2)}, u32[]{:S(2)}) collective-permute-start(bf16[128,1024]{1,0:T(8,128)(2,1)S(1)} %get-tuple-element.30), channel_id=1, source_target_pairs={{0,1},{4,5},{8,9},{12,13},{16,17},{20,21},{24,25},{28,29}} | collective-permute-start | bytes 786440 | tf_op jit(solution)/shard_map/ppermute | solution.py:308
  31.4 0.0 copy-start.4
  31.4 0.8 collective-permute-start.4
  32.2 2.1 %collective-permute-done.12.refs_0_ = bf16[128,1024]{1,0:T(8,128)(2,1)S(1)} collective-permute-done((bf16[128,1024]{1,0:T(8,128)(2,1)S(1)}, bf16[128,1024]{1,0:T(8,128)(2,1)S(1)}, u32[]{:S(2)}, u32[]{:S(2)}) %collective-permute-start.12) | collective-permute-done | bytes 262176 | tf_op jit(solution)/shard_map/ppermute | solution.py:308
  34.3 0.0 collective-permute-done.13.refs_1_
  34.3 1.7 %chain_step.10 = (bf16[128,1024]{1,0:T(8,128)(2,1)S(1)}, bf16[128,1024]{1,0:T(8,128)(2,1)S(1)}) custom-call(bf16[128,1024]{1,0:T(8,128)(2,1)S(1)} %copy-done.3, bf16[1024,8192]{1,0:T(8,128)(2,1)S(1)} %copy-done, bf16[128,1024]{1,0:T(8,128)(2,1)S(1)} %collective-permute-done.12.refs_0_, bf16[128,1024]{1,0:T(8,128)(2,1)S(1)} %collective-permute-done.13.refs_1_), custom_call_target="tpu_custom_call" | custom-call | flops 536870912 | bytes 4194304 | tf_op jit(solution)/shard_map/chain_step/pallas_call | solution.py:170
  36.0 4.4 %collective-permute-start.14 = (bf16[128,1024]{1,0:T(8,128)(2,1)S(1)}, bf16[128,1024]{1,0:T(8,128)(2,1)S(1)}, u32[]{:S(2)}, u32[]{:S(2)}) collective-permute-start(bf16[128,1024]{1,0:T(8,128)(2,1)S(1)} %get-tuple-element.42), channel_id=1, source_target_pairs={{0,1},{1,2},{4,5},{5,6},{8,9},{9,10},{12,13},{13,14},{16,17},{17,1... | collective-permute-start | bytes 786440 | tf_op jit(solution)/shard_map/ppermute | solution.py:308
  40.4 0.7 collective-permute-start.15
  41.1 0.0 collective-permute-done.3.refs_0_
  41.1 0.0 collective-permute-done.4.refs_1_
  41.1 1.8 %chain_step.7 = (bf16[128,1024]{1,0:T(8,128)(2,1)S(1)}, bf16[128,1024]{1,0:T(8,128)(2,1)S(1)}) custom-call(bf16[128,1024]{1,0:T(8,128)(2,1)S(1)} %copy-done.3, bf16[1024,8192]{1,0:T(8,128)(2,1)S(1)} %copy-done, bf16[128,1024]{1,0:T(8,128)(2,1)S(1)} %collective-permute-done.3.refs_0_, bf16[128,1024]{1,0:T(8,128)(2,1)S(1)} %collective-permute-done.4.refs_1_), custom_call_target="tpu_custom_call" | custom-call | flops 536870912 | bytes 4194304 | tf_op jit(solution)/shard_map/chain_step/pallas_call | solution.py:170
  42.9 4.8 %collective-permute-start.5 = (bf16[128,1024]{1,0:T(8,128)(2,1)S(1)}, bf16[128,1024]{1,0:T(8,128)(2,1)S(1)}, u32[]{:S(2)}, u32[]{:S(2)}) collective-permute-start(bf16[128,1024]{1,0:T(8,128)(2,1)S(1)} %get-tuple-element.32), channel_id=1, source_target_pairs={{0,1},{1,2},{4,5},{5,6},{8,9},{9,10},{12,13},{13,14},{16,17},{17,1... | collective-permute-start | bytes 786440 | tf_op jit(solution)/shard_map/ppermute | solution.py:308
  47.7 0.7 collective-permute-start.6
  48.4 2.2 %pack_hidden.1 = (bf16[32,2048]{1,0:T(8,128)(2,1)}, bf16[32,2048]{1,0:T(8,128)(2,1)}, bf16[32,2048]{1,0:T(8,128)(2,1)}, bf16[32,2048]{1,0:T(8,128)(2,1)}) custom-call(s32[1,128]{1,0:T(1,128)} %send_ref.3, bf16[128,2048]{1,0:T(8,128)(2,1)} %h_ref.1), custom_call_target="tpu_custom_call" | custom-call | tf_op jit(solution)/shard_map/pack_hidden/pallas_call | solution.py:85
  50.5 0.0 collective-permute-start.9
  50.6 0.0 collective-permute-done.14.refs_0_
  50.6 1.6 %collective-permute-start.10 = (bf16[32,2048]{1,0:T(8,128)(2,1)}, bf16[32,2048]{1,0:T(8,128)(2,1)S(1)}, u32[]{:S(2)}, u32[]{:S(2)}) collective-permute-start(bf16[32,2048]{1,0:T(8,128)(2,1)} %get-tuple-element.38), channel_id=1, source_target_pairs={{0,8},{4,12},{8,0},{12,4},{1,9},{5,13},{9,1},{13,5},{2,10},{6,14},... | collective-permute-start | bytes 393224 | tf_op jit(solution)/shard_map/ppermute | solution.py:277
  52.1 0.0 collective-permute-done.15.refs_1_
  52.1 5.8 %copy-done.1 = bf16[1024,8192]{1,0:T(8,128)(2,1)S(1)} copy-done((bf16[1024,8192]{1,0:T(8,128)(2,1)S(1)}, bf16[1024,8192]{1,0:T(8,128)(2,1)}, u32[]{:S(2)}) %copy-start.1) | copy-done | bytes 16777240
  57.9 1.7 %chain_step.11 = (bf16[128,1024]{1,0:T(8,128)(2,1)S(1)}, bf16[128,1024]{1,0:T(8,128)(2,1)S(1)}) custom-call(bf16[128,1024]{1,0:T(8,128)(2,1)S(1)} %copy-done.4, bf16[1024,8192]{1,0:T(8,128)(2,1)S(1)} %copy-done.1, bf16[128,1024]{1,0:T(8,128)(2,1)S(1)} %collective-permute-done.14.refs_0_, bf16[128,1024]{1,0:T(8,128)(2,1)S(1)} %collective-permute-done.15.refs_1_), custom_call_target="tpu_custom_call" | custom-call | flops 536870912 | bytes 4194304 | tf_op jit(solution)/shard_map/chain_step/pallas_call | solution.py:170
  59.6 5.2 %collective-permute-start.16 = (bf16[128,1024]{1,0:T(8,128)(2,1)S(1)}, bf16[128,1024]{1,0:T(8,128)(2,1)S(1)}, u32[]{:S(2)}, u32[]{:S(2)}) collective-permute-start(bf16[128,1024]{1,0:T(8,128)(2,1)S(1)} %get-tuple-element.44), channel_id=1, source_target_pairs={{0,1},{1,2},{2,3},{4,5},{5,6},{6,7},{8,9},{9,10},{10,11},{12,13},{... | collective-permute-start | bytes 786440 | tf_op jit(solution)/shard_map/ppermute | solution.py:308
  64.8 0.0 collective-permute-done.5.refs_0_
  64.8 1.4 %collective-permute-start.17 = (bf16[128,1024]{1,0:T(8,128)(2,1)S(1)}, bf16[128,1024]{1,0:T(8,128)(2,1)S(1)}, u32[]{:S(2)}, u32[]{:S(2)}) collective-permute-start(bf16[128,1024]{1,0:T(8,128)(2,1)S(1)} %get-tuple-element.45), channel_id=1, source_target_pairs={{3,2},{2,1},{1,0},{7,6},{6,5},{5,4},{11,10},{10,9},{9,8},{15,14},{... | collective-permute-start | bytes 786440 | tf_op jit(solution)/shard_map/ppermute | solution.py:309
  66.2 0.0 collective-permute-done.6.refs_1_
  66.3 1.7 %chain_step.8 = (bf16[128,1024]{1,0:T(8,128)(2,1)S(1)}, bf16[128,1024]{1,0:T(8,128)(2,1)S(1)}) custom-call(bf16[128,1024]{1,0:T(8,128)(2,1)S(1)} %copy-done.4, bf16[1024,8192]{1,0:T(8,128)(2,1)S(1)} %copy-done.1, bf16[128,1024]{1,0:T(8,128)(2,1)S(1)} %collective-permute-done.5.refs_0_, bf16[128,1024]{1,0:T(8,128)(2,1)S(1)} %collective-permute-done.6.refs_1_), custom_call_target="tpu_custom_call" | custom-call | flops 536870912 | bytes 4194304 | tf_op jit(solution)/shard_map/chain_step/pallas_call | solution.py:170
  68.0 5.2 %collective-permute-start.7 = (bf16[128,1024]{1,0:T(8,128)(2,1)S(1)}, bf16[128,1024]{1,0:T(8,128)(2,1)S(1)}, u32[]{:S(2)}, u32[]{:S(2)}) collective-permute-start(bf16[128,1024]{1,0:T(8,128)(2,1)S(1)} %get-tuple-element.34), channel_id=1, source_target_pairs={{0,1},{1,2},{2,3},{4,5},{5,6},{6,7},{8,9},{9,10},{10,11},{12,13},{... | collective-permute-start | bytes 786440 | tf_op jit(solution)/shard_map/ppermute | solution.py:308
  73.2 0.0 collective-permute-done.9.refs_1_
  73.2 1.3 %collective-permute-start.8 = (bf16[128,1024]{1,0:T(8,128)(2,1)S(1)}, bf16[128,1024]{1,0:T(8,128)(2,1)S(1)}, u32[]{:S(2)}, u32[]{:S(2)}) collective-permute-start(bf16[128,1024]{1,0:T(8,128)(2,1)S(1)} %get-tuple-element.35), channel_id=1, source_target_pairs={{3,2},{2,1},{1,0},{7,6},{6,5},{5,4},{11,10},{10,9},{9,8},{15,14},{... | collective-permute-start | bytes 786440 | tf_op jit(solution)/shard_map/ppermute | solution.py:309
  74.5 0.0 collective-permute-done.10.refs_2_
  74.5 0.1 collective-permute-start.11
  74.6 0.0 copy-done.10
  74.6 0.1 copy.12.scale_ref
  74.8 0.0 copy-start.2
  74.8 5.8 %copy-done.2 = bf16[1024,8192]{1,0:T(8,128)(2,1)S(1)} copy-done((bf16[1024,8192]{1,0:T(8,128)(2,1)S(1)}, bf16[1024,8192]{1,0:T(8,128)(2,1)}, u32[]{:S(2)}) %copy-start.2) | copy-done | bytes 16777240
  80.5 1.8 %own_term.1.own = f32[128,2048]{1,0:T(8,128)S(1)} custom-call(bf16[128,1024]{1,0:T(8,128)(2,1)S(1)} %copy-done.4, bf16[1024,8192]{1,0:T(8,128)(2,1)S(1)} %copy-done.2), custom_call_target="tpu_custom_call" | custom-call | flops 536870912 | bytes 4194304 | tf_op jit(solution)/shard_map/own_term/pallas_call | solution.py:196
  82.3 0.0 collective-permute-done.11.refs_3_
  82.3 0.0 collective-permute-done.16.recv_r
  82.3 0.0 collective-permute-done.17.recv_l
  82.4 1.2 %finish.2 = (f32[128,2048]{1,0:T(8,128)}, f32[8,128]{1,0:T(8,128)S(1)}) custom-call(bf16[128,1024]{1,0:T(8,128)(2,1)S(1)} %collective-permute-done.16.recv_r, bf16[128,1024]{1,0:T(8,128)(2,1)S(1)} %collective-permute-done.17.recv_l, f32[128,2048]{1,0:T(8,128)S(1)} %own_term.1.own, bf16[128,16]{1,0:T(8,128)(2,1)S(1)} %copy.12.scale_ref, ...), custom_call_target="tpu_custom_call" | custom-call | tf_op jit(solution)/shard_map/finish/pallas_call | solution.py:263
  83.5 0.0 collective-permute-done.7.recv_r
  83.5 0.0 collective-permute-done.8.recv_l
  83.5 1.2 %finish.3 = (f32[128,2048]{1,0:T(8,128)}, f32[8,128]{1,0:T(8,128)S(1)}) custom-call(bf16[128,1024]{1,0:T(8,128)(2,1)S(1)} %collective-permute-done.7.recv_r, bf16[128,1024]{1,0:T(8,128)(2,1)S(1)} %collective-permute-done.8.recv_l, f32[128,2048]{1,0:T(8,128)S(1)} %own_term.1.own, ...), custom_call_target="tpu_custom_call", output_to_operand_aliasing={{0}: (9, {})} | custom-call | tf_op jit(solution)/shard_map/finish/pallas_call | solution.py:263
  84.7 3.6 %collective-permute-start.20 = (f32[8,128]{1,0:T(8,128)S(1)}, f32[8,128]{1,0:T(8,128)S(1)}, u32[]{:S(2)}, u32[]{:S(2)}) collective-permute-start(f32[8,128]{1,0:T(8,128)S(1)} %get-tuple-element.49), channel_id=1, source_target_pairs={{0,3},{1,2},{2,1},{3,0},{4,7},{5,6},{6,5},{7,4},{8,11},{9,10},{10,... | collective-permute-start | bytes 12296 | tf_op jit(solution)/shard_map/ppermute | solution.py:286
  88.2 0.5 collective-permute-start.19
  88.8 0.5 collective-permute-start.18
  89.3 0.8 collective-permute-done.20
  90.1 2.7 %collective-permute-done.19 = f32[8,128]{1,0:T(8,128)S(1)} collective-permute-done((f32[8,128]{1,0:T(8,128)S(1)}, f32[8,128]{1,0:T(8,128)S(1)}, u32[]{:S(2)}, u32[]{:S(2)}) %collective-permute-start.19) | collective-permute-done | bytes 4128 | tf_op jit(solution)/shard_map/ppermute | solution.py:286
  92.8 0.0 collective-permute-done.18
  92.8 0.5 multiply_bitcast_fusion
  (18 shorter events, 0.1 us)
Async XLA Ops:
  2.7 3.1 %collective-permute-start = (bf16[32,1280]{1,0:T(8,128)(2,1)}, bf16[32,1280]{1,0:T(8,128)(2,1)S(1)}, u32[]{:S(2)}, u32[]{:S(2)}) collective-permute-start(bf16[32,1280]{1,0:T(8,128)(2,1)} %get-tuple-element.27), channel_id=1, source_target_pairs={{0,4},{4,0},{8,12},{12,8},{1,5},{5,1},{9,13},{13,9},{2,6},{6,2},{1... | collective-permute-start | bytes 245768 | tf_op jit(solution)/shard_map/ppermute | solution.py:277
  3.2 5.9 %collective-permute-start.1 = (bf16[32,1280]{1,0:T(8,128)(2,1)}, bf16[32,1280]{1,0:T(8,128)(2,1)S(1)}, u32[]{:S(2)}, u32[]{:S(2)}) collective-permute-start(bf16[32,1280]{1,0:T(8,128)(2,1)} %get-tuple-element.28), channel_id=1, source_target_pairs={{0,8},{4,12},{8,0},{12,4},{1,9},{5,13},{9,1},{13,5},{2,10},{6,14},... | collective-permute-start | bytes 245768 | tf_op jit(solution)/shard_map/ppermute | solution.py:277
  5.7 4.8 %collective-permute-start.2 = (bf16[32,1280]{1,0:T(8,128)(2,1)}, bf16[32,1280]{1,0:T(8,128)(2,1)S(1)}, u32[]{:S(2)}, u32[]{:S(2)}) collective-permute-start(bf16[32,1280]{1,0:T(8,128)(2,1)} %get-tuple-element.29), channel_id=1, source_target_pairs={{0,12},{4,8},{8,4},{12,0},{1,13},{5,9},{9,5},{13,1},{2,14},{6,10},... | collective-permute-start | bytes 245768 | tf_op jit(solution)/shard_map/ppermute | solution.py:277
  5.8 4.6 %copy-start.6 = (bf16[32,1280]{1,0:T(8,128)(2,1)}, bf16[32,1280]{1,0:T(8,128)(2,1)S(1)}, u32[]{:S(2)}) copy-start(bf16[32,1280]{1,0:T(8,128)(2,1)S(1)} %collective-permute-done.refs_1_) | copy-start | bytes 245764
  9.1 1.4 %copy-start.7 = (bf16[32,1280]{1,0:T(8,128)(2,1)}, bf16[32,1280]{1,0:T(8,128)(2,1)S(1)}, u32[]{:S(2)}) copy-start(bf16[32,1280]{1,0:T(8,128)(2,1)S(1)} %collective-permute-done.1.refs_2_) | copy-start | bytes 245764
  10.5 0.6 copy-start.8
  15.5 5.8 %copy-start = (bf16[1024,8192]{1,0:T(8,128)(2,1)S(1)}, bf16[1024,8192]{1,0:T(8,128)(2,1)}, u32[]{:S(2)}) copy-start(bf16[1024,8192]{1,0:T(8,128)(2,1)} %w_ref.13) | copy-start | bytes 50331652
  21.3 0.9 %copy-start.3 = (bf16[128,1024]{1,0:T(8,128)(2,1)S(1)}, bf16[128,1024]{1,0:T(8,128)(2,1)}, u32[]{:S(2)}) copy-start(bf16[128,1024]{1,0:T(8,128)(2,1)} %attend.1.ctx_ref) | copy-start | bytes 786436
  24.0 10.3 %collective-permute-start.12 = (bf16[128,1024]{1,0:T(8,128)(2,1)S(1)}, bf16[128,1024]{1,0:T(8,128)(2,1)S(1)}, u32[]{:S(2)}, u32[]{:S(2)}) collective-permute-start(bf16[128,1024]{1,0:T(8,128)(2,1)S(1)} %get-tuple-element.40), channel_id=1, source_target_pairs={{0,1},{4,5},{8,9},{12,13},{16,17},{20,21},{24,25},{28,29}} | collective-permute-start | bytes 786440 | tf_op jit(solution)/shard_map/ppermute | solution.py:308
  27.6 6.6 %collective-permute-start.13 = (bf16[128,1024]{1,0:T(8,128)(2,1)S(1)}, bf16[128,1024]{1,0:T(8,128)(2,1)S(1)}, u32[]{:S(2)}, u32[]{:S(2)}) collective-permute-start(bf16[128,1024]{1,0:T(8,128)(2,1)S(1)} %get-tuple-element.41), channel_id=1, source_target_pairs={{3,2},{7,6},{11,10},{15,14},{19,18},{23,22},{27,26},{31,30}} | collective-permute-start | bytes 786440 | tf_op jit(solution)/shard_map/ppermute | solution.py:309
  30.1 11.0 %collective-permute-start.3 = (bf16[128,1024]{1,0:T(8,128)(2,1)S(1)}, bf16[128,1024]{1,0:T(8,128)(2,1)S(1)}, u32[]{:S(2)}, u32[]{:S(2)}) collective-permute-start(bf16[128,1024]{1,0:T(8,128)(2,1)S(1)} %get-tuple-element.30), channel_id=1, source_target_pairs={{0,1},{4,5},{8,9},{12,13},{16,17},{20,21},{24,25},{28,29}} | collective-permute-start | bytes 786440 | tf_op jit(solution)/shard_map/ppermute | solution.py:308
  31.4 20.7 %copy-start.4 = (bf16[128,1024]{1,0:T(8,128)(2,1)S(1)}, bf16[128,1024]{1,0:T(8,128)(2,1)}, u32[]{:S(2)}) copy-start(bf16[128,1024]{1,0:T(8,128)(2,1)} %attend.1.ctx_ref) | copy-start | bytes 786436
  31.4 9.7 %collective-permute-start.4 = (bf16[128,1024]{1,0:T(8,128)(2,1)S(1)}, bf16[128,1024]{1,0:T(8,128)(2,1)S(1)}, u32[]{:S(2)}, u32[]{:S(2)}) collective-permute-start(bf16[128,1024]{1,0:T(8,128)(2,1)S(1)} %get-tuple-element.31), channel_id=1, source_target_pairs={{3,2},{7,6},{11,10},{15,14},{19,18},{23,22},{27,26},{31,30}} | collective-permute-start | bytes 786440 | tf_op jit(solution)/shard_map/ppermute | solution.py:309
  36.0 14.6 %collective-permute-start.14 = (bf16[128,1024]{1,0:T(8,128)(2,1)S(1)}, bf16[128,1024]{1,0:T(8,128)(2,1)S(1)}, u32[]{:S(2)}, u32[]{:S(2)}) collective-permute-start(bf16[128,1024]{1,0:T(8,128)(2,1)S(1)} %get-tuple-element.42), channel_id=1, source_target_pairs={{0,1},{1,2},{4,5},{5,6},{8,9},{9,10},{12,13},{13,14},{16,17},{17,1... | collective-permute-start | bytes 786440 | tf_op jit(solution)/shard_map/ppermute | solution.py:308
  40.4 11.7 %collective-permute-start.15 = (bf16[128,1024]{1,0:T(8,128)(2,1)S(1)}, bf16[128,1024]{1,0:T(8,128)(2,1)S(1)}, u32[]{:S(2)}, u32[]{:S(2)}) collective-permute-start(bf16[128,1024]{1,0:T(8,128)(2,1)S(1)} %get-tuple-element.43), channel_id=1, source_target_pairs={{3,2},{2,1},{7,6},{6,5},{11,10},{10,9},{15,14},{14,13},{19,18},{18... | collective-permute-start | bytes 786440 | tf_op jit(solution)/shard_map/ppermute | solution.py:309
  42.9 21.9 %collective-permute-start.5 = (bf16[128,1024]{1,0:T(8,128)(2,1)S(1)}, bf16[128,1024]{1,0:T(8,128)(2,1)S(1)}, u32[]{:S(2)}, u32[]{:S(2)}) collective-permute-start(bf16[128,1024]{1,0:T(8,128)(2,1)S(1)} %get-tuple-element.32), channel_id=1, source_target_pairs={{0,1},{1,2},{4,5},{5,6},{8,9},{9,10},{12,13},{13,14},{16,17},{17,1... | collective-permute-start | bytes 786440 | tf_op jit(solution)/shard_map/ppermute | solution.py:308
  47.7 18.6 %collective-permute-start.6 = (bf16[128,1024]{1,0:T(8,128)(2,1)S(1)}, bf16[128,1024]{1,0:T(8,128)(2,1)S(1)}, u32[]{:S(2)}, u32[]{:S(2)}) collective-permute-start(bf16[128,1024]{1,0:T(8,128)(2,1)S(1)} %get-tuple-element.33), channel_id=1, source_target_pairs={{3,2},{2,1},{7,6},{6,5},{11,10},{10,9},{15,14},{14,13},{19,18},{18... | collective-permute-start | bytes 786440 | tf_op jit(solution)/shard_map/ppermute | solution.py:309
  50.5 22.6 %collective-permute-start.9 = (bf16[32,2048]{1,0:T(8,128)(2,1)}, bf16[32,2048]{1,0:T(8,128)(2,1)S(1)}, u32[]{:S(2)}, u32[]{:S(2)}) collective-permute-start(bf16[32,2048]{1,0:T(8,128)(2,1)} %get-tuple-element.37), channel_id=1, source_target_pairs={{0,4},{4,0},{8,12},{12,8},{1,5},{5,1},{9,13},{13,9},{2,6},{6,2},{1... | collective-permute-start | bytes 393224 | tf_op jit(solution)/shard_map/ppermute | solution.py:277
  50.6 23.9 %collective-permute-start.10 = (bf16[32,2048]{1,0:T(8,128)(2,1)}, bf16[32,2048]{1,0:T(8,128)(2,1)S(1)}, u32[]{:S(2)}, u32[]{:S(2)}) collective-permute-start(bf16[32,2048]{1,0:T(8,128)(2,1)} %get-tuple-element.38), channel_id=1, source_target_pairs={{0,8},{4,12},{8,0},{12,4},{1,9},{5,13},{9,1},{13,5},{2,10},{6,14},... | collective-permute-start | bytes 393224 | tf_op jit(solution)/shard_map/ppermute | solution.py:277
  52.1 5.8 %copy-start.1 = (bf16[1024,8192]{1,0:T(8,128)(2,1)S(1)}, bf16[1024,8192]{1,0:T(8,128)(2,1)}, u32[]{:S(2)}) copy-start(bf16[1024,8192]{1,0:T(8,128)(2,1)} %w_ref.13) | copy-start | bytes 50331652
  57.9 16.6 %copy-start.11 = (bf16[32,2048]{1,0:T(8,128)(2,1)S(1)}, bf16[32,2048]{1,0:T(8,128)(2,1)}, u32[]{:S(2)}) copy-start(bf16[32,2048]{1,0:T(8,128)(2,1)} %get-tuple-element.39) | copy-start | bytes 393220
  57.9 16.7 %copy-start.10 = (bf16[128,16]{0,1:T(8,128)(2,1)S(1)}, bf16[128,16]{0,1:T(8,128)(2,1)}, u32[]{:S(2)}) copy-start(bf16[128,16]{0,1:T(8,128)(2,1)} %param.14) | copy-start | bytes 12292
  57.9 16.8 %copy-start.9 = (bf16[8192]{0:T(1024)(128)(2,1)S(1)}, bf16[8192]{0:T(1024)(128)(2,1)}, u32[]{:S(2)}) copy-start(bf16[8192]{0:T(1024)(128)(2,1)} %param.15) | copy-start | bytes 49156
  59.6 22.7 %collective-permute-start.16 = (bf16[128,1024]{1,0:T(8,128)(2,1)S(1)}, bf16[128,1024]{1,0:T(8,128)(2,1)S(1)}, u32[]{:S(2)}, u32[]{:S(2)}) collective-permute-start(bf16[128,1024]{1,0:T(8,128)(2,1)S(1)} %get-tuple-element.44), channel_id=1, source_target_pairs={{0,1},{1,2},{2,3},{4,5},{5,6},{6,7},{8,9},{9,10},{10,11},{12,13},{... | collective-permute-start | bytes 786440 | tf_op jit(solution)/shard_map/ppermute | solution.py:308
  64.8 17.5 %copy-start.5 = (bf16[32,2048]{1,0:T(8,128)(2,1)S(1)}, bf16[32,2048]{1,0:T(8,128)(2,1)}, u32[]{:S(2)}) copy-start(bf16[32,2048]{1,0:T(8,128)(2,1)} %get-tuple-element.36.refs_0_) | copy-start | bytes 393220
  64.8 17.5 %collective-permute-start.17 = (bf16[128,1024]{1,0:T(8,128)(2,1)S(1)}, bf16[128,1024]{1,0:T(8,128)(2,1)S(1)}, u32[]{:S(2)}, u32[]{:S(2)}) collective-permute-start(bf16[128,1024]{1,0:T(8,128)(2,1)S(1)} %get-tuple-element.45), channel_id=1, source_target_pairs={{3,2},{2,1},{1,0},{7,6},{6,5},{5,4},{11,10},{10,9},{9,8},{15,14},{... | collective-permute-start | bytes 786440 | tf_op jit(solution)/shard_map/ppermute | solution.py:309
  68.0 15.5 %collective-permute-start.7 = (bf16[128,1024]{1,0:T(8,128)(2,1)S(1)}, bf16[128,1024]{1,0:T(8,128)(2,1)S(1)}, u32[]{:S(2)}, u32[]{:S(2)}) collective-permute-start(bf16[128,1024]{1,0:T(8,128)(2,1)S(1)} %get-tuple-element.34), channel_id=1, source_target_pairs={{0,1},{1,2},{2,3},{4,5},{5,6},{6,7},{8,9},{9,10},{10,11},{12,13},{... | collective-permute-start | bytes 786440 | tf_op jit(solution)/shard_map/ppermute | solution.py:308
  73.2 10.3 %collective-permute-start.8 = (bf16[128,1024]{1,0:T(8,128)(2,1)S(1)}, bf16[128,1024]{1,0:T(8,128)(2,1)S(1)}, u32[]{:S(2)}, u32[]{:S(2)}) collective-permute-start(bf16[128,1024]{1,0:T(8,128)(2,1)S(1)} %get-tuple-element.35), channel_id=1, source_target_pairs={{3,2},{2,1},{1,0},{7,6},{6,5},{5,4},{11,10},{10,9},{9,8},{15,14},{... | collective-permute-start | bytes 786440 | tf_op jit(solution)/shard_map/ppermute | solution.py:309
  74.5 7.8 %collective-permute-start.11 = (bf16[32,2048]{1,0:T(8,128)(2,1)S(1)}, bf16[32,2048]{1,0:T(8,128)(2,1)S(1)}, u32[]{:S(2)}, u32[]{:S(2)}) collective-permute-start(bf16[32,2048]{1,0:T(8,128)(2,1)S(1)} %copy-done.11), channel_id=1, source_target_pairs={{0,12},{4,8},{8,4},{12,0},{1,13},{5,9},{9,5},{13,1},{2,14},{6,10},... | collective-permute-start | bytes 393224 | tf_op jit(solution)/shard_map/ppermute | solution.py:277
  74.8 5.8 %copy-start.2 = (bf16[1024,8192]{1,0:T(8,128)(2,1)S(1)}, bf16[1024,8192]{1,0:T(8,128)(2,1)}, u32[]{:S(2)}) copy-start(bf16[1024,8192]{1,0:T(8,128)(2,1)} %w_ref.13) | copy-start | bytes 50331652
  84.7 5.4 %collective-permute-start.20 = (f32[8,128]{1,0:T(8,128)S(1)}, f32[8,128]{1,0:T(8,128)S(1)}, u32[]{:S(2)}, u32[]{:S(2)}) collective-permute-start(f32[8,128]{1,0:T(8,128)S(1)} %get-tuple-element.49), channel_id=1, source_target_pairs={{0,3},{1,2},{2,1},{3,0},{4,7},{5,6},{6,5},{7,4},{8,11},{9,10},{10,... | collective-permute-start | bytes 12296 | tf_op jit(solution)/shard_map/ppermute | solution.py:286
  88.2 4.5 %collective-permute-start.19 = (f32[8,128]{1,0:T(8,128)S(1)}, f32[8,128]{1,0:T(8,128)S(1)}, u32[]{:S(2)}, u32[]{:S(2)}) collective-permute-start(f32[8,128]{1,0:T(8,128)S(1)} %get-tuple-element.49), channel_id=1, source_target_pairs={{0,2},{1,3},{2,0},{3,1},{4,6},{5,7},{6,4},{7,5},{8,10},{9,11},{10,... | collective-permute-start | bytes 12296 | tf_op jit(solution)/shard_map/ppermute | solution.py:286
  88.8 4.0 %collective-permute-start.18 = (f32[8,128]{1,0:T(8,128)S(1)}, f32[8,128]{1,0:T(8,128)S(1)}, u32[]{:S(2)}, u32[]{:S(2)}) collective-permute-start(f32[8,128]{1,0:T(8,128)S(1)} %get-tuple-element.49), channel_id=1, source_target_pairs={{0,1},{1,0},{2,3},{3,2},{4,5},{5,4},{6,7},{7,6},{8,9},{9,8},{10,11... | collective-permute-start | bytes 12296 | tf_op jit(solution)/shard_map/ppermute | solution.py:286

commit v2 on v1

--- a/solution.py
+++ b/solution.py
@@ -21,6 +21,7 @@
 VMEM = pl.BlockSpec(memory_space=pltpu.VMEM)
 SMEM = pl.BlockSpec(memory_space=pltpu.SMEM)
 ANY = pl.BlockSpec(memory_space=pl.ANY)
+HBM = pl.BlockSpec(memory_space=pltpu.HBM)
 
 
 def params(mib):
@@ -65,6 +66,7 @@
         in_specs=[VMEM] * 3,
         out_specs=[VMEM] * n_dp,
         scratch_shapes=[pltpu.VMEM((rows, width + 2 * HD), BF16)],
+        compiler_params=params(63),
         name="pack_qkv",
     )(send_rows, queries, keys_values)
 
@@ -88,12 +90,17 @@
         in_specs=[VMEM] * 2,
         out_specs=[VMEM] * n_dp,
         scratch_shapes=[pltpu.VMEM((rows, width), BF16)],
+        compiler_params=params(4),
         name="pack_hidden",
     )(send_rows, hidden)
 
 
-def attend_kernel(len_ref, *refs):
-    pieces, out, buf = refs[:-2], refs[-2], refs[-1]
+def attend_kernel(order, len_ref, *refs):
+    n_dp = len(refs) - 6
+    pieces, w_ref = refs[:n_dp], refs[n_dp]
+    out, first, buf, w_buf, sem = refs[n_dp + 1 :]
+    fetch = fetch_block(order, 0, w_ref, w_buf, sem)
+    fetch.start()
     me = lax.axis_index("dp")
     share = pieces[0].shape[0]
     for k, piece in enumerate(pieces):
@@ -110,101 +117,107 @@
         row_seg += (row_id >= end).astype(jnp.int32)
         col_seg += (col_id >= end).astype(jnp.int32)
     allowed = (row_seg == col_seg) & (row_id >= col_id)
+    heads = width // HD
     keys = buf[:, width : width + HD]
-    values = buf[:, width + HD : width + 2 * HD]
-    for h in range(width // HD):
-        cols = slice(h * HD, (h + 1) * HD)
-        scores = lax.dot_general(
-            buf[:, cols], keys, (((1,), (1,)), ((), ())), preferred_element_type=F32
-        ) * HD ** (-0.5)
-        scores = jnp.where(allowed, scores, -jnp.inf)
-        peak = jnp.max(scores, axis=1, keepdims=True)
-        weights = jnp.exp(scores - peak)
-        low = (weights / jnp.sum(weights, axis=1, keepdims=True)).astype(BF16)
-        out[:, cols] = jnp.dot(low, values, preferred_element_type=F32).astype(BF16)
-
-
-def attend(lengths, pieces):
+    values = jnp.concatenate(
+        [buf[:, width + HD : width + 2 * HD], jnp.ones((rows, HD), BF16)], axis=1
+    )
+    query = jnp.concatenate([buf[:, h * HD : (h + 1) * HD] for h in range(heads)], axis=0)
+    scores = lax.dot_general(
+        query, keys, (((1,), (1,)), ((), ())), preferred_element_type=F32
+    ) * HD ** (-0.5)
+    scores = jnp.where(allowed[None], scores.reshape(heads, rows, rows), -jnp.inf)
+    weights = jnp.exp(scores - jnp.max(scores, axis=2, keepdims=True))
+    weights = weights.reshape(heads * rows, rows).astype(BF16)
+    mixed = jnp.dot(weights, values, preferred_element_type=F32)
+    context = (mixed[:, :HD] / mixed[:, HD:]).astype(BF16)
+    context = jnp.concatenate([context[h * rows : (h + 1) * rows] for h in range(heads)], axis=1)
+    out[...] = context
+    fetch.wait()
+    first[...] = jnp.dot(context, w_buf[...], preferred_element_type=F32).astype(BF16)
+
+
+def fetch_block(order, place, w_ref, w_buf, sem):
+    width = w_buf.shape[1]
+    start = pl.multiple_of(order(place) * width, width)
+    return pltpu.make_async_copy(w_ref.at[:, pl.ds(start, width)], w_buf, sem)
+
+
+def attend(lengths, pieces, weight, order, cols):
     n_dp = len(pieces)
     share, wide = pieces[0].shape
     rows, width = share * n_dp, wide - 2 * HD
     return pl.pallas_call(
-        attend_kernel,
-        out_shape=jax.ShapeDtypeStruct((rows, width), BF16),
-        in_specs=[SMEM] + [VMEM] * n_dp,
+        functools.partial(attend_kernel, order),
+        out_shape=[
+            jax.ShapeDtypeStruct((rows, width), BF16),
+            jax.ShapeDtypeStruct((rows, cols), BF16),
+        ],
+        in_specs=[SMEM] + [VMEM] * n_dp + [HBM],
+        out_specs=[VMEM] * 2,
+        scratch_shapes=[
+            pltpu.VMEM((rows, wide), BF16),
+            pltpu.VMEM((width, cols), BF16),
+            pltpu.SemaphoreType.DMA,
+        ],
+        compiler_params=params(52),
+        name="attend",
+    )(lengths, *pieces, weight)
+
+
+def project_kernel(order, ctx_ref, w_ref, *refs):
+    count = len(refs) - 2
+    outs, w_buf, sems = refs[:count], refs[count], refs[count + 1]
+    copies = [
+        fetch_block(order, place + 1, w_ref, w_buf.at[place], sems.at[place])
+        for place in range(count)
+    ]
+    for copy in copies:
+        copy.start()
+    for copy, out, place in zip(copies, outs, range(count)):
+        copy.wait()
+        term = jnp.dot(ctx_ref[...], w_buf[place], preferred_element_type=F32)
+        out[...] = term.astype(out.dtype)
+
+
+def project(context, weight, order, cols, kept):
+    rows, depth = context.shape
+    count = weight.shape[1] // cols - 1
+    return pl.pallas_call(
+        functools.partial(project_kernel, order),
+        out_shape=[
+            jax.ShapeDtypeStruct((rows, cols), F32 if place >= count - kept else BF16)
+            for place in range(count)
+        ],
+        in_specs=[VMEM, HBM],
+        out_specs=[VMEM] * count,
+        scratch_shapes=[
+            pltpu.VMEM((count, depth, cols), BF16),
+            pltpu.SemaphoreType.DMA((count,)),
+        ],
+        compiler_params=params(52),
+        cost_estimate=pl.CostEstimate(
+            flops=2 * rows * depth * cols * count,
+            bytes_accessed=2 * depth * cols * count,
+            transcendentals=0,
+        ),
+        name="project",
+    )(context, weight)
+
+
+def add_kernel(a_ref, b_ref, out):
+    out[...] = (a_ref[...].astype(F32) + b_ref[...].astype(F32)).astype(BF16)
+
+
+def add(a, b):
+    return pl.pallas_call(
+        add_kernel,
+        out_shape=jax.ShapeDtypeStruct(a.shape, BF16),
+        in_specs=[VMEM] * 2,
         out_specs=VMEM,
-        scratch_shapes=[pltpu.VMEM((rows, wide), BF16)],
-        name="attend",
-    )(lengths, *pieces)
-
-
-def step_kernel(n, chunks, step, with_recv, ctx_ref, w_ref, *refs):
-    if with_recv:
-        recv_r, recv_l, out_r, out_l, w_buf, sem = refs
-    else:
-        out_r, out_l, w_buf, sem = refs
-    width = out_r.shape[1]
-    i = lax.axis_index("tensor")
-    turn, part = step // chunks, step % chunks
-    right = jnp.minimum(n - 1 - turn + i, n - 1) * chunks + part
-    left = jnp.maximum(turn - (n - 1 - i), 0) * chunks + part
-    copies = []
-    for side, block in enumerate((right, left)):
-        start = pl.multiple_of(block * width, width)
-        copies.append(
-            pltpu.make_async_copy(w_ref.at[:, pl.ds(start, width)], w_buf.at[side], sem.at[side])
-        )
-        copies[-1].start()
-    for side, out in enumerate((out_r, out_l)):
-        copies[side].wait()
-        term = jnp.dot(ctx_ref[...], w_buf[side], preferred_element_type=F32)
-        if with_recv:
-            term = term + (recv_r, recv_l)[side][...].astype(F32)
-        out[...] = term.astype(BF16)
-
-
-def chain_step(n, chunks, step, context, weight, recv):
-    rows, depth = context.shape
-    width = weight.shape[1] // (n * chunks)
-    out = jax.ShapeDtypeStruct((rows, width), BF16)
-    return pl.pallas_call(
-        functools.partial(step_kernel, n, chunks, step, recv is not None),
-        out_shape=[out] * 2,
-        in_specs=[VMEM, ANY] + [VMEM] * (2 if recv is not None else 0),
-        out_specs=[VMEM] * 2,
-        scratch_shapes=[pltpu.VMEM((2, depth, width), BF16), pltpu.SemaphoreType.DMA((2,))],
-        compiler_params=params(16),
-        cost_estimate=pl.CostEstimate(
-            flops=4 * rows * depth * width, bytes_accessed=4 * depth * width, transcendentals=0
-        ),
-        name="chain_step",
-    )(context, weight, *(recv or ()))
-
-
-def own_kernel(ctx_ref, w_ref, out, w_buf, sem):
-    width = out.shape[1]
-    start = pl.multiple_of(lax.axis_index("tensor") * width, width)
-    copy = pltpu.make_async_copy(w_ref.at[:, pl.ds(start, width)], w_buf, sem)
-    copy.start()
-    copy.wait()
-    out[...] = jnp.dot(ctx_ref[...], w_buf[...], preferred_element_type=F32)
-
-
-def own_term(n, context, weight):
-    rows, depth = context.shape
-    width = weight.shape[1] // n
-    return pl.pallas_call(
-        own_kernel,
-        out_shape=jax.ShapeDtypeStruct((rows, width), F32),
-        in_specs=[VMEM, ANY],
-        out_specs=VMEM,
-        scratch_shapes=[pltpu.VMEM((depth, width), BF16), pltpu.SemaphoreType.DMA],
-        compiler_params=params(16),
-        cost_estimate=pl.CostEstimate(
-            flops=2 * rows * depth * width, bytes_accessed=2 * depth * width, transcendentals=0
-        ),
-        name="own_term",
-    )(context, weight)
+        compiler_params=params(4),
+        name="add",
+    )(a, b)
 
 
 def finish_kernel(n_dp, part, width, recv_r, recv_l, own, scale_ref, head_ref, *refs):
@@ -223,10 +236,9 @@
     dots = jnp.zeros((rows, BLOCK), F32)
     for b in range(cols // BLOCK):
         here = slice(b * BLOCK, (b + 1) * BLOCK)
-        wide = slice(base + b * BLOCK, base + (b + 1) * BLOCK)
         block = base // BLOCK + b
         scale = scale_ref[:, block : block + 1].astype(F32)
-        summed = recv_r[:, here].astype(F32) + recv_l[:, here].astype(F32) + own[:, wide]
+        summed = recv_r[:, here].astype(F32) + recv_l[:, here].astype(F32) + own[:, here]
         residual = out[:, here] + summed
         code = jnp.clip(residual / scale, -CLIP_CODE, CLIP_CODE).astype(BF16)
         restored = code.astype(F32) * scale
@@ -249,7 +261,7 @@
 
 def finish(part, recv_r, recv_l, own, scales, head_row, pieces, before):
     rows, cols = recv_r.shape
-    width = own.shape[1]
+    width = pieces[0].shape[1]
     n_dp = len(pieces)
     out_spec = pl.BlockSpec((rows, cols), lambda g: (0, part))
     whole = lambda x: pl.BlockSpec(x.shape, lambda g: (0,) * x.ndim)
@@ -267,7 +279,7 @@
         in_specs=specs,
         out_specs=[out_spec, pl.BlockSpec((8, rows), lambda g: (0, 0))],
         input_output_aliases=aliases,
-        compiler_params=params(32),
+        compiler_params=params(8),
         name="finish",
     )(*args)
 
@@ -291,32 +303,62 @@
     return values
 
 
+def block_order(n, chunks):
+    def order(place):
+        turn, part = place // chunks, place % chunks
+        i = lax.axis_index("tensor")
+        low = i < 2
+        away = jnp.where(low, 3 - turn, turn)
+        if turn < 2:
+            shard = away
+        elif turn == 2:
+            shard = jnp.where(i == 0, 1, jnp.where(i == 1, 0, jnp.where(i == 2, 3, 2)))
+        else:
+            shard = i
+        return shard * chunks + part
+
+    return order if n == 4 else lambda place: jnp.int32(place)
+
+
+def chain_scatter(terms):
+    ends = [(0, 1), (3, 2)]
+    pairs = [(0, 1), (1, 0), (2, 3), (3, 2)]
+    middle = [(1, 2), (2, 1)]
+    move = lambda value, perm: lax.ppermute(value, "tensor", perm)
+    outer = [move(terms[0], ends), move(terms[1], ends)]
+    inner = []
+    for place in range(4):
+        inner.append(move(add(terms[place], outer[place]), middle))
+        if place < 2:
+            outer.append(move(terms[place + 2], ends))
+        else:
+            outer.append(move(add(terms[place + 2], inner[place - 2]), pairs))
+    return [(outer[4 + part], inner[2 + part]) for part in range(2)]
+
+
 def per_device(
     n_dp, n, hidden_in, queries, keys_values, out_weight, send_rows, lengths, block_scales, value_head
 ):
     chunks = 2
+    cols = hidden_in.shape[1] // chunks
+    order = block_order(n, chunks)
     moved = exchange(pack_qkv(send_rows, queries, keys_values, n_dp), "dp", n_dp)
     hidden = exchange(pack_hidden(send_rows, hidden_in, n_dp), "dp", n_dp)
-    context = attend(lengths, moved)
-    recv = []
-    own = None
-    for step in range((n - 1) * chunks):
-        pair = chain_step(n, chunks, step, context, out_weight, recv[step - chunks] if step >= chunks else None)
-        turn = step // chunks
-        recv.append(
-            (
-                lax.ppermute(pair[0], "tensor", [(i, i + 1) for i in range(n - 1) if turn >= i]),
-                lax.ppermute(
-                    pair[1], "tensor", [(n - 1 - i, n - 2 - i) for i in range(n - 1) if turn >= i]
-                ),
-            )
-        )
-    own = own_term(n, context, out_weight)
+    context, first = attend(lengths, moved, out_weight, order, cols)
+    if n == 4:
+        rest = project(context, out_weight, order, cols, chunks)
+        terms, own = [first, *rest[:-chunks]], rest[-chunks:]
+        recv = chain_scatter(terms)
+    else:
+        partial_term = jnp.dot(context, out_weight, preferred_element_type=F32).astype(BF16)
+        summed = lax.psum_scatter(partial_term, "tensor", scatter_dimension=1, tiled=True)
+        zero = jnp.zeros((hidden_in.shape[0], cols), BF16)
+        recv = [(summed[:, part * cols : (part + 1) * cols], zero) for part in range(chunks)]
+        own = [zero] * chunks
     head_row = value_head.reshape(1, D)
     result = None
     for part in range(chunks):
-        recv_r, recv_l = recv[(n - 2) * chunks + part]
-        result = finish(part, recv_r, recv_l, own, block_scales, head_row, hidden, result)
+        result = finish(part, *recv[part], own[part], block_scales, head_row, hidden, result)
     restored, sums = result
     sums = total_over(sums, "tensor", n)
     values = sums[1] / jnp.sqrt(sums[0] / D + EPS)

time: 93.9 us -> 70.8 us (0.75)
  local copies, waits for them, and re-layouts: 19 us -> 3.78 us
  waiting for transfers between devices: 10.2 us -> 24.4 us
  starting transfers between devices: 39.4 us -> 26.4 us
  Pallas kernels: 23.2 us -> 14.4 us
    unnamed x25 -> x17, local copies, waits for them, and re-layouts: 19 us -> 3.76 us
    ppermute x12 -> x10, starting transfers between devices: 30 us -> 17.4 us  [chain_scatter(): move = lambda value, perm: lax.ppermute(value, 'tensor', perm)]
    ppermute x12 -> x10, waiting for transfers between devices: 2.08 us -> 11.7 us  [chain_scatter(): move = lambda value, perm: lax.ppermute(value, 'tensor', perm)]
    pallas_call x8, Pallas kernels: 16.6 us -> 9.66 us  [the longest x1 6.64 us: project(): pl.pallas_call(functools.partial(project_kernel, order), out_shape=[jax.S...]
    ppermute x6, waiting for transfers between devices: 4.65 us -> 10.2 us  [exchange(): lax.ppermute(pieces[k], axis, [(i, i ^ k) for i in range(n)])]
    pallas_call x1, Pallas kernels: 2.18 us -> 0.35 us  [pack_hidden(): pl.pallas_call(pack_hidden_kernel, out_shape=[out] * n_dp, in_specs=[VMEM...]
    ppermute x3, waiting for transfers between devices: 3.44 us -> 2.42 us  [total_over(): lax.ppermute(values, axis, [(i, i ^ k * done) for i in range(n)])]
  transfers between devices with their start and end apart: 21 -> 19, of which waited for: 5 -> 10; matrix products, arithmetic and copies ran while one was open for 0% -> 0% of each run, Pallas kernels for 15% -> 12%
where the time goes in v2:
time: 70.8 us; the launch traced here: 70.3 us
  starting transfers between devices  26.4 us (37%)
  waiting for transfers between devices  24.4 us (34%)
  Pallas kernels  14.4 us (20%)
  local copies, waits for them, and re-layouts  3.78 us (5%)
  between operations  0.84 us (1%)
    ppermute x10, starting transfers between devices, chain_scatter(): move = lambda value, perm: lax.ppermute(value, 'tensor', perm)  17.4 us
    ppermute x10, waiting for transfers between devices, chain_scatter(): move = lambda value, perm: lax.ppermute(value, 'tensor', perm)  11.7 us
    ppermute x6, waiting for transfers between devices, exchange(): lax.ppermute(pieces[k], axis, [(i, i ^ k) for i in range(n)])  10.2 us
    pallas_call x1, Pallas kernels, project(): pl.pallas_call(functools.partial(project_kernel, order), out_shape=[jax.S...  6.64 us
    ppermute x6, starting transfers between devices, exchange(): lax.ppermute(pieces[k], axis, [(i, i ^ k) for i in range(n)])  4.66 us
    ppermute x3, starting transfers between devices, total_over(): lax.ppermute(values, axis, [(i, i ^ k * done) for i in range(n)])  4.39 us
    unnamed x17, local copies, waits for them, and re-layouts  3.76 us
    pallas_call x1, Pallas kernels, attend(): pl.pallas_call(functools.partial(attend_kernel, order), out_shape=[jax.Sh...  2.64 us
  transfers between devices with their start and end apart: 19, of which 10 were waited for; matrix products, arithmetic and copies ran while one was open for 0% of the time, Pallas kernels for 12%

profile of v2, /device:TPU:0, one launch (start us, length us, event | category | flops | bytes accessed | tf_op | source)
XLA Modules:
  0.0 70.3 jit_solution(17477670033348747127)
XLA Ops:
  0.6 2.1 %pack_qkv.1 = (bf16[32,1280]{1,0:T(8,128)(2,1)}, bf16[32,1280]{1,0:T(8,128)(2,1)}, bf16[32,1280]{1,0:T(8,128)(2,1)}, bf16[32,1280]{1,0:T(8,128)(2,1)}) custom-call(s32[1,128]{1,0:T(1,128)} %send_ref.3, bf16[128,1024]{1,0:T(8,128)(2,1)} %q_ref.1, bf16[128,2,512]{2,1,0:T(2,128)(2,1)} %kv_ref.1), custom_call_target="tpu_custom_call" | custom-call | tf_op jit(solution)/shard_map/pack_qkv/pallas_call | solution.py:63
  2.7 0.5 collective-permute-start
  3.2 2.5 %collective-permute-start.1 = (bf16[32,1280]{1,0:T(8,128)(2,1)}, bf16[32,1280]{1,0:T(8,128)(2,1)S(1)}, u32[]{:S(2)}, u32[]{:S(2)}) collective-permute-start(bf16[32,1280]{1,0:T(8,128)(2,1)} %get-tuple-element.25), channel_id=1, source_target_pairs={{0,8},{4,12},{8,0},{12,4},{1,9},{5,13},{9,1},{13,5},{2,10},{6,14},... | collective-permute-start | bytes 245768 | tf_op jit(solution)/shard_map/ppermute | solution.py:289
  5.7 0.1 collective-permute-start.2
  5.8 0.0 collective-permute-done.refs_1_
  5.8 3.2 %collective-permute-done.1.refs_2_ = bf16[32,1280]{1,0:T(8,128)(2,1)S(1)} collective-permute-done((bf16[32,1280]{1,0:T(8,128)(2,1)}, bf16[32,1280]{1,0:T(8,128)(2,1)S(1)}, u32[]{:S(2)}, u32[]{:S(2)}) %collective-permute-start.1) | collective-permute-done | bytes 81952 | tf_op jit(solution)/shard_map/ppermute | solution.py:289
  9.1 1.4 %collective-permute-done.2.refs_3_ = bf16[32,1280]{1,0:T(8,128)(2,1)S(1)} collective-permute-done((bf16[32,1280]{1,0:T(8,128)(2,1)}, bf16[32,1280]{1,0:T(8,128)(2,1)S(1)}, u32[]{:S(2)}, u32[]{:S(2)}) %collective-permute-start.2) | collective-permute-done | bytes 81952 | tf_op jit(solution)/shard_map/ppermute | solution.py:289
  10.5 0.9 %copy-done.3 = bf16[32,1280]{1,0:T(8,128)(2,1)S(1)} copy-done((bf16[32,1280]{1,0:T(8,128)(2,1)S(1)}, bf16[32,1280]{1,0:T(8,128)(2,1)}, u32[]{:S(2)}) %copy-start.3) | copy-done | bytes 81944
  11.4 0.0 copy-start.5
  11.4 0.7 copy-done.5
  12.0 0.0 copy-start.1
  12.0 0.0 copy-start.4
  12.0 0.0 copy-start.7
  12.0 2.6 %attend.1 = (bf16[128,1024]{1,0:T(8,128)(2,1)S(1)}, bf16[128,1024]{1,0:T(8,128)(2,1)S(1)}) custom-call(s32[1,8]{1,0:T(1,128)S(1)} %copy-done.5, bf16[32,1280]{1,0:T(8,128)(2,1)S(1)} %copy-done.3, bf16[32,1280]{1,0:T(8,128)(2,1)S(1)} %collective-permute-done.refs_1_, bf16[32,1280]{1,0:T(8,128)(2,1)S(1)} %collective-permute-done.1.refs_2_, ...), custom_call_target="tpu_custom_call" | custom-call | tf_op jit(solution)/shard_map/attend/pallas_call | solution.py:150
  14.7 3.6 %collective-permute-start.11 = (bf16[128,1024]{1,0:T(8,128)(2,1)S(1)}, bf16[128,1024]{1,0:T(8,128)(2,1)S(1)}, u32[]{:S(2)}, u32[]{:S(2)}) collective-permute-start(bf16[128,1024]{1,0:T(8,128)(2,1)S(1)} %get-tuple-element.37.a_ref), channel_id=1, source_target_pairs={{0,1},{3,2},{4,5},{7,6},{8,9},{11,10},{12,13},{15,14},{16,17},{19,... | collective-permute-start | bytes 786440 | tf_op jit(solution)/shard_map/ppermute | solution.py:327
  18.3 6.6 %project.1 = (bf16[128,1024]{1,0:T(8,128)(2,1)S(1)}, bf16[128,1024]{1,0:T(8,128)(2,1)S(1)}, bf16[128,1024]{1,0:T(8,128)(2,1)S(1)}, bf16[128,1024]{1,0:T(8,128)(2...) custom-call(bf16[128,1024]{1,0:T(8,128)(2,1)S(1)} %get-tuple-element.27.ctx_ref, ...), custom_call_target="tpu_custom_call" | custom-call | flops 1879048192 | bytes 14680064 | tf_op jit(solution)/shard_map/project/pallas_call | solution.py:186
  25.0 1.3 %collective-permute-start.3 = (bf16[128,1024]{1,0:T(8,128)(2,1)S(1)}, bf16[128,1024]{1,0:T(8,128)(2,1)S(1)}, u32[]{:S(2)}, u32[]{:S(2)}) collective-permute-start(bf16[128,1024]{1,0:T(8,128)(2,1)S(1)} %get-tuple-element.29.a_ref), channel_id=1, source_target_pairs={{0,1},{3,2},{4,5},{7,6},{8,9},{11,10},{12,13},{15,14},{16,17},{19,... | collective-permute-start | bytes 786440 | tf_op jit(solution)/shard_map/ppermute | solution.py:327
  26.3 1.3 %collective-permute-start.14 = (bf16[128,1024]{1,0:T(8,128)(2,1)S(1)}, bf16[128,1024]{1,0:T(8,128)(2,1)S(1)}, u32[]{:S(2)}, u32[]{:S(2)}) collective-permute-start(bf16[128,1024]{1,0:T(8,128)(2,1)S(1)} %get-tuple-element.38.a_ref), channel_id=1, source_target_pairs={{0,1},{3,2},{4,5},{7,6},{8,9},{11,10},{12,13},{15,14},{16,17},{19,... | collective-permute-start | bytes 786440 | tf_op jit(solution)/shard_map/ppermute | solution.py:327
  27.6 1.3 %collective-permute-start.6 = (bf16[128,1024]{1,0:T(8,128)(2,1)S(1)}, bf16[128,1024]{1,0:T(8,128)(2,1)S(1)}, u32[]{:S(2)}, u32[]{:S(2)}) collective-permute-start(bf16[128,1024]{1,0:T(8,128)(2,1)S(1)} %get-tuple-element.30.a_ref), channel_id=1, source_target_pairs={{0,1},{3,2},{4,5},{7,6},{8,9},{11,10},{12,13},{15,14},{16,17},{19,... | collective-permute-start | bytes 786440 | tf_op jit(solution)/shard_map/ppermute | solution.py:327
  28.9 0.0 collective-permute-done.11.b_ref
  28.9 0.1 add.35
  29.0 0.7 collective-permute-start.12
  29.7 3.2 %collective-permute-done.3.b_ref = bf16[128,1024]{1,0:T(8,128)(2,1)S(1)} collective-permute-done((bf16[128,1024]{1,0:T(8,128)(2,1)S(1)}, bf16[128,1024]{1,0:T(8,128)(2,1)S(1)}, u32[]{:S(2)}, u32[]{:S(2)}) %collective-permute-start.3) | collective-permute-done | bytes 262176 | tf_op jit(solution)/shard_map/ppermute | solution.py:327
  32.9 0.1 add.32
  33.0 0.7 collective-permute-start.4
  33.7 0.0 copy-done.1
  33.7 0.0 copy-done.4
  33.7 0.4 pack_hidden.1
  34.0 0.1 collective-permute-start.8
  34.1 4.4 %collective-permute-done.14.b_ref = bf16[128,1024]{1,0:T(8,128)(2,1)S(1)} collective-permute-done((bf16[128,1024]{1,0:T(8,128)(2,1)S(1)}, bf16[128,1024]{1,0:T(8,128)(2,1)S(1)}, u32[]{:S(2)}, u32[]{:S(2)}) %collective-permute-start.14) | collective-permute-done | bytes 262176 | tf_op jit(solution)/shard_map/ppermute | solution.py:327
  38.5 1.5 %collective-permute-start.9 = (bf16[32,2048]{1,0:T(8,128)(2,1)S(1)}, bf16[32,2048]{1,0:T(8,128)(2,1)S(1)}, u32[]{:S(2)}, u32[]{:S(2)}) collective-permute-start(bf16[32,2048]{1,0:T(8,128)(2,1)S(1)} %get-tuple-element.34), channel_id=1, source_target_pairs={{0,8},{4,12},{8,0},{12,4},{1,9},{5,13},{9,1},{13,5},{2,10},{6,14},... | collective-permute-start | bytes 393224 | tf_op jit(solution)/shard_map/ppermute | solution.py:289
  40.0 0.1 add.37
  40.1 3.3 %collective-permute-done.6.b_ref = bf16[128,1024]{1,0:T(8,128)(2,1)S(1)} collective-permute-done((bf16[128,1024]{1,0:T(8,128)(2,1)S(1)}, bf16[128,1024]{1,0:T(8,128)(2,1)S(1)}, u32[]{:S(2)}, u32[]{:S(2)}) %collective-permute-start.6) | collective-permute-done | bytes 262176 | tf_op jit(solution)/shard_map/ppermute | solution.py:327
  43.4 0.7 collective-permute-start.15
  44.1 0.1 add.34
  44.2 0.0 collective-permute-done.12.b_ref
  44.2 0.1 add.36
  44.3 5.4 %collective-permute-start.13 = (bf16[128,1024]{1,0:T(8,128)(2,1)S(1)}, bf16[128,1024]{1,0:T(8,128)(2,1)S(1)}, u32[]{:S(2)}, u32[]{:S(2)}) collective-permute-start(bf16[128,1024]{1,0:T(8,128)(2,1)S(1)} %add.36), channel_id=1, source_target_pairs={{0,1},{1,0},{2,3},{3,2},{4,5},{5,4},{6,7},{7,6},{8,9},{9,8},{10,11... | collective-permute-start | bytes 786440 | tf_op jit(solution)/shard_map/ppermute | solution.py:327
  49.6 0.0 collective-permute-done.4.b_ref
  49.6 0.7 collective-permute-start.7
  50.3 0.1 add.33
  50.4 0.0 collective-permute-done.8.refs_1_
  50.4 1.8 %collective-permute-start.5 = (bf16[128,1024]{1,0:T(8,128)(2,1)S(1)}, bf16[128,1024]{1,0:T(8,128)(2,1)S(1)}, u32[]{:S(2)}, u32[]{:S(2)}) collective-permute-start(bf16[128,1024]{1,0:T(8,128)(2,1)S(1)} %add.33), channel_id=1, source_target_pairs={{0,1},{1,0},{2,3},{3,2},{4,5},{5,4},{6,7},{7,6},{8,9},{9,8},{10,11... | collective-permute-start | bytes 786440 | tf_op jit(solution)/shard_map/ppermute | solution.py:327
  52.2 0.0 collective-permute-done.9.refs_2_
  52.2 0.0 collective-permute-start.10
  52.2 0.0 copy-done.7
  52.2 0.1 copy.12.scale_ref
  52.3 0.0 copy-done.6
  52.3 5.6 %collective-permute-done.10.refs_3_ = bf16[32,2048]{1,0:T(8,128)(2,1)S(1)} collective-permute-done((bf16[32,2048]{1,0:T(8,128)(2,1)S(1)}, bf16[32,2048]{1,0:T(8,128)(2,1)S(1)}, u32[]{:S(2)}, u32[]{:S(2)}) %collective-permute-start.10) | collective-permute-done | bytes 131104 | tf_op jit(solution)/shard_map/ppermute | solution.py:289
  57.9 0.0 collective-permute-done.15.recv_l
  57.9 0.0 collective-permute-done.13.recv_r
  57.9 1.0 %copy-done = f32[128,1024]{1,0:T(8,128)S(1)} copy-done((f32[128,1024]{1,0:T(8,128)S(1)}, f32[128,1024]{1,0:T(8,128)}, u32[]{:S(2)}) %copy-start) | copy-done | bytes 524312
  59.0 1.1 %finish.2 = (f32[128,2048]{1,0:T(8,128)}, f32[8,128]{1,0:T(8,128)S(1)}) custom-call(bf16[128,1024]{1,0:T(8,128)(2,1)S(1)} %collective-permute-done.13.recv_r, bf16[128,1024]{1,0:T(8,128)(2,1)S(1)} %collective-permute-done.15.recv_l, f32[128,1024]{1,0:T(8,128)S(1)} %copy-done, bf16[128,16]{1,0:T(8,128)(2,1)S(1)} %copy.12.scale_ref, ...), custom_call_target="tpu_custom_call" | custom-call | tf_op jit(solution)/shard_map/finish/pallas_call | solution.py:275
  60.1 0.0 collective-permute-done.7.recv_l
  60.1 0.7 %collective-permute-done.5.recv_r = bf16[128,1024]{1,0:T(8,128)(2,1)S(1)} collective-permute-done((bf16[128,1024]{1,0:T(8,128)(2,1)S(1)}, bf16[128,1024]{1,0:T(8,128)(2,1)S(1)}, u32[]{:S(2)}, u32[]{:S(2)}) %collective-permute-start.5) | collective-permute-done | bytes 262176 | tf_op jit(solution)/shard_map/ppermute | solution.py:327
  60.8 1.0 %copy-done.2 = f32[128,1024]{1,0:T(8,128)S(1)} copy-done((f32[128,1024]{1,0:T(8,128)S(1)}, f32[128,1024]{1,0:T(8,128)}, u32[]{:S(2)}) %copy-start.2) | copy-done | bytes 524312
  61.9 1.1 %finish.3 = (f32[128,2048]{1,0:T(8,128)}, f32[8,128]{1,0:T(8,128)S(1)}) custom-call(bf16[128,1024]{1,0:T(8,128)(2,1)S(1)} %collective-permute-done.5.recv_r, bf16[128,1024]{1,0:T(8,128)(2,1)S(1)} %collective-permute-done.7.recv_l, f32[128,1024]{1,0:T(8,128)S(1)} %copy-done.2, bf16[128,16]{1,0:T(8,128)(2,1)S(1)} %copy.12.scale_ref, ...), custom_call_target="tpu_custom_call", output_to_operand_aliasing={{0}: (9, {})} | custom-call | tf_op jit(solution)/shard_map/finish/pallas_call | solution.py:275
  63.0 1.8 %collective-permute-start.18 = (f32[8,128]{1,0:T(8,128)S(1)}, f32[8,128]{1,0:T(8,128)S(1)}, u32[]{:S(2)}, u32[]{:S(2)}) collective-permute-start(f32[8,128]{1,0:T(8,128)S(1)} %get-tuple-element.43), channel_id=1, source_target_pairs={{0,3},{1,2},{2,1},{3,0},{4,7},{5,6},{6,5},{7,4},{8,11},{9,10},{10,... | collective-permute-start | bytes 12296 | tf_op jit(solution)/shard_map/ppermute | solution.py:298
  64.8 1.4 %collective-permute-start.17 = (f32[8,128]{1,0:T(8,128)S(1)}, f32[8,128]{1,0:T(8,128)S(1)}, u32[]{:S(2)}, u32[]{:S(2)}) collective-permute-start(f32[8,128]{1,0:T(8,128)S(1)} %get-tuple-element.43), channel_id=1, source_target_pairs={{0,2},{1,3},{2,0},{3,1},{4,6},{5,7},{6,4},{7,5},{8,10},{9,11},{10,... | collective-permute-start | bytes 12296 | tf_op jit(solution)/shard_map/ppermute | solution.py:298
  66.2 1.2 %collective-permute-start.16 = (f32[8,128]{1,0:T(8,128)S(1)}, f32[8,128]{1,0:T(8,128)S(1)}, u32[]{:S(2)}, u32[]{:S(2)}) collective-permute-start(f32[8,128]{1,0:T(8,128)S(1)} %get-tuple-element.43), channel_id=1, source_target_pairs={{0,1},{1,0},{2,3},{3,2},{4,5},{5,4},{6,7},{7,6},{8,9},{9,8},{10,11... | collective-permute-start | bytes 12296 | tf_op jit(solution)/shard_map/ppermute | solution.py:298
  67.4 1.0 %collective-permute-done.18 = f32[8,128]{1,0:T(8,128)S(1)} collective-permute-done((f32[8,128]{1,0:T(8,128)S(1)}, f32[8,128]{1,0:T(8,128)S(1)}, u32[]{:S(2)}, u32[]{:S(2)}) %collective-permute-start.18) | collective-permute-done | bytes 4128 | tf_op jit(solution)/shard_map/ppermute | solution.py:298
  68.4 0.9 %collective-permute-done.17 = f32[8,128]{1,0:T(8,128)S(1)} collective-permute-done((f32[8,128]{1,0:T(8,128)S(1)}, f32[8,128]{1,0:T(8,128)S(1)}, u32[]{:S(2)}, u32[]{:S(2)}) %collective-permute-start.17) | collective-permute-done | bytes 4128 | tf_op jit(solution)/shard_map/ppermute | solution.py:298
  69.3 0.5 collective-permute-done.16
  69.8 0.5 multiply_bitcast_fusion
  (6 shorter events, 0.0 us)
Async XLA Ops:
  2.7 3.1 %collective-permute-start = (bf16[32,1280]{1,0:T(8,128)(2,1)}, bf16[32,1280]{1,0:T(8,128)(2,1)S(1)}, u32[]{:S(2)}, u32[]{:S(2)}) collective-permute-start(bf16[32,1280]{1,0:T(8,128)(2,1)} %get-tuple-element.24), channel_id=1, source_target_pairs={{0,4},{4,0},{8,12},{12,8},{1,5},{5,1},{9,13},{13,9},{2,6},{6,2},{1... | collective-permute-start | bytes 245768 | tf_op jit(solution)/shard_map/ppermute | solution.py:289
  3.2 5.9 %collective-permute-start.1 = (bf16[32,1280]{1,0:T(8,128)(2,1)}, bf16[32,1280]{1,0:T(8,128)(2,1)S(1)}, u32[]{:S(2)}, u32[]{:S(2)}) collective-permute-start(bf16[32,1280]{1,0:T(8,128)(2,1)} %get-tuple-element.25), channel_id=1, source_target_pairs={{0,8},{4,12},{8,0},{12,4},{1,9},{5,13},{9,1},{13,5},{2,10},{6,14},... | collective-permute-start | bytes 245768 | tf_op jit(solution)/shard_map/ppermute | solution.py:289
  5.7 4.8 %collective-permute-start.2 = (bf16[32,1280]{1,0:T(8,128)(2,1)}, bf16[32,1280]{1,0:T(8,128)(2,1)S(1)}, u32[]{:S(2)}, u32[]{:S(2)}) collective-permute-start(bf16[32,1280]{1,0:T(8,128)(2,1)} %get-tuple-element.26), channel_id=1, source_target_pairs={{0,12},{4,8},{8,4},{12,0},{1,13},{5,9},{9,5},{13,1},{2,14},{6,10},... | collective-permute-start | bytes 245768 | tf_op jit(solution)/shard_map/ppermute | solution.py:289
  10.5 0.9 %copy-start.3 = (bf16[32,1280]{1,0:T(8,128)(2,1)S(1)}, bf16[32,1280]{1,0:T(8,128)(2,1)}, u32[]{:S(2)}) copy-start(bf16[32,1280]{1,0:T(8,128)(2,1)} %get-tuple-element.23.refs_0_) | copy-start | bytes 245764
  11.4 0.7 copy-start.5
  12.0 21.6 %copy-start.1 = (bf16[128,2048]{1,0:T(8,128)(2,1)S(1)}, bf16[128,2048]{1,0:T(8,128)(2,1)}, u32[]{:S(2)}) copy-start(bf16[128,2048]{1,0:T(8,128)(2,1)} %h_ref.1) | copy-start | bytes 1572868
  12.0 21.7 %copy-start.4 = (s32[1,128]{1,0:T(1,128)S(1)}, s32[1,128]{1,0:T(1,128)}, u32[]{:S(2)}) copy-start(s32[1,128]{1,0:T(1,128)} %send_ref.3) | copy-start | bytes 1540
  12.0 40.1 %copy-start.7 = (bf16[128,16]{0,1:T(8,128)(2,1)S(1)}, bf16[128,16]{0,1:T(8,128)(2,1)}, u32[]{:S(2)}) copy-start(bf16[128,16]{0,1:T(8,128)(2,1)} %param.14) | copy-start | bytes 12292
  12.0 40.3 %copy-start.6 = (bf16[8192]{0:T(1024)(128)(2,1)S(1)}, bf16[8192]{0:T(1024)(128)(2,1)}, u32[]{:S(2)}) copy-start(bf16[8192]{0:T(1024)(128)(2,1)} %param.15) | copy-start | bytes 49156
  14.7 14.2 %collective-permute-start.11 = (bf16[128,1024]{1,0:T(8,128)(2,1)S(1)}, bf16[128,1024]{1,0:T(8,128)(2,1)S(1)}, u32[]{:S(2)}, u32[]{:S(2)}) collective-permute-start(bf16[128,1024]{1,0:T(8,128)(2,1)S(1)} %get-tuple-element.37.a_ref), channel_id=1, source_target_pairs={{0,1},{3,2},{4,5},{7,6},{8,9},{11,10},{12,13},{15,14},{16,17},{19,... | collective-permute-start | bytes 786440 | tf_op jit(solution)/shard_map/ppermute | solution.py:327
  25.0 7.9 %collective-permute-start.3 = (bf16[128,1024]{1,0:T(8,128)(2,1)S(1)}, bf16[128,1024]{1,0:T(8,128)(2,1)S(1)}, u32[]{:S(2)}, u32[]{:S(2)}) collective-permute-start(bf16[128,1024]{1,0:T(8,128)(2,1)S(1)} %get-tuple-element.29.a_ref), channel_id=1, source_target_pairs={{0,1},{3,2},{4,5},{7,6},{8,9},{11,10},{12,13},{15,14},{16,17},{19,... | collective-permute-start | bytes 786440 | tf_op jit(solution)/shard_map/ppermute | solution.py:327
  26.3 12.2 %collective-permute-start.14 = (bf16[128,1024]{1,0:T(8,128)(2,1)S(1)}, bf16[128,1024]{1,0:T(8,128)(2,1)S(1)}, u32[]{:S(2)}, u32[]{:S(2)}) collective-permute-start(bf16[128,1024]{1,0:T(8,128)(2,1)S(1)} %get-tuple-element.38.a_ref), channel_id=1, source_target_pairs={{0,1},{3,2},{4,5},{7,6},{8,9},{11,10},{12,13},{15,14},{16,17},{19,... | collective-permute-start | bytes 786440 | tf_op jit(solution)/shard_map/ppermute | solution.py:327
  27.6 15.8 %collective-permute-start.6 = (bf16[128,1024]{1,0:T(8,128)(2,1)S(1)}, bf16[128,1024]{1,0:T(8,128)(2,1)S(1)}, u32[]{:S(2)}, u32[]{:S(2)}) collective-permute-start(bf16[128,1024]{1,0:T(8,128)(2,1)S(1)} %get-tuple-element.30.a_ref), channel_id=1, source_target_pairs={{0,1},{3,2},{4,5},{7,6},{8,9},{11,10},{12,13},{15,14},{16,17},{19,... | collective-permute-start | bytes 786440 | tf_op jit(solution)/shard_map/ppermute | solution.py:327
  29.0 15.2 %collective-permute-start.12 = (bf16[128,1024]{1,0:T(8,128)(2,1)S(1)}, bf16[128,1024]{1,0:T(8,128)(2,1)S(1)}, u32[]{:S(2)}, u32[]{:S(2)}) collective-permute-start(bf16[128,1024]{1,0:T(8,128)(2,1)S(1)} %add.35), channel_id=1, source_target_pairs={{1,2},{2,1},{5,6},{6,5},{9,10},{10,9},{13,14},{14,13},{17,18},{18,... | collective-permute-start | bytes 786440 | tf_op jit(solution)/shard_map/ppermute | solution.py:327
  33.0 16.6 %collective-permute-start.4 = (bf16[128,1024]{1,0:T(8,128)(2,1)S(1)}, bf16[128,1024]{1,0:T(8,128)(2,1)S(1)}, u32[]{:S(2)}, u32[]{:S(2)}) collective-permute-start(bf16[128,1024]{1,0:T(8,128)(2,1)S(1)} %add.32), channel_id=1, source_target_pairs={{1,2},{2,1},{5,6},{6,5},{9,10},{10,9},{13,14},{14,13},{17,18},{18,... | collective-permute-start | bytes 786440 | tf_op jit(solution)/shard_map/ppermute | solution.py:327
  34.0 16.3 %collective-permute-start.8 = (bf16[32,2048]{1,0:T(8,128)(2,1)S(1)}, bf16[32,2048]{1,0:T(8,128)(2,1)S(1)}, u32[]{:S(2)}, u32[]{:S(2)}) collective-permute-start(bf16[32,2048]{1,0:T(8,128)(2,1)S(1)} %get-tuple-element.33), channel_id=1, source_target_pairs={{0,4},{4,0},{8,12},{12,8},{1,5},{5,1},{9,13},{13,9},{2,6},{6,2},{1... | collective-permute-start | bytes 393224 | tf_op jit(solution)/shard_map/ppermute | solution.py:289
  38.5 13.6 %collective-permute-start.9 = (bf16[32,2048]{1,0:T(8,128)(2,1)S(1)}, bf16[32,2048]{1,0:T(8,128)(2,1)S(1)}, u32[]{:S(2)}, u32[]{:S(2)}) collective-permute-start(bf16[32,2048]{1,0:T(8,128)(2,1)S(1)} %get-tuple-element.34), channel_id=1, source_target_pairs={{0,8},{4,12},{8,0},{12,4},{1,9},{5,13},{9,1},{13,5},{2,10},{6,14},... | collective-permute-start | bytes 393224 | tf_op jit(solution)/shard_map/ppermute | solution.py:289
  43.4 14.5 %collective-permute-start.15 = (bf16[128,1024]{1,0:T(8,128)(2,1)S(1)}, bf16[128,1024]{1,0:T(8,128)(2,1)S(1)}, u32[]{:S(2)}, u32[]{:S(2)}) collective-permute-start(bf16[128,1024]{1,0:T(8,128)(2,1)S(1)} %add.37), channel_id=1, source_target_pairs={{1,2},{2,1},{5,6},{6,5},{9,10},{10,9},{13,14},{14,13},{17,18},{18,... | collective-permute-start | bytes 786440 | tf_op jit(solution)/shard_map/ppermute | solution.py:327
  44.3 13.6 %collective-permute-start.13 = (bf16[128,1024]{1,0:T(8,128)(2,1)S(1)}, bf16[128,1024]{1,0:T(8,128)(2,1)S(1)}, u32[]{:S(2)}, u32[]{:S(2)}) collective-permute-start(bf16[128,1024]{1,0:T(8,128)(2,1)S(1)} %add.36), channel_id=1, source_target_pairs={{0,1},{1,0},{2,3},{3,2},{4,5},{5,4},{6,7},{7,6},{8,9},{9,8},{10,11... | collective-permute-start | bytes 786440 | tf_op jit(solution)/shard_map/ppermute | solution.py:327
  49.6 10.5 %collective-permute-start.7 = (bf16[128,1024]{1,0:T(8,128)(2,1)S(1)}, bf16[128,1024]{1,0:T(8,128)(2,1)S(1)}, u32[]{:S(2)}, u32[]{:S(2)}) collective-permute-start(bf16[128,1024]{1,0:T(8,128)(2,1)S(1)} %add.34), channel_id=1, source_target_pairs={{1,2},{2,1},{5,6},{6,5},{9,10},{10,9},{13,14},{14,13},{17,18},{18,... | collective-permute-start | bytes 786440 | tf_op jit(solution)/shard_map/ppermute | solution.py:327
  50.4 10.4 %collective-permute-start.5 = (bf16[128,1024]{1,0:T(8,128)(2,1)S(1)}, bf16[128,1024]{1,0:T(8,128)(2,1)S(1)}, u32[]{:S(2)}, u32[]{:S(2)}) collective-permute-start(bf16[128,1024]{1,0:T(8,128)(2,1)S(1)} %add.33), channel_id=1, source_target_pairs={{0,1},{1,0},{2,3},{3,2},{4,5},{5,4},{6,7},{7,6},{8,9},{9,8},{10,11... | collective-permute-start | bytes 786440 | tf_op jit(solution)/shard_map/ppermute | solution.py:327
  52.2 5.7 %collective-permute-start.10 = (bf16[32,2048]{1,0:T(8,128)(2,1)S(1)}, bf16[32,2048]{1,0:T(8,128)(2,1)S(1)}, u32[]{:S(2)}, u32[]{:S(2)}) collective-permute-start(bf16[32,2048]{1,0:T(8,128)(2,1)S(1)} %get-tuple-element.35), channel_id=1, source_target_pairs={{0,12},{4,8},{8,4},{12,0},{1,13},{5,9},{9,5},{13,1},{2,14},{6,10},... | collective-permute-start | bytes 393224 | tf_op jit(solution)/shard_map/ppermute | solution.py:289
  57.9 1.0 %copy-start = (f32[128,1024]{1,0:T(8,128)S(1)}, f32[128,1024]{1,0:T(8,128)}, u32[]{:S(2)}) copy-start(f32[128,1024]{1,0:T(8,128)} %get-tuple-element.39.own) | copy-start | bytes 1572868
  60.8 1.0 %copy-start.2 = (f32[128,1024]{1,0:T(8,128)S(1)}, f32[128,1024]{1,0:T(8,128)}, u32[]{:S(2)}) copy-start(f32[128,1024]{1,0:T(8,128)} %get-tuple-element.31.own) | copy-start | bytes 1572868
  63.0 5.4 %collective-permute-start.18 = (f32[8,128]{1,0:T(8,128)S(1)}, f32[8,128]{1,0:T(8,128)S(1)}, u32[]{:S(2)}, u32[]{:S(2)}) collective-permute-start(f32[8,128]{1,0:T(8,128)S(1)} %get-tuple-element.43), channel_id=1, source_target_pairs={{0,3},{1,2},{2,1},{3,0},{4,7},{5,6},{6,5},{7,4},{8,11},{9,10},{10,... | collective-permute-start | bytes 12296 | tf_op jit(solution)/shard_map/ppermute | solution.py:298
  64.8 4.5 %collective-permute-start.17 = (f32[8,128]{1,0:T(8,128)S(1)}, f32[8,128]{1,0:T(8,128)S(1)}, u32[]{:S(2)}, u32[]{:S(2)}) collective-permute-start(f32[8,128]{1,0:T(8,128)S(1)} %get-tuple-element.43), channel_id=1, source_target_pairs={{0,2},{1,3},{2,0},{3,1},{4,6},{5,7},{6,4},{7,5},{8,10},{9,11},{10,... | collective-permute-start | bytes 12296 | tf_op jit(solution)/shard_map/ppermute | solution.py:298
  66.2 3.6 %collective-permute-start.16 = (f32[8,128]{1,0:T(8,128)S(1)}, f32[8,128]{1,0:T(8,128)S(1)}, u32[]{:S(2)}, u32[]{:S(2)}) collective-permute-start(f32[8,128]{1,0:T(8,128)S(1)} %get-tuple-element.43), channel_id=1, source_target_pairs={{0,1},{1,0},{2,3},{3,2},{4,5},{5,4},{6,7},{7,6},{8,9},{9,8},{10,11... | collective-permute-start | bytes 12296 | tf_op jit(solution)/shard_map/ppermute | solution.py:298

commit v3 on v2

--- a/solution.py
+++ b/solution.py
@@ -22,6 +22,22 @@
 SMEM = pl.BlockSpec(memory_space=pltpu.SMEM)
 ANY = pl.BlockSpec(memory_space=pl.ANY)
 HBM = pl.BlockSpec(memory_space=pltpu.HBM)
+
+
+def near(shape, dtype=BF16):
+    return pltpu.VMEM(shape, dtype)
+
+
+def held(value):
+    return pltpu.with_memory_space_constraint(value, pltpu.VMEM)
+
+
+def far(value):
+    return pltpu.with_memory_space_constraint(value, pltpu.HBM)
+
+
+def together(*values):
+    return lax.optimization_barrier(values)
 
 
 def params(mib):
@@ -59,48 +75,74 @@
 
 def pack_qkv(send_rows, queries, keys_values, n_dp):
     rows, width = queries.shape
-    out = jax.ShapeDtypeStruct((rows // n_dp, width + 2 * HD), BF16)
+    out = near((rows // n_dp, width + 2 * HD))
     return pl.pallas_call(
         functools.partial(pack_qkv_kernel, width // HD),
         out_shape=[out] * n_dp,
         in_specs=[VMEM] * 3,
         out_specs=[VMEM] * n_dp,
         scratch_shapes=[pltpu.VMEM((rows, width + 2 * HD), BF16)],
-        compiler_params=params(63),
+        compiler_params=params(8),
         name="pack_qkv",
-    )(send_rows, queries, keys_values)
-
-
-def pack_hidden_kernel(send_ref, h_ref, *refs):
-    outs, buf = refs[:-1], refs[-1]
+    )(far(send_rows), far(queries), far(keys_values))
+
+
+FETCHES = 4
+
+
+class Fetch:
+    def __init__(self, order, place, w_ref, out, sems):
+        depth, width = out.shape
+        start = pl.multiple_of(order(place) * width, width)
+        share = depth // FETCHES
+        self.copies = []
+        for k in range(FETCHES):
+            rows = pl.ds(k * share, share)
+            self.copies.append(
+                pltpu.make_async_copy(w_ref.at[rows, pl.ds(start, width)], out.at[rows, :], sems.at[k])
+            )
+            self.copies[-1].start()
+
+    def wait(self):
+        for copy in self.copies:
+            copy.wait()
+
+
+def fetch_sems(blocks):
+    return pltpu.SemaphoreType.DMA((max(blocks, 1), FETCHES))
+
+
+def pack_hidden_kernel(n_dp, order, send_ref, h_ref, w_ref, *refs):
+    outs, blocks, (buf, sems) = refs[:n_dp], refs[n_dp:-2], refs[-2:]
+    copies = [Fetch(order, k, w_ref, block, sems.at[k]) for k, block in enumerate(blocks)]
     me = lax.axis_index("dp")
     buf[...] = reorder(one_hot_columns(send_ref), h_ref[...])
     share = outs[0].shape[0]
     for k, out in enumerate(outs):
         start = pl.multiple_of((me ^ k) * share, share)
         out[...] = buf[pl.ds(start, share), :]
-
-
-def pack_hidden(send_rows, hidden, n_dp):
+    for copy in copies:
+        copy.wait()
+
+
+def pack_hidden(send_rows, hidden, weight, n_dp, order, cols, blocks):
     rows, width = hidden.shape
-    out = jax.ShapeDtypeStruct((rows // n_dp, width), BF16)
-    return pl.pallas_call(
-        pack_hidden_kernel,
-        out_shape=[out] * n_dp,
-        in_specs=[VMEM] * 2,
-        out_specs=[VMEM] * n_dp,
-        scratch_shapes=[pltpu.VMEM((rows, width), BF16)],
-        compiler_params=params(4),
+    depth = weight.shape[0]
+    got = pl.pallas_call(
+        functools.partial(pack_hidden_kernel, n_dp, order),
+        out_shape=[near((rows // n_dp, width))] * n_dp + [near((depth, cols))] * blocks,
+        in_specs=[VMEM] * 2 + [HBM],
+        out_specs=[VMEM] * (n_dp + blocks),
+        scratch_shapes=[pltpu.VMEM((rows, width), BF16), fetch_sems(blocks)],
+        compiler_params=params(4 + 2 * blocks),
         name="pack_hidden",
-    )(send_rows, hidden)
-
-
-def attend_kernel(order, len_ref, *refs):
-    n_dp = len(refs) - 6
-    pieces, w_ref = refs[:n_dp], refs[n_dp]
-    out, first, buf, w_buf, sem = refs[n_dp + 1 :]
-    fetch = fetch_block(order, 0, w_ref, w_buf, sem)
-    fetch.start()
+    )(far(send_rows), far(hidden), far(weight))
+    return got[:n_dp], got[n_dp:]
+
+
+def attend_kernel(n_dp, len_ref, *refs):
+    pieces, refs = refs[:n_dp], refs[n_dp:]
+    w_ref, out, first, buf = refs if len(refs) == 4 else (None, refs[0], None, refs[1])
     me = lax.axis_index("dp")
     share = pieces[0].shape[0]
     for k, piece in enumerate(pieces):
@@ -133,96 +175,80 @@
     context = (mixed[:, :HD] / mixed[:, HD:]).astype(BF16)
     context = jnp.concatenate([context[h * rows : (h + 1) * rows] for h in range(heads)], axis=1)
     out[...] = context
-    fetch.wait()
-    first[...] = jnp.dot(context, w_buf[...], preferred_element_type=F32).astype(BF16)
-
-
-def fetch_block(order, place, w_ref, w_buf, sem):
-    width = w_buf.shape[1]
-    start = pl.multiple_of(order(place) * width, width)
-    return pltpu.make_async_copy(w_ref.at[:, pl.ds(start, width)], w_buf, sem)
-
-
-def attend(lengths, pieces, weight, order, cols):
+    if first is not None:
+        first[...] = jnp.dot(context, w_ref[...], preferred_element_type=F32).astype(BF16)
+
+
+def attend(lengths, pieces, block=None):
     n_dp = len(pieces)
     share, wide = pieces[0].shape
     rows, width = share * n_dp, wide - 2 * HD
+    args = [lengths, *map(held, pieces)]
+    outs = [near((rows, width))]
+    if block is not None:
+        args.append(held(block))
+        outs.append(near((rows, block.shape[1])))
     return pl.pallas_call(
-        functools.partial(attend_kernel, order),
+        functools.partial(attend_kernel, n_dp),
+        out_shape=outs,
+        in_specs=[SMEM] + [VMEM] * (len(args) - 1),
+        out_specs=[VMEM] * len(outs),
+        scratch_shapes=[pltpu.VMEM((rows, wide), BF16)],
+        compiler_params=params(8),
+        name="attend",
+    )(*args)
+
+
+def project_kernel(order, at, ctx_ref, w_ref, *outs):
+    for k, out in enumerate(outs):
+        width = out.shape[1]
+        start = pl.multiple_of(order(at + k) * width, width)
+        term = jnp.dot(ctx_ref[...], w_ref[:, pl.ds(start, width)], preferred_element_type=F32)
+        out[...] = term.astype(out.dtype)
+
+
+def project(context, weight, order, at, cols, kept):
+    rows, depth = context.shape
+    count = weight.shape[1] // cols - at
+    return pl.pallas_call(
+        functools.partial(project_kernel, order, at),
         out_shape=[
-            jax.ShapeDtypeStruct((rows, width), BF16),
-            jax.ShapeDtypeStruct((rows, cols), BF16),
+            near((rows, cols), F32 if place >= count - kept else BF16) for place in range(count)
         ],
-        in_specs=[SMEM] + [VMEM] * n_dp + [HBM],
-        out_specs=[VMEM] * 2,
-        scratch_shapes=[
-            pltpu.VMEM((rows, wide), BF16),
-            pltpu.VMEM((width, cols), BF16),
-            pltpu.SemaphoreType.DMA,
-        ],
-        compiler_params=params(52),
-        name="attend",
-    )(lengths, *pieces, weight)
-
-
-def project_kernel(order, ctx_ref, w_ref, *refs):
-    count = len(refs) - 2
-    outs, w_buf, sems = refs[:count], refs[count], refs[count + 1]
-    copies = [
-        fetch_block(order, place + 1, w_ref, w_buf.at[place], sems.at[place])
-        for place in range(count)
-    ]
-    for copy in copies:
-        copy.start()
-    for copy, out, place in zip(copies, outs, range(count)):
-        copy.wait()
-        term = jnp.dot(ctx_ref[...], w_buf[place], preferred_element_type=F32)
-        out[...] = term.astype(out.dtype)
-
-
-def project(context, weight, order, cols, kept):
-    rows, depth = context.shape
-    count = weight.shape[1] // cols - 1
-    return pl.pallas_call(
-        functools.partial(project_kernel, order),
-        out_shape=[
-            jax.ShapeDtypeStruct((rows, cols), F32 if place >= count - kept else BF16)
-            for place in range(count)
-        ],
-        in_specs=[VMEM, HBM],
+        in_specs=[VMEM] * 2,
         out_specs=[VMEM] * count,
-        scratch_shapes=[
-            pltpu.VMEM((count, depth, cols), BF16),
-            pltpu.SemaphoreType.DMA((count,)),
-        ],
-        compiler_params=params(52),
+        compiler_params=params(8),
         cost_estimate=pl.CostEstimate(
             flops=2 * rows * depth * cols * count,
             bytes_accessed=2 * depth * cols * count,
             transcendentals=0,
         ),
         name="project",
-    )(context, weight)
-
-
-def add_kernel(a_ref, b_ref, out):
-    out[...] = (a_ref[...].astype(F32) + b_ref[...].astype(F32)).astype(BF16)
-
-
-def add(a, b):
+    )(held(context), held(weight))
+
+
+def add_kernel(count, *refs):
+    for a_ref, b_ref, out in zip(refs[:count], refs[count : 2 * count], refs[-count:]):
+        out[...] = (a_ref[...].astype(F32) + b_ref[...].astype(F32)).astype(BF16)
+
+
+def add(*pairs, after=()):
+    count = len(pairs)
+    left, right = zip(*pairs)
     return pl.pallas_call(
-        add_kernel,
-        out_shape=jax.ShapeDtypeStruct(a.shape, BF16),
-        in_specs=[VMEM] * 2,
-        out_specs=VMEM,
+        functools.partial(add_kernel, count),
+        out_shape=[near(a.shape) for a in (*after, *left)],
+        in_specs=[VMEM] * (2 * count) + [ANY] * len(after),
+        out_specs=[ANY] * len(after) + [VMEM] * count,
+        input_output_aliases={2 * count + k: k for k in range(len(after))},
         compiler_params=params(4),
         name="add",
-    )(a, b)
+    )(*map(held, left), *map(held, right), *map(held, after))
 
 
 def finish_kernel(n_dp, part, width, recv_r, recv_l, own, scale_ref, head_ref, *refs):
     pieces = refs[:n_dp]
-    out, sums = refs[-2:]
+    restored_ref, sums, out, sem = refs[-4:]
     earlier = refs[n_dp + 1] if part else None
     me = lax.axis_index("dp")
     i = lax.axis_index("tensor")
@@ -246,6 +272,8 @@
         power += restored * restored
         start = pl.multiple_of(i * width + base + b * BLOCK, BLOCK)
         dots += restored * head_ref[:, pl.ds(start, BLOCK)].astype(F32)
+    copy = pltpu.make_async_copy(out, restored_ref.at[:, pl.ds(base, cols)], sem)
+    copy.start()
     total = jnp.concatenate(
         [
             jnp.sum(jnp.transpose(power), axis=0, keepdims=True),
@@ -257,47 +285,45 @@
     if part:
         total = total + earlier[...]
     sums[...] = total
+    copy.wait()
 
 
 def finish(part, recv_r, recv_l, own, scales, head_row, pieces, before):
     rows, cols = recv_r.shape
     width = pieces[0].shape[1]
     n_dp = len(pieces)
-    out_spec = pl.BlockSpec((rows, cols), lambda g: (0, part))
-    whole = lambda x: pl.BlockSpec(x.shape, lambda g: (0,) * x.ndim)
-    args = [recv_r, recv_l, own, scales, head_row, *pieces]
-    specs = [whole(x) for x in args]
+    args = [*map(held, (recv_r, recv_l, own)), scales, head_row, *map(held, pieces)]
+    specs = [VMEM] * len(args)
     aliases = {}
     if before is not None:
         aliases = {len(args): 0}
-        args += list(before)
-        specs += [ANY, whole(before[1])]
+        args += [before[0], held(before[1])]
+        specs += [ANY, VMEM]
     return pl.pallas_call(
         functools.partial(finish_kernel, n_dp, part, width),
-        grid=(1,),
         out_shape=[jax.ShapeDtypeStruct((rows, width), F32), jax.ShapeDtypeStruct((8, rows), F32)],
         in_specs=specs,
-        out_specs=[out_spec, pl.BlockSpec((8, rows), lambda g: (0, 0))],
+        out_specs=[ANY, VMEM],
         input_output_aliases=aliases,
+        scratch_shapes=[pltpu.VMEM((rows, cols), F32), pltpu.SemaphoreType.DMA],
         compiler_params=params(8),
         name="finish",
     )(*args)
 
 
+def swap(piece, axis, n, bits):
+    return lax.ppermute(piece, axis, [(i, i ^ bits) for i in range(n)])
+
+
 def exchange(pieces, axis, n):
-    return [pieces[0]] + [
-        lax.ppermute(pieces[k], axis, [(i, i ^ k) for i in range(n)]) for k in range(1, n)
-    ]
+    return [pieces[0]] + [swap(pieces[k], axis, n, k) for k in range(1, n)]
 
 
 def total_over(values, axis, n):
     done = 1
     while done < n:
         radix = min(4, n // done)
-        got = [values] + [
-            lax.ppermute(values, axis, [(i, i ^ (k * done)) for i in range(n)])
-            for k in range(1, radix)
-        ]
+        got = [values] + [swap(values, axis, n, k * done) for k in range(1, radix)]
         values = got[0] + got[1] if radix == 2 else (got[0] + got[1]) + (got[2] + got[3])
         done *= radix
     return values
@@ -320,20 +346,26 @@
     return order if n == 4 else lambda place: jnp.int32(place)
 
 
-def chain_scatter(terms):
+def chain_scatter(terms, beside):
     ends = [(0, 1), (3, 2)]
     pairs = [(0, 1), (1, 0), (2, 3), (3, 2)]
     middle = [(1, 2), (2, 1)]
     move = lambda value, perm: lax.ppermute(value, "tensor", perm)
-    outer = [move(terms[0], ends), move(terms[1], ends)]
-    inner = []
-    for place in range(4):
-        inner.append(move(add(terms[place], outer[place]), middle))
-        if place < 2:
-            outer.append(move(terms[place + 2], ends))
-        else:
-            outer.append(move(add(terms[place + 2], inner[place - 2]), pairs))
-    return [(outer[4 + part], inner[2 + part]) for part in range(2)]
+    t = list(terms)
+    outer = [move(t[0], ends), move(t[1], ends)]
+    t[2], t[3], sent = add((t[0], outer[0]), after=[t[2], t[3]])
+    outer.append(move(t[2], ends))
+    inner = [move(sent, middle)]
+    t[3], t[4], *beside, sent = add((t[1], outer[1]), after=[t[3], t[4], *beside])
+    outer.append(move(t[3], ends))
+    inner.append(move(sent, middle))
+    t[5], sent, owed = add((t[2], outer[2]), (t[4], inner[0]), after=[t[5]])
+    outer.append(move(owed, pairs))
+    inner.append(move(sent, middle))
+    sent, owed = add((t[3], outer[3]), (t[5], inner[1]))
+    outer.append(move(owed, pairs))
+    inner.append(move(sent, middle))
+    return [(outer[4 + part], inner[2 + part]) for part in range(2)], beside
 
 
 def per_device(
@@ -342,14 +374,20 @@
     chunks = 2
     cols = hidden_in.shape[1] // chunks
     order = block_order(n, chunks)
-    moved = exchange(pack_qkv(send_rows, queries, keys_values, n_dp), "dp", n_dp)
-    hidden = exchange(pack_hidden(send_rows, hidden_in, n_dp), "dp", n_dp)
-    context, first = attend(lengths, moved, out_weight, order, cols)
+    packed = pack_qkv(send_rows, queries, keys_values, n_dp)
+    *packed, hidden_in = together(*packed, hidden_in)
+    moved = exchange(packed, "dp", n_dp)
+    packed_hidden, w_early = pack_hidden(
+        send_rows, hidden_in, out_weight, n_dp, order, cols, 1 if n == 4 else 0
+    )
+    hidden = exchange(packed_hidden, "dp", n_dp)
     if n == 4:
-        rest = project(context, out_weight, order, cols, chunks)
+        context, first = attend(lengths, moved, w_early[0])
+        rest = project(context, out_weight, order, 1, cols, chunks)
         terms, own = [first, *rest[:-chunks]], rest[-chunks:]
-        recv = chain_scatter(terms)
+        recv, hidden[1:] = chain_scatter(terms, hidden[1:])
     else:
+        context = attend(lengths, moved)[0]
         partial_term = jnp.dot(context, out_weight, preferred_element_type=F32).astype(BF16)
         summed = lax.psum_scatter(partial_term, "tensor", scatter_dimension=1, tiled=True)
         zero = jnp.zeros((hidden_in.shape[0], cols), BF16)

time: 70.8 us -> 60 us (0.85)
  waiting for transfers between devices: 24.4 us -> 15.3 us
  starting transfers between devices: 26.4 us -> 31.6 us
  local copies, waits for them, and re-layouts: 3.78 us -> 0.17 us
  Pallas kernels: 14.4 us -> 11.3 us
    ppermute x9, waiting for transfers between devices: 12.7 us -> 5.58 us  [swap(): return lax.ppermute(piece, axis, [(i, i ^ bits) for i in range(n)])]
    ppermute x10, starting transfers between devices: 17.4 us -> 21.6 us  [chain_scatter(): move = lambda value, perm: lax.ppermute(value, 'tensor', perm)]
    unnamed x17 -> x9, local copies, waits for them, and re-layouts: 3.76 us -> 0.15 us
    pallas_call x11 -> x9, Pallas kernels: 12.3 us -> 9.7 us  [the longest x1 2.85 us: pack_hidden(): pl.pallas_call(functools.partial(pack_hidden_kernel, n_dp, order), out_sh...]
    ppermute x10, waiting for transfers between devices: 11.7 us -> 9.74 us  [chain_scatter(): move = lambda value, perm: lax.ppermute(value, 'tensor', perm)]
    ppermute x9, starting transfers between devices: 9.04 us -> 10 us  [swap(): return lax.ppermute(piece, axis, [(i, i ^ bits) for i in range(n)])]
where the time goes in v3:
time: 60 us; the launch traced here: 59.7 us
  starting transfers between devices  31.6 us (53%)
  waiting for transfers between devices  15.3 us (26%)
  Pallas kernels  11.3 us (19%)
  between operations  0.86 us (1%)
    ppermute x10, starting transfers between devices, chain_scatter(): move = lambda value, perm: lax.ppermute(value, 'tensor', perm)  21.6 us
    ppermute x9, starting transfers between devices, swap(): return lax.ppermute(piece, axis, [(i, i ^ bits) for i in range(n)])  10 us
    ppermute x10, waiting for transfers between devices, chain_scatter(): move = lambda value, perm: lax.ppermute(value, 'tensor', perm)  9.74 us
    ppermute x9, waiting for transfers between devices, swap(): return lax.ppermute(piece, axis, [(i, i ^ bits) for i in range(n)])  5.58 us
    pallas_call x1, Pallas kernels, pack_hidden(): pl.pallas_call(functools.partial(pack_hidden_kernel, n_dp, order), out_sh...  2.85 us
    pallas_call x2, Pallas kernels, finish(): pl.pallas_call(functools.partial(finish_kernel, n_dp, part, width), out_s...  2.28 us
    pallas_call x1, Pallas kernels, project(): pl.pallas_call(functools.partial(project_kernel, order, at), out_shape=[n...  2.11 us
    pallas_call x1, Pallas kernels, pack_qkv(): pl.pallas_call(functools.partial(pack_qkv_kernel, width // HD), out_shape...  1.56 us
  transfers between devices with their start and end apart: 19, of which 10 were waited for; matrix products, arithmetic and copies ran while one was open for 0% of the time, Pallas kernels for 12%

profile of v3, /device:TPU:0, one launch (start us, length us, event | category | flops | bytes accessed | tf_op | source)
XLA Modules:
  0.0 59.7 jit_solution(13738775904310164134)
XLA Ops:
  0.6 0.0 copy-start
  0.6 0.0 copy-start.1
  0.7 1.6 %pack_qkv.1 = (bf16[32,1280]{1,0:T(8,128)(2,1)S(1)}, bf16[32,1280]{1,0:T(8,128)(2,1)S(1)}, bf16[32,1280]{1,0:T(8,128)(2,1)S(1)}, bf16[32,1280]{1,0:T(8,128)(2,1)S(1)}) custom-call(s32[1,128]{1,0:T(1,128)} %send_ref.3, bf16[128,1024]{1,0:T(8,128)(2,1)} %q_ref.1, bf16[128,2,512]{2,1,0:T(2,128)(2,1)} %kv_ref.1), custom_call_target="tpu_custom_call" | custom-call | tf_op jit(solution)/shard_map/pack_qkv/pallas_call | solution.py:79
  2.2 0.0 copy-start.3
  2.2 0.0 copy-start.2
  2.2 0.5 collective-permute-start
  2.8 2.6 %collective-permute-start.1 = (bf16[32,1280]{1,0:T(8,128)(2,1)S(1)}, bf16[32,1280]{1,0:T(8,128)(2,1)S(1)}, u32[]{:S(2)}, u32[]{:S(2)}) collective-permute-start(bf16[32,1280]{1,0:T(8,128)(2,1)S(1)} %get-tuple-element.49), channel_id=1, source_target_pairs={{0,8},{4,12},{8,0},{12,4},{1,9},{5,13},{9,1},{13,5},{2,10},{6,14},... | collective-permute-start | bytes 245768 | tf_op jit(solution)/shard_map/ppermute | solution.py:315
  5.3 0.1 collective-permute-start.2
  5.4 2.9 %pack_hidden.1 = (bf16[32,2048]{1,0:T(8,128)(2,1)S(1)}, bf16[32,2048]{1,0:T(8,128)(2,1)S(1)}, bf16[32,2048]{1,0:T(8,128)(2,1)S(1)}, bf16[32,2048]{1,0:T(8,128)(2,1)S(1)}, bf16[1024,1024]{1,0:T(8,128)(2,1)S(1)}) custom-call(s32[1,128]{1,0:T(1,128)} %send_ref.3, bf16[128,2048]{1,0:T(8,128)(2,1)} %h_ref, bf16[1024,8192]{1,0:T(8,128)(2,1)} %w_ref.3), custom_call_target="tpu_custom_call" | custom-call | tf_op jit(solution)/shard_map/pack_hidden/pallas_call | solution.py:131
  8.3 0.0 collective-permute-done.refs_1_
  8.3 0.1 collective-permute-done.1.refs_2_
  8.4 1.5 %collective-permute-done.2.refs_3_ = bf16[32,1280]{1,0:T(8,128)(2,1)S(1)} collective-permute-done((bf16[32,1280]{1,0:T(8,128)(2,1)S(1)}, bf16[32,1280]{1,0:T(8,128)(2,1)S(1)}, u32[]{:S(2)}, u32[]{:S(2)}) %collective-permute-start.2) | collective-permute-done | bytes 81952 | tf_op jit(solution)/shard_map/ppermute | solution.py:315
  9.8 0.0 copy-done.1
  9.8 1.5 %attend.1 = (bf16[128,1024]{1,0:T(8,128)(2,1)S(1)}, bf16[128,1024]{1,0:T(8,128)(2,1)S(1)}) custom-call(s32[1,8]{1,0:T(1,128)S(1)} %copy-done.1, bf16[32,1280]{1,0:T(8,128)(2,1)S(1)} %get-tuple-element.47.refs_0_, bf16[32,1280]{1,0:T(8,128)(2,1)S(1)} %collective-permute-done.refs_1_, bf16[32,1280]{1,0:T(8,128)(2,1)S(1)} %collective-permute-done.1.refs_2_, ...), custom_call_target="tpu_custom_call" | custom-call | tf_op jit(solution)/shard_map/attend/pallas_call | solution.py:191
  11.3 3.7 %collective-permute-start.4 = (bf16[128,1024]{1,0:T(8,128)(2,1)S(1)}, bf16[128,1024]{1,0:T(8,128)(2,1)S(1)}, u32[]{:S(2)}, u32[]{:S(2)}) collective-permute-start(bf16[128,1024]{1,0:T(8,128)(2,1)S(1)} %get-tuple-element.55.refs_0_), channel_id=1, source_target_pairs={{0,1},{3,2},{4,5},{7,6},{8,9},{11,10},{12,13},{15,14},{16,17},{19,... | collective-permute-start | bytes 786440 | tf_op jit(solution)/shard_map/ppermute | solution.py:353
  15.0 0.0 copy-done
  15.0 2.1 %project.1 = (bf16[128,1024]{1,0:T(8,128)(2,1)S(1)}, bf16[128,1024]{1,0:T(8,128)(2,1)S(1)}, bf16[128,1024]{1,0:T(8,128)(2,1)S(1)}, bf16[128,1024]{1,0:T(8,128)(2...) custom-call(bf16[128,1024]{1,0:T(8,128)(2,1)S(1)} %get-tuple-element.53.ctx_ref, ...), custom_call_target="tpu_custom_call" | custom-call | flops 1879048192 | bytes 14680064 | tf_op jit(solution)/shard_map/project/pallas_call | solution.py:213
  17.2 1.3 %collective-permute-start.3 = (bf16[128,1024]{1,0:T(8,128)(2,1)S(1)}, bf16[128,1024]{1,0:T(8,128)(2,1)S(1)}, u32[]{:S(2)}, u32[]{:S(2)}) collective-permute-start(bf16[128,1024]{1,0:T(8,128)(2,1)S(1)} %get-tuple-element.54.refs_0_), channel_id=1, source_target_pairs={{0,1},{3,2},{4,5},{7,6},{8,9},{11,10},{12,13},{15,14},{16,17},{19,... | collective-permute-start | bytes 786440 | tf_op jit(solution)/shard_map/ppermute | solution.py:353
  18.5 0.1 collective-permute-start.5
  18.6 1.4 %collective-permute-start.6 = (bf16[32,2048]{1,0:T(8,128)(2,1)S(1)}, bf16[32,2048]{1,0:T(8,128)(2,1)S(1)}, u32[]{:S(2)}, u32[]{:S(2)}) collective-permute-start(bf16[32,2048]{1,0:T(8,128)(2,1)S(1)} %get-tuple-element.61), channel_id=1, source_target_pairs={{0,8},{4,12},{8,0},{12,4},{1,9},{5,13},{9,1},{13,5},{2,10},{6,14},... | collective-permute-start | bytes 393224 | tf_op jit(solution)/shard_map/ppermute | solution.py:315
  20.0 0.4 collective-permute-start.7
  20.4 1.3 %collective-permute-done.4.refs_1_ = bf16[128,1024]{1,0:T(8,128)(2,1)S(1)} collective-permute-done((bf16[128,1024]{1,0:T(8,128)(2,1)S(1)}, bf16[128,1024]{1,0:T(8,128)(2,1)S(1)}, u32[]{:S(2)}, u32[]{:S(2)}) %collective-permute-start.4) | collective-permute-done | bytes 262176 | tf_op jit(solution)/shard_map/ppermute | solution.py:353
  21.7 0.1 add.30
  21.7 4.4 %collective-permute-start.8 = (bf16[128,1024]{1,0:T(8,128)(2,1)S(1)}, bf16[128,1024]{1,0:T(8,128)(2,1)S(1)}, u32[]{:S(2)}, u32[]{:S(2)}) collective-permute-start(bf16[128,1024]{1,0:T(8,128)(2,1)S(1)} %get-tuple-element.64.refs_0_), channel_id=1, source_target_pairs={{0,1},{3,2},{4,5},{7,6},{8,9},{11,10},{12,13},{15,14},{16,17},{19,... | collective-permute-start | bytes 786440 | tf_op jit(solution)/shard_map/ppermute | solution.py:353
  26.1 0.0 collective-permute-done.5.refs_4_
  26.2 0.7 %collective-permute-start.9 = (bf16[128,1024]{1,0:T(8,128)(2,1)S(1)}, bf16[128,1024]{1,0:T(8,128)(2,1)S(1)}, u32[]{:S(2)}, u32[]{:S(2)}) collective-permute-start(bf16[128,1024]{1,0:T(8,128)(2,1)S(1)} %get-tuple-element.66), channel_id=1, source_target_pairs={{1,2},{2,1},{5,6},{6,5},{9,10},{10,9},{13,14},{14,13},{17,18},{18,... | collective-permute-start | bytes 786440 | tf_op jit(solution)/shard_map/ppermute | solution.py:353
  26.8 0.0 collective-permute-done.6.refs_5_
  26.8 0.0 collective-permute-done.7.refs_6_
  26.9 0.4 collective-permute-done.3.refs_1_
  27.3 0.1 add.31
  27.4 4.4 %collective-permute-start.10 = (bf16[128,1024]{1,0:T(8,128)(2,1)S(1)}, bf16[128,1024]{1,0:T(8,128)(2,1)S(1)}, u32[]{:S(2)}, u32[]{:S(2)}) collective-permute-start(bf16[128,1024]{1,0:T(8,128)(2,1)S(1)} %get-tuple-element.63.refs_0_), channel_id=1, source_target_pairs={{0,1},{3,2},{4,5},{7,6},{8,9},{11,10},{12,13},{15,14},{16,17},{19,... | collective-permute-start | bytes 786440 | tf_op jit(solution)/shard_map/ppermute | solution.py:353
  31.8 0.7 %collective-permute-start.11 = (bf16[128,1024]{1,0:T(8,128)(2,1)S(1)}, bf16[128,1024]{1,0:T(8,128)(2,1)S(1)}, u32[]{:S(2)}, u32[]{:S(2)}) collective-permute-start(bf16[128,1024]{1,0:T(8,128)(2,1)S(1)} %get-tuple-element.69), channel_id=1, source_target_pairs={{1,2},{2,1},{5,6},{6,5},{9,10},{10,9},{13,14},{14,13},{17,18},{18,... | collective-permute-start | bytes 786440 | tf_op jit(solution)/shard_map/ppermute | solution.py:353
  32.4 0.5 collective-permute-done.8.refs_2_
  32.9 0.0 collective-permute-done.9.refs_3_
  32.9 0.1 add.32
  33.0 2.5 %collective-permute-start.14 = (bf16[128,1024]{1,0:T(8,128)(2,1)S(1)}, bf16[128,1024]{1,0:T(8,128)(2,1)S(1)}, u32[]{:S(2)}, u32[]{:S(2)}) collective-permute-start(bf16[128,1024]{1,0:T(8,128)(2,1)S(1)} %get-tuple-element.77), channel_id=1, source_target_pairs={{0,1},{1,0},{2,3},{3,2},{4,5},{5,4},{6,7},{7,6},{8,9},{9,8},{10,11... | collective-permute-start | bytes 786440 | tf_op jit(solution)/shard_map/ppermute | solution.py:353
  35.6 0.7 %collective-permute-start.15 = (bf16[128,1024]{1,0:T(8,128)(2,1)S(1)}, bf16[128,1024]{1,0:T(8,128)(2,1)S(1)}, u32[]{:S(2)}, u32[]{:S(2)}) collective-permute-start(bf16[128,1024]{1,0:T(8,128)(2,1)S(1)} %get-tuple-element.78), channel_id=1, source_target_pairs={{1,2},{2,1},{5,6},{6,5},{9,10},{10,9},{13,14},{14,13},{17,18},{18,... | collective-permute-start | bytes 786440 | tf_op jit(solution)/shard_map/ppermute | solution.py:353
  36.3 2.3 %collective-permute-done.10.refs_2_ = bf16[128,1024]{1,0:T(8,128)(2,1)S(1)} collective-permute-done((bf16[128,1024]{1,0:T(8,128)(2,1)S(1)}, bf16[128,1024]{1,0:T(8,128)(2,1)S(1)}, u32[]{:S(2)}, u32[]{:S(2)}) %collective-permute-start.10) | collective-permute-done | bytes 262176 | tf_op jit(solution)/shard_map/ppermute | solution.py:353
  38.5 0.0 collective-permute-done.11.refs_3_
  38.5 0.8 %add.33 = (bf16[128,1024]{1,0:T(8,128)(2,1)S(1)}, bf16[128,1024]{1,0:T(8,128)(2,1)}) custom-call(bf16[128,1024]{1,0:T(8,128)(2,1)S(1)} %get-tuple-element.63.refs_0_, bf16[128,1024]{1,0:T(8,128)(2,1)S(1)} %get-tuple-element.68.refs_1_, bf16[128,1024]{1,0:T(8,128)(2,1)S(1)} %collective-permute-done.10.refs_2_, ...), custom_call_target="tpu_custom_call" | custom-call | tf_op jit(solution)/shard_map/add/pallas_call | solution.py:238
  39.3 2.5 %collective-permute-start.12 = (bf16[128,1024]{1,0:T(8,128)(2,1)}, bf16[128,1024]{1,0:T(8,128)(2,1)S(1)}, u32[]{:S(2)}, u32[]{:S(2)}) collective-permute-start(bf16[128,1024]{1,0:T(8,128)(2,1)} %get-tuple-element.70), channel_id=1, source_target_pairs={{0,1},{1,0},{2,3},{3,2},{4,5},{5,4},{6,7},{7,6},{8,9},{9,8},{10,11... | collective-permute-start | bytes 786440 | tf_op jit(solution)/shard_map/ppermute | solution.py:353
  41.8 0.7 %collective-permute-start.13 = (bf16[128,1024]{1,0:T(8,128)(2,1)S(1)}, bf16[128,1024]{1,0:T(8,128)(2,1)S(1)}, u32[]{:S(2)}, u32[]{:S(2)}) collective-permute-start(bf16[128,1024]{1,0:T(8,128)(2,1)S(1)} %get-tuple-element.71), channel_id=1, source_target_pairs={{1,2},{2,1},{5,6},{6,5},{9,10},{10,9},{13,14},{14,13},{17,18},{18,... | collective-permute-start | bytes 786440 | tf_op jit(solution)/shard_map/ppermute | solution.py:353
  42.4 0.0 copy-done.3
  42.4 0.1 copy.20.scale_ref
  42.6 0.0 copy-done.2
  42.6 1.5 %collective-permute-done.14.recv_r = bf16[128,1024]{1,0:T(8,128)(2,1)S(1)} collective-permute-done((bf16[128,1024]{1,0:T(8,128)(2,1)S(1)}, bf16[128,1024]{1,0:T(8,128)(2,1)S(1)}, u32[]{:S(2)}, u32[]{:S(2)}) %collective-permute-start.14) | collective-permute-done | bytes 262176 | tf_op jit(solution)/shard_map/ppermute | solution.py:353
  44.1 0.0 collective-permute-done.15.recv_l
  44.1 1.1 %finish.2 = (f32[128,2048]{1,0:T(8,128)}, f32[8,128]{1,0:T(8,128)S(1)}) custom-call(bf16[128,1024]{1,0:T(8,128)(2,1)S(1)} %collective-permute-done.14.recv_r, bf16[128,1024]{1,0:T(8,128)(2,1)S(1)} %collective-permute-done.15.recv_l, f32[128,1024]{1,0:T(8,128)S(1)} %get-tuple-element.79.own, bf16[128,16]{1,0:T(8,128)(2,1)S(1)} %copy.20.scale_ref, ...), custom_call_target="tpu_custom_call" | custom-call | tf_op jit(solution)/shard_map/finish/pallas_call | solution.py:302
  45.3 3.8 %collective-permute-done.12.recv_r = bf16[128,1024]{1,0:T(8,128)(2,1)S(1)} collective-permute-done((bf16[128,1024]{1,0:T(8,128)(2,1)}, bf16[128,1024]{1,0:T(8,128)(2,1)S(1)}, u32[]{:S(2)}, u32[]{:S(2)}) %collective-permute-start.12) | collective-permute-done | bytes 262176 | tf_op jit(solution)/shard_map/ppermute | solution.py:353
  49.1 0.0 collective-permute-done.13.recv_l
  49.1 1.1 %finish.3 = (f32[128,2048]{1,0:T(8,128)}, f32[8,128]{1,0:T(8,128)S(1)}) custom-call(bf16[128,1024]{1,0:T(8,128)(2,1)S(1)} %collective-permute-done.12.recv_r, bf16[128,1024]{1,0:T(8,128)(2,1)S(1)} %collective-permute-done.13.recv_l, f32[128,1024]{1,0:T(8,128)S(1)} %get-tuple-element.72.own, ...), custom_call_target="tpu_custom_call", output_to_operand_aliasing={{0}: (9, {})} | custom-call | tf_op jit(solution)/shard_map/finish/pallas_call | solution.py:302
  50.2 2.4 %collective-permute-start.16 = (f32[8,128]{1,0:T(8,128)S(1)}, f32[8,128]{1,0:T(8,128)S(1)}, u32[]{:S(2)}, u32[]{:S(2)}) collective-permute-start(f32[8,128]{1,0:T(8,128)S(1)} %get-tuple-element.83), channel_id=1, source_target_pairs={{0,1},{1,0},{2,3},{3,2},{4,5},{5,4},{6,7},{7,6},{8,9},{9,8},{10,11... | collective-permute-start | bytes 12296 | tf_op jit(solution)/shard_map/ppermute | solution.py:315
  52.7 1.1 %collective-permute-start.17 = (f32[8,128]{1,0:T(8,128)S(1)}, f32[8,128]{1,0:T(8,128)S(1)}, u32[]{:S(2)}, u32[]{:S(2)}) collective-permute-start(f32[8,128]{1,0:T(8,128)S(1)} %get-tuple-element.83), channel_id=1, source_target_pairs={{0,2},{1,3},{2,0},{3,1},{4,6},{5,7},{6,4},{7,5},{8,10},{9,11},{10,... | collective-permute-start | bytes 12296 | tf_op jit(solution)/shard_map/ppermute | solution.py:315
  53.8 1.4 %collective-permute-start.18 = (f32[8,128]{1,0:T(8,128)S(1)}, f32[8,128]{1,0:T(8,128)S(1)}, u32[]{:S(2)}, u32[]{:S(2)}) collective-permute-start(f32[8,128]{1,0:T(8,128)S(1)} %get-tuple-element.83), channel_id=1, source_target_pairs={{0,3},{1,2},{2,1},{3,0},{4,7},{5,6},{6,5},{7,4},{8,11},{9,10},{10,... | collective-permute-start | bytes 12296 | tf_op jit(solution)/shard_map/ppermute | solution.py:315
  55.1 0.0 collective-permute-done.16
  55.1 2.0 %collective-permute-done.17 = f32[8,128]{1,0:T(8,128)S(1)} collective-permute-done((f32[8,128]{1,0:T(8,128)S(1)}, f32[8,128]{1,0:T(8,128)S(1)}, u32[]{:S(2)}, u32[]{:S(2)}) %collective-permute-start.17) | collective-permute-done | bytes 4128 | tf_op jit(solution)/shard_map/ppermute | solution.py:315
  57.2 2.0 %collective-permute-done.18 = f32[8,128]{1,0:T(8,128)S(1)} collective-permute-done((f32[8,128]{1,0:T(8,128)S(1)}, f32[8,128]{1,0:T(8,128)S(1)}, u32[]{:S(2)}, u32[]{:S(2)}) %collective-permute-start.18) | collective-permute-done | bytes 4128 | tf_op jit(solution)/shard_map/ppermute | solution.py:315
  59.2 0.5 multiply_bitcast_fusion
  (2 shorter events, 0.0 us)
Async XLA Ops:
  0.6 14.4 %copy-start = (bf16[1024,8192]{1,0:T(8,128)(2,1)S(1)}, bf16[1024,8192]{1,0:T(8,128)(2,1)}, u32[]{:S(2)}) copy-start(bf16[1024,8192]{1,0:T(8,128)(2,1)} %w_ref.3) | copy-start | bytes 50331652
  0.6 9.2 %copy-start.1 = (s32[1,8]{1,0:T(1,128)S(1)}, s32[1,8]{1,0:T(1,128)}, u32[]{:S(2)}) copy-start(s32[1,8]{1,0:T(1,128)} %len_ref.1) | copy-start | bytes 100
  2.2 40.2 %copy-start.3 = (bf16[128,16]{0,1:T(8,128)(2,1)S(1)}, bf16[128,16]{0,1:T(8,128)(2,1)}, u32[]{:S(2)}) copy-start(bf16[128,16]{0,1:T(8,128)(2,1)} %param.14) | copy-start | bytes 12292
  2.2 40.3 %copy-start.2 = (bf16[8192]{0:T(1024)(128)(2,1)S(1)}, bf16[8192]{0:T(1024)(128)(2,1)}, u32[]{:S(2)}) copy-start(bf16[8192]{0:T(1024)(128)(2,1)} %param.15) | copy-start | bytes 49156
  2.2 6.0 %collective-permute-start = (bf16[32,1280]{1,0:T(8,128)(2,1)S(1)}, bf16[32,1280]{1,0:T(8,128)(2,1)S(1)}, u32[]{:S(2)}, u32[]{:S(2)}) collective-permute-start(bf16[32,1280]{1,0:T(8,128)(2,1)S(1)} %get-tuple-element.48), channel_id=1, source_target_pairs={{0,4},{4,0},{8,12},{12,8},{1,5},{5,1},{9,13},{13,9},{2,6},{6,2},{1... | collective-permute-start | bytes 245768 | tf_op jit(solution)/shard_map/ppermute | solution.py:315
  2.8 5.6 %collective-permute-start.1 = (bf16[32,1280]{1,0:T(8,128)(2,1)S(1)}, bf16[32,1280]{1,0:T(8,128)(2,1)S(1)}, u32[]{:S(2)}, u32[]{:S(2)}) collective-permute-start(bf16[32,1280]{1,0:T(8,128)(2,1)S(1)} %get-tuple-element.49), channel_id=1, source_target_pairs={{0,8},{4,12},{8,0},{12,4},{1,9},{5,13},{9,1},{13,5},{2,10},{6,14},... | collective-permute-start | bytes 245768 | tf_op jit(solution)/shard_map/ppermute | solution.py:315
  5.3 4.5 %collective-permute-start.2 = (bf16[32,1280]{1,0:T(8,128)(2,1)S(1)}, bf16[32,1280]{1,0:T(8,128)(2,1)S(1)}, u32[]{:S(2)}, u32[]{:S(2)}) collective-permute-start(bf16[32,1280]{1,0:T(8,128)(2,1)S(1)} %get-tuple-element.50), channel_id=1, source_target_pairs={{0,12},{4,8},{8,4},{12,0},{1,13},{5,9},{9,5},{13,1},{2,14},{6,10},... | collective-permute-start | bytes 245768 | tf_op jit(solution)/shard_map/ppermute | solution.py:315
  11.3 10.4 %collective-permute-start.4 = (bf16[128,1024]{1,0:T(8,128)(2,1)S(1)}, bf16[128,1024]{1,0:T(8,128)(2,1)S(1)}, u32[]{:S(2)}, u32[]{:S(2)}) collective-permute-start(bf16[128,1024]{1,0:T(8,128)(2,1)S(1)} %get-tuple-element.55.refs_0_), channel_id=1, source_target_pairs={{0,1},{3,2},{4,5},{7,6},{8,9},{11,10},{12,13},{15,14},{16,17},{19,... | collective-permute-start | bytes 786440 | tf_op jit(solution)/shard_map/ppermute | solution.py:353
  17.2 10.1 %collective-permute-start.3 = (bf16[128,1024]{1,0:T(8,128)(2,1)S(1)}, bf16[128,1024]{1,0:T(8,128)(2,1)S(1)}, u32[]{:S(2)}, u32[]{:S(2)}) collective-permute-start(bf16[128,1024]{1,0:T(8,128)(2,1)S(1)} %get-tuple-element.54.refs_0_), channel_id=1, source_target_pairs={{0,1},{3,2},{4,5},{7,6},{8,9},{11,10},{12,13},{15,14},{16,17},{19,... | collective-permute-start | bytes 786440 | tf_op jit(solution)/shard_map/ppermute | solution.py:353
  18.5 7.7 %collective-permute-start.5 = (bf16[32,2048]{1,0:T(8,128)(2,1)S(1)}, bf16[32,2048]{1,0:T(8,128)(2,1)S(1)}, u32[]{:S(2)}, u32[]{:S(2)}) collective-permute-start(bf16[32,2048]{1,0:T(8,128)(2,1)S(1)} %get-tuple-element.60), channel_id=1, source_target_pairs={{0,4},{4,0},{8,12},{12,8},{1,5},{5,1},{9,13},{13,9},{2,6},{6,2},{1... | collective-permute-start | bytes 393224 | tf_op jit(solution)/shard_map/ppermute | solution.py:315
  18.6 8.3 %collective-permute-start.6 = (bf16[32,2048]{1,0:T(8,128)(2,1)S(1)}, bf16[32,2048]{1,0:T(8,128)(2,1)S(1)}, u32[]{:S(2)}, u32[]{:S(2)}) collective-permute-start(bf16[32,2048]{1,0:T(8,128)(2,1)S(1)} %get-tuple-element.61), channel_id=1, source_target_pairs={{0,8},{4,12},{8,0},{12,4},{1,9},{5,13},{9,1},{13,5},{2,10},{6,14},... | collective-permute-start | bytes 393224 | tf_op jit(solution)/shard_map/ppermute | solution.py:315
  20.0 6.9 %collective-permute-start.7 = (bf16[32,2048]{1,0:T(8,128)(2,1)S(1)}, bf16[32,2048]{1,0:T(8,128)(2,1)S(1)}, u32[]{:S(2)}, u32[]{:S(2)}) collective-permute-start(bf16[32,2048]{1,0:T(8,128)(2,1)S(1)} %get-tuple-element.62), channel_id=1, source_target_pairs={{0,12},{4,8},{8,4},{12,0},{1,13},{5,9},{9,5},{13,1},{2,14},{6,10},... | collective-permute-start | bytes 393224 | tf_op jit(solution)/shard_map/ppermute | solution.py:315
  21.7 11.2 %collective-permute-start.8 = (bf16[128,1024]{1,0:T(8,128)(2,1)S(1)}, bf16[128,1024]{1,0:T(8,128)(2,1)S(1)}, u32[]{:S(2)}, u32[]{:S(2)}) collective-permute-start(bf16[128,1024]{1,0:T(8,128)(2,1)S(1)} %get-tuple-element.64.refs_0_), channel_id=1, source_target_pairs={{0,1},{3,2},{4,5},{7,6},{8,9},{11,10},{12,13},{15,14},{16,17},{19,... | collective-permute-start | bytes 786440 | tf_op jit(solution)/shard_map/ppermute | solution.py:353
  26.2 6.8 %collective-permute-start.9 = (bf16[128,1024]{1,0:T(8,128)(2,1)S(1)}, bf16[128,1024]{1,0:T(8,128)(2,1)S(1)}, u32[]{:S(2)}, u32[]{:S(2)}) collective-permute-start(bf16[128,1024]{1,0:T(8,128)(2,1)S(1)} %get-tuple-element.66), channel_id=1, source_target_pairs={{1,2},{2,1},{5,6},{6,5},{9,10},{10,9},{13,14},{14,13},{17,18},{18,... | collective-permute-start | bytes 786440 | tf_op jit(solution)/shard_map/ppermute | solution.py:353
  27.4 11.2 %collective-permute-start.10 = (bf16[128,1024]{1,0:T(8,128)(2,1)S(1)}, bf16[128,1024]{1,0:T(8,128)(2,1)S(1)}, u32[]{:S(2)}, u32[]{:S(2)}) collective-permute-start(bf16[128,1024]{1,0:T(8,128)(2,1)S(1)} %get-tuple-element.63.refs_0_), channel_id=1, source_target_pairs={{0,1},{3,2},{4,5},{7,6},{8,9},{11,10},{12,13},{15,14},{16,17},{19,... | collective-permute-start | bytes 786440 | tf_op jit(solution)/shard_map/ppermute | solution.py:353
  31.8 6.8 %collective-permute-start.11 = (bf16[128,1024]{1,0:T(8,128)(2,1)S(1)}, bf16[128,1024]{1,0:T(8,128)(2,1)S(1)}, u32[]{:S(2)}, u32[]{:S(2)}) collective-permute-start(bf16[128,1024]{1,0:T(8,128)(2,1)S(1)} %get-tuple-element.69), channel_id=1, source_target_pairs={{1,2},{2,1},{5,6},{6,5},{9,10},{10,9},{13,14},{14,13},{17,18},{18,... | collective-permute-start | bytes 786440 | tf_op jit(solution)/shard_map/ppermute | solution.py:353
  33.0 11.1 %collective-permute-start.14 = (bf16[128,1024]{1,0:T(8,128)(2,1)S(1)}, bf16[128,1024]{1,0:T(8,128)(2,1)S(1)}, u32[]{:S(2)}, u32[]{:S(2)}) collective-permute-start(bf16[128,1024]{1,0:T(8,128)(2,1)S(1)} %get-tuple-element.77), channel_id=1, source_target_pairs={{0,1},{1,0},{2,3},{3,2},{4,5},{5,4},{6,7},{7,6},{8,9},{9,8},{10,11... | collective-permute-start | bytes 786440 | tf_op jit(solution)/shard_map/ppermute | solution.py:353
  35.6 8.6 %collective-permute-start.15 = (bf16[128,1024]{1,0:T(8,128)(2,1)S(1)}, bf16[128,1024]{1,0:T(8,128)(2,1)S(1)}, u32[]{:S(2)}, u32[]{:S(2)}) collective-permute-start(bf16[128,1024]{1,0:T(8,128)(2,1)S(1)} %get-tuple-element.78), channel_id=1, source_target_pairs={{1,2},{2,1},{5,6},{6,5},{9,10},{10,9},{13,14},{14,13},{17,18},{18,... | collective-permute-start | bytes 786440 | tf_op jit(solution)/shard_map/ppermute | solution.py:353
  39.3 9.8 %collective-permute-start.12 = (bf16[128,1024]{1,0:T(8,128)(2,1)}, bf16[128,1024]{1,0:T(8,128)(2,1)S(1)}, u32[]{:S(2)}, u32[]{:S(2)}) collective-permute-start(bf16[128,1024]{1,0:T(8,128)(2,1)} %get-tuple-element.70), channel_id=1, source_target_pairs={{0,1},{1,0},{2,3},{3,2},{4,5},{5,4},{6,7},{7,6},{8,9},{9,8},{10,11... | collective-permute-start | bytes 786440 | tf_op jit(solution)/shard_map/ppermute | solution.py:353
  41.8 7.3 %collective-permute-start.13 = (bf16[128,1024]{1,0:T(8,128)(2,1)S(1)}, bf16[128,1024]{1,0:T(8,128)(2,1)S(1)}, u32[]{:S(2)}, u32[]{:S(2)}) collective-permute-start(bf16[128,1024]{1,0:T(8,128)(2,1)S(1)} %get-tuple-element.71), channel_id=1, source_target_pairs={{1,2},{2,1},{5,6},{6,5},{9,10},{10,9},{13,14},{14,13},{17,18},{18,... | collective-permute-start | bytes 786440 | tf_op jit(solution)/shard_map/ppermute | solution.py:353
  50.2 4.9 %collective-permute-start.16 = (f32[8,128]{1,0:T(8,128)S(1)}, f32[8,128]{1,0:T(8,128)S(1)}, u32[]{:S(2)}, u32[]{:S(2)}) collective-permute-start(f32[8,128]{1,0:T(8,128)S(1)} %get-tuple-element.83), channel_id=1, source_target_pairs={{0,1},{1,0},{2,3},{3,2},{4,5},{5,4},{6,7},{7,6},{8,9},{9,8},{10,11... | collective-permute-start | bytes 12296 | tf_op jit(solution)/shard_map/ppermute | solution.py:315
  52.7 4.5 %collective-permute-start.17 = (f32[8,128]{1,0:T(8,128)S(1)}, f32[8,128]{1,0:T(8,128)S(1)}, u32[]{:S(2)}, u32[]{:S(2)}) collective-permute-start(f32[8,128]{1,0:T(8,128)S(1)} %get-tuple-element.83), channel_id=1, source_target_pairs={{0,2},{1,3},{2,0},{3,1},{4,6},{5,7},{6,4},{7,5},{8,10},{9,11},{10,... | collective-permute-start | bytes 12296 | tf_op jit(solution)/shard_map/ppermute | solution.py:315
  53.8 5.4 %collective-permute-start.18 = (f32[8,128]{1,0:T(8,128)S(1)}, f32[8,128]{1,0:T(8,128)S(1)}, u32[]{:S(2)}, u32[]{:S(2)}) collective-permute-start(f32[8,128]{1,0:T(8,128)S(1)} %get-tuple-element.83), channel_id=1, source_target_pairs={{0,3},{1,2},{2,1},{3,0},{4,7},{5,6},{6,5},{7,4},{8,11},{9,10},{10,... | collective-permute-start | bytes 12296 | tf_op jit(solution)/shard_map/ppermute | solution.py:315

commit v4 on v3

--- a/solution.py
+++ b/solution.py
@@ -145,7 +145,7 @@
     w_ref, out, first, buf = refs if len(refs) == 4 else (None, refs[0], None, refs[1])
     me = lax.axis_index("dp")
     share = pieces[0].shape[0]
-    for k, piece in enumerate(pieces):
+    for k, piece in zip(arrivals(n_dp), pieces):
         start = pl.multiple_of((me ^ k) * share, share)
         buf[pl.ds(start, share), :] = piece[...]
     rows, width = out.shape
@@ -179,11 +179,15 @@
         first[...] = jnp.dot(context, w_ref[...], preferred_element_type=F32).astype(BF16)
 
 
+def arrivals(n_dp):
+    return [0, 2, 1, *range(3, n_dp)] if n_dp > 2 else [*range(n_dp)]
+
+
 def attend(lengths, pieces, block=None):
     n_dp = len(pieces)
     share, wide = pieces[0].shape
     rows, width = share * n_dp, wide - 2 * HD
-    args = [lengths, *map(held, pieces)]
+    args = [lengths, *(held(pieces[k]) for k in arrivals(n_dp))]
     outs = [near((rows, width))]
     if block is not None:
         args.append(held(block))
@@ -248,8 +252,8 @@
 
 def finish_kernel(n_dp, part, width, recv_r, recv_l, own, scale_ref, head_ref, *refs):
     pieces = refs[:n_dp]
-    restored_ref, sums, out, sem = refs[-4:]
-    earlier = refs[n_dp + 1] if part else None
+    out, sums = refs[-2:]
+    earlier = refs[n_dp] if part else None
     me = lax.axis_index("dp")
     i = lax.axis_index("tensor")
     share = pieces[0].shape[0]
@@ -272,8 +276,6 @@
         power += restored * restored
         start = pl.multiple_of(i * width + base + b * BLOCK, BLOCK)
         dots += restored * head_ref[:, pl.ds(start, BLOCK)].astype(F32)
-    copy = pltpu.make_async_copy(out, restored_ref.at[:, pl.ds(base, cols)], sem)
-    copy.start()
     total = jnp.concatenate(
         [
             jnp.sum(jnp.transpose(power), axis=0, keepdims=True),
@@ -285,29 +287,51 @@
     if part:
         total = total + earlier[...]
     sums[...] = total
-    copy.wait()
-
-
-def finish(part, recv_r, recv_l, own, scales, head_row, pieces, before):
+
+
+def finish(part, recv_r, recv_l, own, scales, head_row, pieces, earlier=None, stored=None):
     rows, cols = recv_r.shape
     width = pieces[0].shape[1]
     n_dp = len(pieces)
     args = [*map(held, (recv_r, recv_l, own)), scales, head_row, *map(held, pieces)]
-    specs = [VMEM] * len(args)
-    aliases = {}
-    if before is not None:
-        aliases = {len(args): 0}
-        args += [before[0], held(before[1])]
-        specs += [ANY, VMEM]
+    outs = [near((rows, cols), F32), near((8, rows), F32)]
+    if part:
+        args += [held(earlier), far(stored)]
+        outs = [jax.ShapeDtypeStruct(stored.shape, F32), *outs]
     return pl.pallas_call(
         functools.partial(finish_kernel, n_dp, part, width),
-        out_shape=[jax.ShapeDtypeStruct((rows, width), F32), jax.ShapeDtypeStruct((8, rows), F32)],
-        in_specs=specs,
-        out_specs=[ANY, VMEM],
-        input_output_aliases=aliases,
-        scratch_shapes=[pltpu.VMEM((rows, cols), F32), pltpu.SemaphoreType.DMA],
+        out_shape=outs,
+        in_specs=[VMEM] * (len(args) - 1) + [ANY if part else VMEM],
+        out_specs=[ANY] * (len(outs) - 2) + [VMEM] * 2,
+        input_output_aliases={len(args) - 1: 0} if part else {},
         compiler_params=params(8),
         name="finish",
+    )(*args)
+
+
+def store_kernel(part, value_ref, *refs):
+    out, sem = refs[-2:]
+    cols = value_ref.shape[1]
+    copy = pltpu.make_async_copy(value_ref, out.at[:, pl.ds(part * cols, cols)], sem)
+    copy.start()
+    copy.wait()
+
+
+def store(part, chunks, value, before):
+    rows, cols = value.shape
+    args = [held(value)] + ([] if before is None else [before])
+    return pl.pallas_call(
+        functools.partial(store_kernel, part),
+        out_shape=jax.ShapeDtypeStruct((rows, cols * chunks), F32),
+        in_specs=[VMEM] + [ANY] * (len(args) - 1),
+        out_specs=ANY,
+        input_output_aliases={1: 0} if len(args) > 1 else {},
+        scratch_shapes=[pltpu.SemaphoreType.DMA],
+        compiler_params=params(4),
+        cost_estimate=pl.CostEstimate(
+            flops=0, bytes_accessed=4 * rows * cols, transcendentals=0
+        ),
+        name="store",
     )(*args)
 
 
@@ -324,7 +348,7 @@
     while done < n:
         radix = min(4, n // done)
         got = [values] + [swap(values, axis, n, k * done) for k in range(1, radix)]
-        values = got[0] + got[1] if radix == 2 else (got[0] + got[1]) + (got[2] + got[3])
+        values = got[0] + got[1] if radix == 2 else (got[2] + got[0]) + (got[1] + got[3])
         done *= radix
     return values
 
@@ -394,10 +418,12 @@
         recv = [(summed[:, part * cols : (part + 1) * cols], zero) for part in range(chunks)]
         own = [zero] * chunks
     head_row = value_head.reshape(1, D)
-    result = None
+    restored = sums = None
     for part in range(chunks):
-        result = finish(part, *recv[part], own[part], block_scales, head_row, hidden, result)
-    restored, sums = result
+        *rest, value, sums = finish(
+            part, *recv[part], own[part], block_scales, head_row, hidden, sums, restored
+        )
+        restored = store(part, chunks, value, rest[0] if rest else None)
     sums = total_over(sums, "tensor", n)
     values = sums[1] / jnp.sqrt(sums[0] / D + EPS)
     return restored, values

time: 60 us -> 58.8 us (0.980)
  waiting for transfers between devices: 15.3 us -> 13.5 us
    pallas_call x0 -> x2, Pallas kernels: none -> 1.61 us  [store(): pl.pallas_call(functools.partial(store_kernel, part), out_shape=jax.Shape...]
    ppermute x9, waiting for transfers between devices: 5.58 us -> 4.13 us  [swap(): return lax.ppermute(piece, axis, [(i, i ^ bits) for i in range(n)])]
    pallas_call x2, Pallas kernels: 2.28 us -> 0.84 us  [finish(): pl.pallas_call(functools.partial(finish_kernel, n_dp, part, width), out_s...]
  transfers between devices with their start and end apart: 19 -> 19, of which waited for: 10 -> 9; matrix products, arithmetic and copies ran while one was open for 0% -> 0% of each run, Pallas kernels for 12% -> 14%
where the time goes in v4:
time: 58.8 us; the launch traced here: 58.5 us
  starting transfers between devices  32.1 us (55%)
  waiting for transfers between devices  13.5 us (23%)
  Pallas kernels  11.4 us (19%)
  between operations  0.88 us (1%)
    ppermute x10, starting transfers between devices, chain_scatter(): move = lambda value, perm: lax.ppermute(value, 'tensor', perm)  21.9 us
    ppermute x9, starting transfers between devices, swap(): return lax.ppermute(piece, axis, [(i, i ^ bits) for i in range(n)])  10.1 us
    ppermute x10, waiting for transfers between devices, chain_scatter(): move = lambda value, perm: lax.ppermute(value, 'tensor', perm)  9.38 us
    ppermute x9, waiting for transfers between devices, swap(): return lax.ppermute(piece, axis, [(i, i ^ bits) for i in range(n)])  4.13 us
    pallas_call x1, Pallas kernels, pack_hidden(): pl.pallas_call(functools.partial(pack_hidden_kernel, n_dp, order), out_sh...  2.79 us
    pallas_call x1, Pallas kernels, project(): pl.pallas_call(functools.partial(project_kernel, order, at), out_shape=[n...  2.11 us
    pallas_call x2, Pallas kernels, store(): pl.pallas_call(functools.partial(store_kernel, part), out_shape=jax.Shape...  1.61 us
    pallas_call x1, Pallas kernels, pack_qkv(): pl.pallas_call(functools.partial(pack_qkv_kernel, width // HD), out_shape...  1.56 us
  transfers between devices with their start and end apart: 19, of which 9 were waited for; matrix products, arithmetic and copies ran while one was open for 0% of the time, Pallas kernels for 14%

profile of v4, /device:TPU:0, one launch (start us, length us, event | category | flops | bytes accessed | tf_op | source)
XLA Modules:
  0.0 58.5 jit_solution(1430039156034776809)
XLA Ops:
  0.6 0.0 copy-start
  0.6 0.0 copy-start.1
  0.7 1.6 %pack_qkv.1 = (bf16[32,1280]{1,0:T(8,128)(2,1)S(1)}, bf16[32,1280]{1,0:T(8,128)(2,1)S(1)}, bf16[32,1280]{1,0:T(8,128)(2,1)S(1)}, bf16[32,1280]{1,0:T(8,128)(2,1)S(1)}) custom-call(s32[1,128]{1,0:T(1,128)} %send_ref.3, bf16[128,1024]{1,0:T(8,128)(2,1)} %q_ref.1, bf16[128,2,512]{2,1,0:T(2,128)(2,1)} %kv_ref.1), custom_call_target="tpu_custom_call" | custom-call | tf_op jit(solution)/shard_map/pack_qkv/pallas_call | solution.py:79
  2.2 0.0 copy-start.3
  2.2 0.0 copy-start.2
  2.2 3.0 %collective-permute-start = (bf16[32,1280]{1,0:T(8,128)(2,1)S(1)}, bf16[32,1280]{1,0:T(8,128)(2,1)S(1)}, u32[]{:S(2)}, u32[]{:S(2)}) collective-permute-start(bf16[32,1280]{1,0:T(8,128)(2,1)S(1)} %get-tuple-element.49), channel_id=1, source_target_pairs={{0,8},{4,12},{8,0},{12,4},{1,9},{5,13},{9,1},{13,5},{2,10},{6,14},... | collective-permute-start | bytes 245768 | tf_op jit(solution)/shard_map/ppermute | solution.py:339
  5.3 0.0 collective-permute-start.1
  5.3 0.2 collective-permute-start.2
  5.5 2.8 %pack_hidden.1 = (bf16[32,2048]{1,0:T(8,128)(2,1)S(1)}, bf16[32,2048]{1,0:T(8,128)(2,1)S(1)}, bf16[32,2048]{1,0:T(8,128)(2,1)S(1)}, bf16[32,2048]{1,0:T(8,128)(2,1)S(1)}, bf16[1024,1024]{1,0:T(8,128)(2,1)S(1)}) custom-call(s32[1,128]{1,0:T(1,128)} %send_ref.3, bf16[128,2048]{1,0:T(8,128)(2,1)} %h_ref, bf16[1024,8192]{1,0:T(8,128)(2,1)} %w_ref.3), custom_call_target="tpu_custom_call" | custom-call | tf_op jit(solution)/shard_map/pack_hidden/pallas_call | solution.py:131
  8.3 0.0 collective-permute-done.refs_1_
  8.3 0.0 collective-permute-done.1.refs_2_
  8.3 1.1 %collective-permute-done.2.refs_3_ = bf16[32,1280]{1,0:T(8,128)(2,1)S(1)} collective-permute-done((bf16[32,1280]{1,0:T(8,128)(2,1)S(1)}, bf16[32,1280]{1,0:T(8,128)(2,1)S(1)}, u32[]{:S(2)}, u32[]{:S(2)}) %collective-permute-start.2) | collective-permute-done | bytes 81952 | tf_op jit(solution)/shard_map/ppermute | solution.py:339
  9.4 0.0 copy-done.1
  9.4 1.5 %attend.1 = (bf16[128,1024]{1,0:T(8,128)(2,1)S(1)}, bf16[128,1024]{1,0:T(8,128)(2,1)S(1)}) custom-call(s32[1,8]{1,0:T(1,128)S(1)} %copy-done.1, bf16[32,1280]{1,0:T(8,128)(2,1)S(1)} %get-tuple-element.48.refs_0_, bf16[32,1280]{1,0:T(8,128)(2,1)S(1)} %collective-permute-done.refs_1_, bf16[32,1280]{1,0:T(8,128)(2,1)S(1)} %collective-permute-done.1.refs_2_, ...), custom_call_target="tpu_custom_call" | custom-call | tf_op jit(solution)/shard_map/attend/pallas_call | solution.py:195
  10.8 3.5 %collective-permute-start.4 = (bf16[128,1024]{1,0:T(8,128)(2,1)S(1)}, bf16[128,1024]{1,0:T(8,128)(2,1)S(1)}, u32[]{:S(2)}, u32[]{:S(2)}) collective-permute-start(bf16[128,1024]{1,0:T(8,128)(2,1)S(1)} %get-tuple-element.56.refs_0_), channel_id=1, source_target_pairs={{0,1},{3,2},{4,5},{7,6},{8,9},{11,10},{12,13},{15,14},{16,17},{19,... | collective-permute-start | bytes 786440 | tf_op jit(solution)/shard_map/ppermute | solution.py:377
  14.3 0.0 copy-done
  14.3 2.1 %project.1 = (bf16[128,1024]{1,0:T(8,128)(2,1)S(1)}, bf16[128,1024]{1,0:T(8,128)(2,1)S(1)}, bf16[128,1024]{1,0:T(8,128)(2,1)S(1)}, bf16[128,1024]{1,0:T(8,128)(2...) custom-call(bf16[128,1024]{1,0:T(8,128)(2,1)S(1)} %get-tuple-element.54.ctx_ref, ...), custom_call_target="tpu_custom_call" | custom-call | flops 1879048192 | bytes 14680064 | tf_op jit(solution)/shard_map/project/pallas_call | solution.py:217
  16.5 1.3 %collective-permute-start.3 = (bf16[128,1024]{1,0:T(8,128)(2,1)S(1)}, bf16[128,1024]{1,0:T(8,128)(2,1)S(1)}, u32[]{:S(2)}, u32[]{:S(2)}) collective-permute-start(bf16[128,1024]{1,0:T(8,128)(2,1)S(1)} %get-tuple-element.55.refs_0_), channel_id=1, source_target_pairs={{0,1},{3,2},{4,5},{7,6},{8,9},{11,10},{12,13},{15,14},{16,17},{19,... | collective-permute-start | bytes 786440 | tf_op jit(solution)/shard_map/ppermute | solution.py:377
  17.8 0.2 collective-permute-start.5
  18.0 1.4 %collective-permute-start.6 = (bf16[32,2048]{1,0:T(8,128)(2,1)S(1)}, bf16[32,2048]{1,0:T(8,128)(2,1)S(1)}, u32[]{:S(2)}, u32[]{:S(2)}) collective-permute-start(bf16[32,2048]{1,0:T(8,128)(2,1)S(1)} %get-tuple-element.62), channel_id=1, source_target_pairs={{0,8},{4,12},{8,0},{12,4},{1,9},{5,13},{9,1},{13,5},{2,10},{6,14},... | collective-permute-start | bytes 393224 | tf_op jit(solution)/shard_map/ppermute | solution.py:339
  19.4 0.3 collective-permute-start.7
  19.7 1.2 %collective-permute-done.4.refs_1_ = bf16[128,1024]{1,0:T(8,128)(2,1)S(1)} collective-permute-done((bf16[128,1024]{1,0:T(8,128)(2,1)S(1)}, bf16[128,1024]{1,0:T(8,128)(2,1)S(1)}, u32[]{:S(2)}, u32[]{:S(2)}) %collective-permute-start.4) | collective-permute-done | bytes 262176 | tf_op jit(solution)/shard_map/ppermute | solution.py:377
  20.9 0.1 add.30
  21.0 4.4 %collective-permute-start.8 = (bf16[128,1024]{1,0:T(8,128)(2,1)S(1)}, bf16[128,1024]{1,0:T(8,128)(2,1)S(1)}, u32[]{:S(2)}, u32[]{:S(2)}) collective-permute-start(bf16[128,1024]{1,0:T(8,128)(2,1)S(1)} %get-tuple-element.65.refs_0_), channel_id=1, source_target_pairs={{0,1},{3,2},{4,5},{7,6},{8,9},{11,10},{12,13},{15,14},{16,17},{19,... | collective-permute-start | bytes 786440 | tf_op jit(solution)/shard_map/ppermute | solution.py:377
  25.4 0.0 collective-permute-done.5.refs_4_
  25.4 0.7 %collective-permute-start.9 = (bf16[128,1024]{1,0:T(8,128)(2,1)S(1)}, bf16[128,1024]{1,0:T(8,128)(2,1)S(1)}, u32[]{:S(2)}, u32[]{:S(2)}) collective-permute-start(bf16[128,1024]{1,0:T(8,128)(2,1)S(1)} %get-tuple-element.67), channel_id=1, source_target_pairs={{1,2},{2,1},{5,6},{6,5},{9,10},{10,9},{13,14},{14,13},{17,18},{18,... | collective-permute-start | bytes 786440 | tf_op jit(solution)/shard_map/ppermute | solution.py:377
  26.1 0.0 collective-permute-done.6.refs_5_
  26.1 0.0 collective-permute-done.7.refs_6_
  26.1 0.4 collective-permute-done.3.refs_1_
  26.5 0.1 add.31
  26.6 4.4 %collective-permute-start.10 = (bf16[128,1024]{1,0:T(8,128)(2,1)S(1)}, bf16[128,1024]{1,0:T(8,128)(2,1)S(1)}, u32[]{:S(2)}, u32[]{:S(2)}) collective-permute-start(bf16[128,1024]{1,0:T(8,128)(2,1)S(1)} %get-tuple-element.64.refs_0_), channel_id=1, source_target_pairs={{0,1},{3,2},{4,5},{7,6},{8,9},{11,10},{12,13},{15,14},{16,17},{19,... | collective-permute-start | bytes 786440 | tf_op jit(solution)/shard_map/ppermute | solution.py:377
  31.0 0.7 %collective-permute-start.11 = (bf16[128,1024]{1,0:T(8,128)(2,1)S(1)}, bf16[128,1024]{1,0:T(8,128)(2,1)S(1)}, u32[]{:S(2)}, u32[]{:S(2)}) collective-permute-start(bf16[128,1024]{1,0:T(8,128)(2,1)S(1)} %get-tuple-element.70), channel_id=1, source_target_pairs={{1,2},{2,1},{5,6},{6,5},{9,10},{10,9},{13,14},{14,13},{17,18},{18,... | collective-permute-start | bytes 786440 | tf_op jit(solution)/shard_map/ppermute | solution.py:377
  31.7 0.5 collective-permute-done.8.refs_2_
  32.2 0.0 collective-permute-done.9.refs_3_
  32.2 0.1 add.32
  32.3 2.5 %collective-permute-start.14 = (bf16[128,1024]{1,0:T(8,128)(2,1)S(1)}, bf16[128,1024]{1,0:T(8,128)(2,1)S(1)}, u32[]{:S(2)}, u32[]{:S(2)}) collective-permute-start(bf16[128,1024]{1,0:T(8,128)(2,1)S(1)} %get-tuple-element.78), channel_id=1, source_target_pairs={{0,1},{1,0},{2,3},{3,2},{4,5},{5,4},{6,7},{7,6},{8,9},{9,8},{10,11... | collective-permute-start | bytes 786440 | tf_op jit(solution)/shard_map/ppermute | solution.py:377
  34.8 0.7 %collective-permute-start.15 = (bf16[128,1024]{1,0:T(8,128)(2,1)S(1)}, bf16[128,1024]{1,0:T(8,128)(2,1)S(1)}, u32[]{:S(2)}, u32[]{:S(2)}) collective-permute-start(bf16[128,1024]{1,0:T(8,128)(2,1)S(1)} %get-tuple-element.79), channel_id=1, source_target_pairs={{1,2},{2,1},{5,6},{6,5},{9,10},{10,9},{13,14},{14,13},{17,18},{18,... | collective-permute-start | bytes 786440 | tf_op jit(solution)/shard_map/ppermute | solution.py:377
  35.5 2.3 %collective-permute-done.10.refs_2_ = bf16[128,1024]{1,0:T(8,128)(2,1)S(1)} collective-permute-done((bf16[128,1024]{1,0:T(8,128)(2,1)S(1)}, bf16[128,1024]{1,0:T(8,128)(2,1)S(1)}, u32[]{:S(2)}, u32[]{:S(2)}) %collective-permute-start.10) | collective-permute-done | bytes 262176 | tf_op jit(solution)/shard_map/ppermute | solution.py:377
  37.8 0.0 collective-permute-done.11.refs_3_
  37.8 0.8 %add.33 = (bf16[128,1024]{1,0:T(8,128)(2,1)S(1)}, bf16[128,1024]{1,0:T(8,128)(2,1)}) custom-call(bf16[128,1024]{1,0:T(8,128)(2,1)S(1)} %get-tuple-element.64.refs_0_, bf16[128,1024]{1,0:T(8,128)(2,1)S(1)} %get-tuple-element.69.refs_1_, bf16[128,1024]{1,0:T(8,128)(2,1)S(1)} %collective-permute-done.10.refs_2_, ...), custom_call_target="tpu_custom_call" | custom-call | tf_op jit(solution)/shard_map/add/pallas_call | solution.py:242
  38.5 3.1 %collective-permute-start.12 = (bf16[128,1024]{1,0:T(8,128)(2,1)}, bf16[128,1024]{1,0:T(8,128)(2,1)S(1)}, u32[]{:S(2)}, u32[]{:S(2)}) collective-permute-start(bf16[128,1024]{1,0:T(8,128)(2,1)} %get-tuple-element.71), channel_id=1, source_target_pairs={{0,1},{1,0},{2,3},{3,2},{4,5},{5,4},{6,7},{7,6},{8,9},{9,8},{10,11... | collective-permute-start | bytes 786440 | tf_op jit(solution)/shard_map/ppermute | solution.py:377
  41.6 0.7 %collective-permute-start.13 = (bf16[128,1024]{1,0:T(8,128)(2,1)S(1)}, bf16[128,1024]{1,0:T(8,128)(2,1)S(1)}, u32[]{:S(2)}, u32[]{:S(2)}) collective-permute-start(bf16[128,1024]{1,0:T(8,128)(2,1)S(1)} %get-tuple-element.72), channel_id=1, source_target_pairs={{1,2},{2,1},{5,6},{6,5},{9,10},{10,9},{13,14},{14,13},{17,18},{18,... | collective-permute-start | bytes 786440 | tf_op jit(solution)/shard_map/ppermute | solution.py:377
  42.3 0.0 copy-done.3
  42.3 0.1 copy.21.scale_ref
  42.4 0.0 copy-done.2
  42.4 1.0 %collective-permute-done.14.recv_r = bf16[128,1024]{1,0:T(8,128)(2,1)S(1)} collective-permute-done((bf16[128,1024]{1,0:T(8,128)(2,1)S(1)}, bf16[128,1024]{1,0:T(8,128)(2,1)S(1)}, u32[]{:S(2)}, u32[]{:S(2)}) %collective-permute-start.14) | collective-permute-done | bytes 262176 | tf_op jit(solution)/shard_map/ppermute | solution.py:377
  43.4 0.0 collective-permute-done.15.recv_l
  43.4 0.4 finish.2
  43.8 0.8 %store.2.refs_5_ = f32[128,2048]{1,0:T(8,128)} custom-call(f32[128,1024]{1,0:T(8,128)S(1)} %get-tuple-element.82.value_ref), custom_call_target="tpu_custom_call" | custom-call | bytes 524288 | tf_op jit(solution)/shard_map/store/pallas_call | solution.py:323
  44.6 4.0 %collective-permute-done.12.recv_r = bf16[128,1024]{1,0:T(8,128)(2,1)S(1)} collective-permute-done((bf16[128,1024]{1,0:T(8,128)(2,1)}, bf16[128,1024]{1,0:T(8,128)(2,1)S(1)}, u32[]{:S(2)}, u32[]{:S(2)}) %collective-permute-start.12) | collective-permute-done | bytes 262176 | tf_op jit(solution)/shard_map/ppermute | solution.py:377
  48.7 0.0 collective-permute-done.13.recv_l
  48.7 0.4 finish.3
  49.1 3.5 %collective-permute-start.16 = (f32[8,128]{1,0:T(8,128)S(1)}, f32[8,128]{1,0:T(8,128)S(1)}, u32[]{:S(2)}, u32[]{:S(2)}) collective-permute-start(f32[8,128]{1,0:T(8,128)S(1)} %get-tuple-element.85), channel_id=1, source_target_pairs={{0,2},{1,3},{2,0},{3,1},{4,6},{5,7},{6,4},{7,5},{8,10},{9,11},{10,... | collective-permute-start | bytes 12296 | tf_op jit(solution)/shard_map/ppermute | solution.py:339
  52.6 0.0 collective-permute-start.17
  52.6 1.5 %collective-permute-start.18 = (f32[8,128]{1,0:T(8,128)S(1)}, f32[8,128]{1,0:T(8,128)S(1)}, u32[]{:S(2)}, u32[]{:S(2)}) collective-permute-start(f32[8,128]{1,0:T(8,128)S(1)} %get-tuple-element.85), channel_id=1, source_target_pairs={{0,3},{1,2},{2,1},{3,0},{4,7},{5,6},{6,5},{7,4},{8,11},{9,10},{10,... | collective-permute-start | bytes 12296 | tf_op jit(solution)/shard_map/ppermute | solution.py:339
  54.1 0.8 %store.3 = f32[128,2048]{1,0:T(8,128)} custom-call(f32[128,1024]{1,0:T(8,128)S(1)} %get-tuple-element.83.value_ref, f32[128,2048]{1,0:T(8,128)} %get-tuple-element.84.refs_0_), custom_call_target="tpu_custom_call", output_to_operand_aliasing={{}: (1, {})} | custom-call | bytes 524288 | tf_op jit(solution)/shard_map/store/pallas_call | solution.py:323
  54.9 0.0 collective-permute-done.16
  54.9 1.2 %collective-permute-done.17 = f32[8,128]{1,0:T(8,128)S(1)} collective-permute-done((f32[8,128]{1,0:T(8,128)S(1)}, f32[8,128]{1,0:T(8,128)S(1)}, u32[]{:S(2)}, u32[]{:S(2)}) %collective-permute-start.17) | collective-permute-done | bytes 4128 | tf_op jit(solution)/shard_map/ppermute | solution.py:339
  56.2 1.8 %collective-permute-done.18 = f32[8,128]{1,0:T(8,128)S(1)} collective-permute-done((f32[8,128]{1,0:T(8,128)S(1)}, f32[8,128]{1,0:T(8,128)S(1)}, u32[]{:S(2)}, u32[]{:S(2)}) %collective-permute-start.18) | collective-permute-done | bytes 4128 | tf_op jit(solution)/shard_map/ppermute | solution.py:339
  58.0 0.5 multiply_bitcast_fusion
  (2 shorter events, 0.0 us)
Async XLA Ops:
  0.6 13.7 %copy-start = (bf16[1024,8192]{1,0:T(8,128)(2,1)S(1)}, bf16[1024,8192]{1,0:T(8,128)(2,1)}, u32[]{:S(2)}) copy-start(bf16[1024,8192]{1,0:T(8,128)(2,1)} %w_ref.3) | copy-start | bytes 50331652
  0.6 8.7 %copy-start.1 = (s32[1,8]{1,0:T(1,128)S(1)}, s32[1,8]{1,0:T(1,128)}, u32[]{:S(2)}) copy-start(s32[1,8]{1,0:T(1,128)} %len_ref.1) | copy-start | bytes 100
  2.2 40.1 %copy-start.3 = (bf16[128,16]{0,1:T(8,128)(2,1)S(1)}, bf16[128,16]{0,1:T(8,128)(2,1)}, u32[]{:S(2)}) copy-start(bf16[128,16]{0,1:T(8,128)(2,1)} %param.14) | copy-start | bytes 12292
  2.2 40.2 %copy-start.2 = (bf16[8192]{0:T(1024)(128)(2,1)S(1)}, bf16[8192]{0:T(1024)(128)(2,1)}, u32[]{:S(2)}) copy-start(bf16[8192]{0:T(1024)(128)(2,1)} %param.15) | copy-start | bytes 49156
  2.2 6.0 %collective-permute-start = (bf16[32,1280]{1,0:T(8,128)(2,1)S(1)}, bf16[32,1280]{1,0:T(8,128)(2,1)S(1)}, u32[]{:S(2)}, u32[]{:S(2)}) collective-permute-start(bf16[32,1280]{1,0:T(8,128)(2,1)S(1)} %get-tuple-element.49), channel_id=1, source_target_pairs={{0,8},{4,12},{8,0},{12,4},{1,9},{5,13},{9,1},{13,5},{2,10},{6,14},... | collective-permute-start | bytes 245768 | tf_op jit(solution)/shard_map/ppermute | solution.py:339
  5.3 3.0 %collective-permute-start.1 = (bf16[32,1280]{1,0:T(8,128)(2,1)S(1)}, bf16[32,1280]{1,0:T(8,128)(2,1)S(1)}, u32[]{:S(2)}, u32[]{:S(2)}) collective-permute-start(bf16[32,1280]{1,0:T(8,128)(2,1)S(1)} %get-tuple-element.50), channel_id=1, source_target_pairs={{0,4},{4,0},{8,12},{12,8},{1,5},{5,1},{9,13},{13,9},{2,6},{6,2},{1... | collective-permute-start | bytes 245768 | tf_op jit(solution)/shard_map/ppermute | solution.py:339
  5.3 4.1 %collective-permute-start.2 = (bf16[32,1280]{1,0:T(8,128)(2,1)S(1)}, bf16[32,1280]{1,0:T(8,128)(2,1)S(1)}, u32[]{:S(2)}, u32[]{:S(2)}) collective-permute-start(bf16[32,1280]{1,0:T(8,128)(2,1)S(1)} %get-tuple-element.51), channel_id=1, source_target_pairs={{0,12},{4,8},{8,4},{12,0},{1,13},{5,9},{9,5},{13,1},{2,14},{6,10},... | collective-permute-start | bytes 245768 | tf_op jit(solution)/shard_map/ppermute | solution.py:339
  10.8 10.1 %collective-permute-start.4 = (bf16[128,1024]{1,0:T(8,128)(2,1)S(1)}, bf16[128,1024]{1,0:T(8,128)(2,1)S(1)}, u32[]{:S(2)}, u32[]{:S(2)}) collective-permute-start(bf16[128,1024]{1,0:T(8,128)(2,1)S(1)} %get-tuple-element.56.refs_0_), channel_id=1, source_target_pairs={{0,1},{3,2},{4,5},{7,6},{8,9},{11,10},{12,13},{15,14},{16,17},{19,... | collective-permute-start | bytes 786440 | tf_op jit(solution)/shard_map/ppermute | solution.py:377
  16.5 10.1 %collective-permute-start.3 = (bf16[128,1024]{1,0:T(8,128)(2,1)S(1)}, bf16[128,1024]{1,0:T(8,128)(2,1)S(1)}, u32[]{:S(2)}, u32[]{:S(2)}) collective-permute-start(bf16[128,1024]{1,0:T(8,128)(2,1)S(1)} %get-tuple-element.55.refs_0_), channel_id=1, source_target_pairs={{0,1},{3,2},{4,5},{7,6},{8,9},{11,10},{12,13},{15,14},{16,17},{19,... | collective-permute-start | bytes 786440 | tf_op jit(solution)/shard_map/ppermute | solution.py:377
  17.8 7.6 %collective-permute-start.5 = (bf16[32,2048]{1,0:T(8,128)(2,1)S(1)}, bf16[32,2048]{1,0:T(8,128)(2,1)S(1)}, u32[]{:S(2)}, u32[]{:S(2)}) collective-permute-start(bf16[32,2048]{1,0:T(8,128)(2,1)S(1)} %get-tuple-element.61), channel_id=1, source_target_pairs={{0,4},{4,0},{8,12},{12,8},{1,5},{5,1},{9,13},{13,9},{2,6},{6,2},{1... | collective-permute-start | bytes 393224 | tf_op jit(solution)/shard_map/ppermute | solution.py:339
  18.0 8.1 %collective-permute-start.6 = (bf16[32,2048]{1,0:T(8,128)(2,1)S(1)}, bf16[32,2048]{1,0:T(8,128)(2,1)S(1)}, u32[]{:S(2)}, u32[]{:S(2)}) collective-permute-start(bf16[32,2048]{1,0:T(8,128)(2,1)S(1)} %get-tuple-element.62), channel_id=1, source_target_pairs={{0,8},{4,12},{8,0},{12,4},{1,9},{5,13},{9,1},{13,5},{2,10},{6,14},... | collective-permute-start | bytes 393224 | tf_op jit(solution)/shard_map/ppermute | solution.py:339
  19.4 6.7 %collective-permute-start.7 = (bf16[32,2048]{1,0:T(8,128)(2,1)S(1)}, bf16[32,2048]{1,0:T(8,128)(2,1)S(1)}, u32[]{:S(2)}, u32[]{:S(2)}) collective-permute-start(bf16[32,2048]{1,0:T(8,128)(2,1)S(1)} %get-tuple-element.63), channel_id=1, source_target_pairs={{0,12},{4,8},{8,4},{12,0},{1,13},{5,9},{9,5},{13,1},{2,14},{6,10},... | collective-permute-start | bytes 393224 | tf_op jit(solution)/shard_map/ppermute | solution.py:339
  21.0 11.2 %collective-permute-start.8 = (bf16[128,1024]{1,0:T(8,128)(2,1)S(1)}, bf16[128,1024]{1,0:T(8,128)(2,1)S(1)}, u32[]{:S(2)}, u32[]{:S(2)}) collective-permute-start(bf16[128,1024]{1,0:T(8,128)(2,1)S(1)} %get-tuple-element.65.refs_0_), channel_id=1, source_target_pairs={{0,1},{3,2},{4,5},{7,6},{8,9},{11,10},{12,13},{15,14},{16,17},{19,... | collective-permute-start | bytes 786440 | tf_op jit(solution)/shard_map/ppermute | solution.py:377
  25.4 6.8 %collective-permute-start.9 = (bf16[128,1024]{1,0:T(8,128)(2,1)S(1)}, bf16[128,1024]{1,0:T(8,128)(2,1)S(1)}, u32[]{:S(2)}, u32[]{:S(2)}) collective-permute-start(bf16[128,1024]{1,0:T(8,128)(2,1)S(1)} %get-tuple-element.67), channel_id=1, source_target_pairs={{1,2},{2,1},{5,6},{6,5},{9,10},{10,9},{13,14},{14,13},{17,18},{18,... | collective-permute-start | bytes 786440 | tf_op jit(solution)/shard_map/ppermute | solution.py:377
  26.6 11.2 %collective-permute-start.10 = (bf16[128,1024]{1,0:T(8,128)(2,1)S(1)}, bf16[128,1024]{1,0:T(8,128)(2,1)S(1)}, u32[]{:S(2)}, u32[]{:S(2)}) collective-permute-start(bf16[128,1024]{1,0:T(8,128)(2,1)S(1)} %get-tuple-element.64.refs_0_), channel_id=1, source_target_pairs={{0,1},{3,2},{4,5},{7,6},{8,9},{11,10},{12,13},{15,14},{16,17},{19,... | collective-permute-start | bytes 786440 | tf_op jit(solution)/shard_map/ppermute | solution.py:377
  31.0 6.8 %collective-permute-start.11 = (bf16[128,1024]{1,0:T(8,128)(2,1)S(1)}, bf16[128,1024]{1,0:T(8,128)(2,1)S(1)}, u32[]{:S(2)}, u32[]{:S(2)}) collective-permute-start(bf16[128,1024]{1,0:T(8,128)(2,1)S(1)} %get-tuple-element.70), channel_id=1, source_target_pairs={{1,2},{2,1},{5,6},{6,5},{9,10},{10,9},{13,14},{14,13},{17,18},{18,... | collective-permute-start | bytes 786440 | tf_op jit(solution)/shard_map/ppermute | solution.py:377
  32.3 11.1 %collective-permute-start.14 = (bf16[128,1024]{1,0:T(8,128)(2,1)S(1)}, bf16[128,1024]{1,0:T(8,128)(2,1)S(1)}, u32[]{:S(2)}, u32[]{:S(2)}) collective-permute-start(bf16[128,1024]{1,0:T(8,128)(2,1)S(1)} %get-tuple-element.78), channel_id=1, source_target_pairs={{0,1},{1,0},{2,3},{3,2},{4,5},{5,4},{6,7},{7,6},{8,9},{9,8},{10,11... | collective-permute-start | bytes 786440 | tf_op jit(solution)/shard_map/ppermute | solution.py:377
  34.8 8.6 %collective-permute-start.15 = (bf16[128,1024]{1,0:T(8,128)(2,1)S(1)}, bf16[128,1024]{1,0:T(8,128)(2,1)S(1)}, u32[]{:S(2)}, u32[]{:S(2)}) collective-permute-start(bf16[128,1024]{1,0:T(8,128)(2,1)S(1)} %get-tuple-element.79), channel_id=1, source_target_pairs={{1,2},{2,1},{5,6},{6,5},{9,10},{10,9},{13,14},{14,13},{17,18},{18,... | collective-permute-start | bytes 786440 | tf_op jit(solution)/shard_map/ppermute | solution.py:377
  38.5 10.1 %collective-permute-start.12 = (bf16[128,1024]{1,0:T(8,128)(2,1)}, bf16[128,1024]{1,0:T(8,128)(2,1)S(1)}, u32[]{:S(2)}, u32[]{:S(2)}) collective-permute-start(bf16[128,1024]{1,0:T(8,128)(2,1)} %get-tuple-element.71), channel_id=1, source_target_pairs={{0,1},{1,0},{2,3},{3,2},{4,5},{5,4},{6,7},{7,6},{8,9},{9,8},{10,11... | collective-permute-start | bytes 786440 | tf_op jit(solution)/shard_map/ppermute | solution.py:377
  41.6 7.1 %collective-permute-start.13 = (bf16[128,1024]{1,0:T(8,128)(2,1)S(1)}, bf16[128,1024]{1,0:T(8,128)(2,1)S(1)}, u32[]{:S(2)}, u32[]{:S(2)}) collective-permute-start(bf16[128,1024]{1,0:T(8,128)(2,1)S(1)} %get-tuple-element.72), channel_id=1, source_target_pairs={{1,2},{2,1},{5,6},{6,5},{9,10},{10,9},{13,14},{14,13},{17,18},{18,... | collective-permute-start | bytes 786440 | tf_op jit(solution)/shard_map/ppermute | solution.py:377
  49.1 5.8 %collective-permute-start.16 = (f32[8,128]{1,0:T(8,128)S(1)}, f32[8,128]{1,0:T(8,128)S(1)}, u32[]{:S(2)}, u32[]{:S(2)}) collective-permute-start(f32[8,128]{1,0:T(8,128)S(1)} %get-tuple-element.85), channel_id=1, source_target_pairs={{0,2},{1,3},{2,0},{3,1},{4,6},{5,7},{6,4},{7,5},{8,10},{9,11},{10,... | collective-permute-start | bytes 12296 | tf_op jit(solution)/shard_map/ppermute | solution.py:339
  52.6 3.6 %collective-permute-start.17 = (f32[8,128]{1,0:T(8,128)S(1)}, f32[8,128]{1,0:T(8,128)S(1)}, u32[]{:S(2)}, u32[]{:S(2)}) collective-permute-start(f32[8,128]{1,0:T(8,128)S(1)} %get-tuple-element.85), channel_id=1, source_target_pairs={{0,1},{1,0},{2,3},{3,2},{4,5},{5,4},{6,7},{7,6},{8,9},{9,8},{10,11... | collective-permute-start | bytes 12296 | tf_op jit(solution)/shard_map/ppermute | solution.py:339
  52.6 5.4 %collective-permute-start.18 = (f32[8,128]{1,0:T(8,128)S(1)}, f32[8,128]{1,0:T(8,128)S(1)}, u32[]{:S(2)}, u32[]{:S(2)}) collective-permute-start(f32[8,128]{1,0:T(8,128)S(1)} %get-tuple-element.85), channel_id=1, source_target_pairs={{0,3},{1,2},{2,1},{3,0},{4,7},{5,6},{6,5},{7,4},{8,11},{9,10},{10,... | collective-permute-start | bytes 12296 | tf_op jit(solution)/shard_map/ppermute | solution.py:339

commit v5 on v4

--- a/solution.py
+++ b/solution.py
@@ -140,15 +140,14 @@
     return got[:n_dp], got[n_dp:]
 
 
-def attend_kernel(n_dp, len_ref, *refs):
-    pieces, refs = refs[:n_dp], refs[n_dp:]
-    w_ref, out, first, buf = refs if len(refs) == 4 else (None, refs[0], None, refs[1])
+def attention(len_ref, pieces, buf, width):
+    n_dp = len(pieces)
+    rows = buf.shape[0]
     me = lax.axis_index("dp")
     share = pieces[0].shape[0]
     for k, piece in zip(arrivals(n_dp), pieces):
         start = pl.multiple_of((me ^ k) * share, share)
         buf[pl.ds(start, share), :] = piece[...]
-    rows, width = out.shape
     row_id = lax.broadcasted_iota(jnp.int32, (rows, rows), 0)
     col_id = lax.broadcasted_iota(jnp.int32, (rows, rows), 1)
     row_seg = jnp.zeros((rows, rows), jnp.int32)
@@ -173,9 +172,26 @@
     weights = weights.reshape(heads * rows, rows).astype(BF16)
     mixed = jnp.dot(weights, values, preferred_element_type=F32)
     context = (mixed[:, :HD] / mixed[:, HD:]).astype(BF16)
-    context = jnp.concatenate([context[h * rows : (h + 1) * rows] for h in range(heads)], axis=1)
-    out[...] = context
-    if first is not None:
+    return jnp.concatenate([context[h * rows : (h + 1) * rows] for h in range(heads)], axis=1)
+
+
+def attend_kernel(len_ref, *refs):
+    pieces, out, buf = refs[:-2], refs[-2], refs[-1]
+    out[...] = attention(len_ref, pieces, buf, out.shape[1])
+
+
+def at_an_end():
+    i = lax.axis_index("tensor")
+    return (i == 0) | (i == 3)
+
+
+def first_kernel(len_ref, *refs):
+    pieces, (w_ref, out, first, buf) = refs[:-4], refs[-4:]
+
+    @pl.when(at_an_end())
+    def _():
+        context = attention(len_ref, pieces, buf, out.shape[1])
+        out[...] = context
         first[...] = jnp.dot(context, w_ref[...], preferred_element_type=F32).astype(BF16)
 
 
@@ -183,44 +199,69 @@
     return [0, 2, 1, *range(3, n_dp)] if n_dp > 2 else [*range(n_dp)]
 
 
-def attend(lengths, pieces, block=None):
-    n_dp = len(pieces)
+def arrived(pieces):
+    return [held(pieces[k]) for k in arrivals(len(pieces))]
+
+
+def attend(lengths, pieces):
     share, wide = pieces[0].shape
-    rows, width = share * n_dp, wide - 2 * HD
-    args = [lengths, *(held(pieces[k]) for k in arrivals(n_dp))]
-    outs = [near((rows, width))]
-    if block is not None:
-        args.append(held(block))
-        outs.append(near((rows, block.shape[1])))
-    return pl.pallas_call(
-        functools.partial(attend_kernel, n_dp),
-        out_shape=outs,
-        in_specs=[SMEM] + [VMEM] * (len(args) - 1),
-        out_specs=[VMEM] * len(outs),
+    rows, width = share * len(pieces), wide - 2 * HD
+    return pl.pallas_call(
+        attend_kernel,
+        out_shape=near((rows, width)),
+        in_specs=[SMEM] + [VMEM] * len(pieces),
+        out_specs=VMEM,
         scratch_shapes=[pltpu.VMEM((rows, wide), BF16)],
         compiler_params=params(8),
         name="attend",
-    )(*args)
-
-
-def project_kernel(order, at, ctx_ref, w_ref, *outs):
+    )(lengths, *arrived(pieces))
+
+
+def attend_first(lengths, pieces, block):
+    share, wide = pieces[0].shape
+    rows, width = share * len(pieces), wide - 2 * HD
+    return pl.pallas_call(
+        first_kernel,
+        out_shape=[near((rows, width)), near((rows, block.shape[1]))],
+        in_specs=[SMEM] + [VMEM] * (len(pieces) + 1),
+        out_specs=[VMEM] * 2,
+        scratch_shapes=[pltpu.VMEM((rows, wide), BF16)],
+        compiler_params=params(8),
+        name="attend_first",
+    )(lengths, *arrived(pieces), held(block))
+
+
+def project_kernel(n_dp, order, len_ref, ctx_ref, w_ref, *refs):
+    pieces, outs, (context, buf) = refs[:n_dp], refs[n_dp:-2], refs[-2:]
+    end = at_an_end()
+
+    @pl.when(end)
+    def _():
+        context[...] = ctx_ref[...]
+
+    @pl.when(jnp.logical_not(end))
+    def _():
+        context[...] = attention(len_ref, pieces, buf, context.shape[1])
+
     for k, out in enumerate(outs):
         width = out.shape[1]
-        start = pl.multiple_of(order(at + k) * width, width)
-        term = jnp.dot(ctx_ref[...], w_ref[:, pl.ds(start, width)], preferred_element_type=F32)
+        start = pl.multiple_of(order(k) * width, width)
+        term = jnp.dot(context[...], w_ref[:, pl.ds(start, width)], preferred_element_type=F32)
         out[...] = term.astype(out.dtype)
 
 
-def project(context, weight, order, at, cols, kept):
+def project(lengths, pieces, context, weight, order, cols, kept):
     rows, depth = context.shape
-    count = weight.shape[1] // cols - at
-    return pl.pallas_call(
-        functools.partial(project_kernel, order, at),
+    wide = pieces[0].shape[1]
+    count = weight.shape[1] // cols
+    return pl.pallas_call(
+        functools.partial(project_kernel, len(pieces), order),
         out_shape=[
             near((rows, cols), F32 if place >= count - kept else BF16) for place in range(count)
         ],
-        in_specs=[VMEM] * 2,
+        in_specs=[SMEM] + [VMEM] * (2 + len(pieces)),
         out_specs=[VMEM] * count,
+        scratch_shapes=[pltpu.VMEM((rows, depth), BF16), pltpu.VMEM((rows, wide), BF16)],
         compiler_params=params(8),
         cost_estimate=pl.CostEstimate(
             flops=2 * rows * depth * cols * count,
@@ -228,7 +269,7 @@
             transcendentals=0,
         ),
         name="project",
-    )(held(context), held(weight))
+    )(lengths, held(context), held(weight), *arrived(pieces))
 
 
 def add_kernel(count, *refs):
@@ -370,13 +411,13 @@
     return order if n == 4 else lambda place: jnp.int32(place)
 
 
-def chain_scatter(terms, beside):
+def chain_scatter(first, terms, beside):
     ends = [(0, 1), (3, 2)]
     pairs = [(0, 1), (1, 0), (2, 3), (3, 2)]
     middle = [(1, 2), (2, 1)]
     move = lambda value, perm: lax.ppermute(value, "tensor", perm)
     t = list(terms)
-    outer = [move(t[0], ends), move(t[1], ends)]
+    outer = [move(first, ends), move(t[1], ends)]
     t[2], t[3], sent = add((t[0], outer[0]), after=[t[2], t[3]])
     outer.append(move(t[2], ends))
     inner = [move(sent, middle)]
@@ -406,12 +447,12 @@
     )
     hidden = exchange(packed_hidden, "dp", n_dp)
     if n == 4:
-        context, first = attend(lengths, moved, w_early[0])
-        rest = project(context, out_weight, order, 1, cols, chunks)
-        terms, own = [first, *rest[:-chunks]], rest[-chunks:]
-        recv, hidden[1:] = chain_scatter(terms, hidden[1:])
+        context, first = attend_first(lengths, moved, w_early[0])
+        blocks = project(lengths, moved, context, out_weight, order, cols, chunks)
+        terms, own = blocks[:-chunks], blocks[-chunks:]
+        recv, hidden[1:] = chain_scatter(first, terms, hidden[1:])
     else:
-        context = attend(lengths, moved)[0]
+        context = attend(lengths, moved)
         partial_term = jnp.dot(context, out_weight, preferred_element_type=F32).astype(BF16)
         summed = lax.psum_scatter(partial_term, "tensor", scatter_dimension=1, tiled=True)
         zero = jnp.zeros((hidden_in.shape[0], cols), BF16)

time: 58.8 us -> 58.1 us (0.988)
  starting transfers between devices: 32.1 us -> 30.8 us
  Pallas kernels: 11.4 us -> 12.3 us
    ppermute x10, waiting for transfers between devices: 9.38 us -> 7.64 us  [chain_scatter(): move = lambda value, perm: lax.ppermute(value, 'tensor', perm)]
    ppermute x10, starting transfers between devices: 21.9 us -> 20.5 us  [chain_scatter(): move = lambda value, perm: lax.ppermute(value, 'tensor', perm)]
    ppermute x9, waiting for transfers between devices: 4.13 us -> 5.49 us  [swap(): return lax.ppermute(piece, axis, [(i, i ^ bits) for i in range(n)])]
    pallas_call x2, Pallas kernels: 3.57 us -> 4.46 us  [the longest x1 2.99 us: project(): pl.pallas_call(functools.partial(project_kernel, len(pieces), order), out...]
  transfers between devices with their start and end apart: 19 -> 19, of which waited for: 9 -> 8; matrix products, arithmetic and copies ran while one was open for 0% -> 0% of each run, Pallas kernels for 14% -> 15%
where the time goes in v5:
time: 58.1 us; the launch traced here: 57.8 us
  starting transfers between devices  30.8 us (53%)
  waiting for transfers between devices  13.1 us (23%)
  Pallas kernels  12.3 us (21%)
  between operations  0.87 us (1%)
    ppermute x10, starting transfers between devices, chain_scatter(): move = lambda value, perm: lax.ppermute(value, 'tensor', perm)  20.5 us
    ppermute x9, starting transfers between devices, swap(): return lax.ppermute(piece, axis, [(i, i ^ bits) for i in range(n)])  10.3 us
    ppermute x10, waiting for transfers between devices, chain_scatter(): move = lambda value, perm: lax.ppermute(value, 'tensor', perm)  7.64 us
    ppermute x9, waiting for transfers between devices, swap(): return lax.ppermute(piece, axis, [(i, i ^ bits) for i in range(n)])  5.49 us
    pallas_call x1, Pallas kernels, project(): pl.pallas_call(functools.partial(project_kernel, len(pieces), order), out...  2.99 us
    pallas_call x1, Pallas kernels, pack_hidden(): pl.pallas_call(functools.partial(pack_hidden_kernel, n_dp, order), out_sh...  2.79 us
    pallas_call x2, Pallas kernels, store(): pl.pallas_call(functools.partial(store_kernel, part), out_shape=jax.Shape...  1.61 us
    pallas_call x1, Pallas kernels, pack_qkv(): pl.pallas_call(functools.partial(pack_qkv_kernel, width // HD), out_shape...  1.56 us
  transfers between devices with their start and end apart: 19, of which 8 were waited for; matrix products, arithmetic and copies ran while one was open for 0% of the time, Pallas kernels for 15%

profile of v5, /device:TPU:0, one launch (start us, length us, event | category | flops | bytes accessed | tf_op | source)
XLA Modules:
  0.0 57.8 jit_solution(16508275548178403691)
XLA Ops:
  0.6 0.0 copy-start
  0.6 0.0 copy-start.1
  0.7 1.6 %pack_qkv.1 = (bf16[32,1280]{1,0:T(8,128)(2,1)S(1)}, bf16[32,1280]{1,0:T(8,128)(2,1)S(1)}, bf16[32,1280]{1,0:T(8,128)(2,1)S(1)}, bf16[32,1280]{1,0:T(8,128)(2,1)S(1)}) custom-call(s32[1,128]{1,0:T(1,128)} %send_ref.3, bf16[128,1024]{1,0:T(8,128)(2,1)} %q_ref.1, bf16[128,2,512]{2,1,0:T(2,128)(2,1)} %kv_ref.1), custom_call_target="tpu_custom_call" | custom-call | tf_op jit(solution)/shard_map/pack_qkv/pallas_call | solution.py:79
  2.2 0.0 copy-start.3
  2.2 0.0 copy-start.2
  2.2 3.0 %collective-permute-start = (bf16[32,1280]{1,0:T(8,128)(2,1)S(1)}, bf16[32,1280]{1,0:T(8,128)(2,1)S(1)}, u32[]{:S(2)}, u32[]{:S(2)}) collective-permute-start(bf16[32,1280]{1,0:T(8,128)(2,1)S(1)} %get-tuple-element.50), channel_id=1, source_target_pairs={{0,8},{4,12},{8,0},{12,4},{1,9},{5,13},{9,1},{13,5},{2,10},{6,14},... | collective-permute-start | bytes 245768 | tf_op jit(solution)/shard_map/ppermute | solution.py:380
  5.3 0.0 collective-permute-start.1
  5.3 0.2 collective-permute-start.2
  5.5 2.8 %pack_hidden.1 = (bf16[32,2048]{1,0:T(8,128)(2,1)S(1)}, bf16[32,2048]{1,0:T(8,128)(2,1)S(1)}, bf16[32,2048]{1,0:T(8,128)(2,1)S(1)}, bf16[32,2048]{1,0:T(8,128)(2,1)S(1)}, bf16[1024,1024]{1,0:T(8,128)(2,1)S(1)}) custom-call(s32[1,128]{1,0:T(1,128)} %send_ref.3, bf16[128,2048]{1,0:T(8,128)(2,1)} %h_ref, bf16[1024,8192]{1,0:T(8,128)(2,1)} %w_ref.3), custom_call_target="tpu_custom_call" | custom-call | tf_op jit(solution)/shard_map/pack_hidden/pallas_call | solution.py:131
  8.3 0.0 collective-permute-done.refs_1_
  8.3 0.0 collective-permute-done.1.refs_2_
  8.3 1.1 %collective-permute-done.2.refs_3_ = bf16[32,1280]{1,0:T(8,128)(2,1)S(1)} collective-permute-done((bf16[32,1280]{1,0:T(8,128)(2,1)S(1)}, bf16[32,1280]{1,0:T(8,128)(2,1)S(1)}, u32[]{:S(2)}, u32[]{:S(2)}) %collective-permute-start.2) | collective-permute-done | bytes 81952 | tf_op jit(solution)/shard_map/ppermute | solution.py:380
  9.4 0.0 copy-done.1
  9.4 1.5 %attend_first.1 = (bf16[128,1024]{1,0:T(8,128)(2,1)S(1)}, bf16[128,1024]{1,0:T(8,128)(2,1)S(1)}) custom-call(s32[1,8]{1,0:T(1,128)S(1)} %copy-done.1, bf16[32,1280]{1,0:T(8,128)(2,1)S(1)} %get-tuple-element.49.refs_0_, bf16[32,1280]{1,0:T(8,128)(2,1)S(1)} %collective-permute-done.refs_1_, bf16[32,1280]{1,0:T(8,128)(2,1)S(1)} %collective-permute-done.1.refs_2_, ...), custom_call_target="tpu_custom_call" | custom-call | tf_op jit(solution)/shard_map/attend_first/pallas_call | solution.py:223
  10.8 2.6 %collective-permute-start.4 = (bf16[128,1024]{1,0:T(8,128)(2,1)S(1)}, bf16[128,1024]{1,0:T(8,128)(2,1)S(1)}, u32[]{:S(2)}, u32[]{:S(2)}) collective-permute-start(bf16[128,1024]{1,0:T(8,128)(2,1)S(1)} %get-tuple-element.58), channel_id=1, source_target_pairs={{0,1},{3,2},{4,5},{7,6},{8,9},{11,10},{12,13},{15,14},{16,17},{19,... | collective-permute-start | bytes 786440 | tf_op jit(solution)/shard_map/ppermute | solution.py:418
  13.4 0.0 copy-done
  13.4 3.0 %project.1 = (bf16[128,1024]{1,0:T(8,128)(2,1)S(1)}, bf16[128,1024]{1,0:T(8,128)(2,1)S(1)}, bf16[128,1024]{1,0:T(8,128)(2,1)S(1)}, bf16[128,1024]{1,0:T(8,128)(2...) custom-call(s32[1,8]{1,0:T(1,128)S(1)} %copy-done.1, ...), custom_call_target="tpu_custom_call" | custom-call | flops 2147483648 | bytes 16777216 | tf_op jit(solution)/shard_map/project/pallas_call | solution.py:257
  16.4 1.9 %collective-permute-start.3 = (bf16[128,1024]{1,0:T(8,128)(2,1)S(1)}, bf16[128,1024]{1,0:T(8,128)(2,1)S(1)}, u32[]{:S(2)}, u32[]{:S(2)}) collective-permute-start(bf16[128,1024]{1,0:T(8,128)(2,1)S(1)} %get-tuple-element.56.refs_0_), channel_id=1, source_target_pairs={{0,1},{3,2},{4,5},{7,6},{8,9},{11,10},{12,13},{15,14},{16,17},{19,... | collective-permute-start | bytes 786440 | tf_op jit(solution)/shard_map/ppermute | solution.py:418
  18.4 0.2 collective-permute-start.5
  18.6 1.4 %collective-permute-start.6 = (bf16[32,2048]{1,0:T(8,128)(2,1)S(1)}, bf16[32,2048]{1,0:T(8,128)(2,1)S(1)}, u32[]{:S(2)}, u32[]{:S(2)}) collective-permute-start(bf16[32,2048]{1,0:T(8,128)(2,1)S(1)} %get-tuple-element.64), channel_id=1, source_target_pairs={{0,8},{4,12},{8,0},{12,4},{1,9},{5,13},{9,1},{13,5},{2,10},{6,14},... | collective-permute-start | bytes 393224 | tf_op jit(solution)/shard_map/ppermute | solution.py:380
  20.0 0.3 collective-permute-start.7
  20.3 0.0 collective-permute-done.4.refs_1_
  20.3 0.1 add.30
  20.4 4.1 %collective-permute-start.8 = (bf16[128,1024]{1,0:T(8,128)(2,1)S(1)}, bf16[128,1024]{1,0:T(8,128)(2,1)S(1)}, u32[]{:S(2)}, u32[]{:S(2)}) collective-permute-start(bf16[128,1024]{1,0:T(8,128)(2,1)S(1)} %get-tuple-element.67.refs_0_), channel_id=1, source_target_pairs={{0,1},{3,2},{4,5},{7,6},{8,9},{11,10},{12,13},{15,14},{16,17},{19,... | collective-permute-start | bytes 786440 | tf_op jit(solution)/shard_map/ppermute | solution.py:418
  24.5 0.0 collective-permute-done.5.refs_4_
  24.5 0.7 %collective-permute-start.9 = (bf16[128,1024]{1,0:T(8,128)(2,1)S(1)}, bf16[128,1024]{1,0:T(8,128)(2,1)S(1)}, u32[]{:S(2)}, u32[]{:S(2)}) collective-permute-start(bf16[128,1024]{1,0:T(8,128)(2,1)S(1)} %get-tuple-element.69), channel_id=1, source_target_pairs={{1,2},{2,1},{5,6},{6,5},{9,10},{10,9},{13,14},{14,13},{17,18},{18,... | collective-permute-start | bytes 786440 | tf_op jit(solution)/shard_map/ppermute | solution.py:418
  25.2 0.0 collective-permute-done.6.refs_5_
  25.2 1.4 %collective-permute-done.7.refs_6_ = bf16[32,2048]{1,0:T(8,128)(2,1)S(1)} collective-permute-done((bf16[32,2048]{1,0:T(8,128)(2,1)S(1)}, bf16[32,2048]{1,0:T(8,128)(2,1)S(1)}, u32[]{:S(2)}, u32[]{:S(2)}) %collective-permute-start.7) | collective-permute-done | bytes 131104 | tf_op jit(solution)/shard_map/ppermute | solution.py:380
  26.6 0.0 collective-permute-done.3.refs_1_
  26.6 0.1 add.31
  26.6 3.5 %collective-permute-start.10 = (bf16[128,1024]{1,0:T(8,128)(2,1)S(1)}, bf16[128,1024]{1,0:T(8,128)(2,1)S(1)}, u32[]{:S(2)}, u32[]{:S(2)}) collective-permute-start(bf16[128,1024]{1,0:T(8,128)(2,1)S(1)} %get-tuple-element.66.refs_0_), channel_id=1, source_target_pairs={{0,1},{3,2},{4,5},{7,6},{8,9},{11,10},{12,13},{15,14},{16,17},{19,... | collective-permute-start | bytes 786440 | tf_op jit(solution)/shard_map/ppermute | solution.py:418
  30.1 0.7 %collective-permute-start.11 = (bf16[128,1024]{1,0:T(8,128)(2,1)S(1)}, bf16[128,1024]{1,0:T(8,128)(2,1)S(1)}, u32[]{:S(2)}, u32[]{:S(2)}) collective-permute-start(bf16[128,1024]{1,0:T(8,128)(2,1)S(1)} %get-tuple-element.72), channel_id=1, source_target_pairs={{1,2},{2,1},{5,6},{6,5},{9,10},{10,9},{13,14},{14,13},{17,18},{18,... | collective-permute-start | bytes 786440 | tf_op jit(solution)/shard_map/ppermute | solution.py:418
  30.8 0.5 collective-permute-done.8.refs_2_
  31.3 0.0 collective-permute-done.9.refs_3_
  31.3 0.1 add.32
  31.4 2.5 %collective-permute-start.14 = (bf16[128,1024]{1,0:T(8,128)(2,1)S(1)}, bf16[128,1024]{1,0:T(8,128)(2,1)S(1)}, u32[]{:S(2)}, u32[]{:S(2)}) collective-permute-start(bf16[128,1024]{1,0:T(8,128)(2,1)S(1)} %get-tuple-element.80), channel_id=1, source_target_pairs={{0,1},{1,0},{2,3},{3,2},{4,5},{5,4},{6,7},{7,6},{8,9},{9,8},{10,11... | collective-permute-start | bytes 786440 | tf_op jit(solution)/shard_map/ppermute | solution.py:418
  33.9 0.7 %collective-permute-start.15 = (bf16[128,1024]{1,0:T(8,128)(2,1)S(1)}, bf16[128,1024]{1,0:T(8,128)(2,1)S(1)}, u32[]{:S(2)}, u32[]{:S(2)}) collective-permute-start(bf16[128,1024]{1,0:T(8,128)(2,1)S(1)} %get-tuple-element.81), channel_id=1, source_target_pairs={{1,2},{2,1},{5,6},{6,5},{9,10},{10,9},{13,14},{14,13},{17,18},{18,... | collective-permute-start | bytes 786440 | tf_op jit(solution)/shard_map/ppermute | solution.py:418
  34.6 2.3 %collective-permute-done.10.refs_2_ = bf16[128,1024]{1,0:T(8,128)(2,1)S(1)} collective-permute-done((bf16[128,1024]{1,0:T(8,128)(2,1)S(1)}, bf16[128,1024]{1,0:T(8,128)(2,1)S(1)}, u32[]{:S(2)}, u32[]{:S(2)}) %collective-permute-start.10) | collective-permute-done | bytes 262176 | tf_op jit(solution)/shard_map/ppermute | solution.py:418
  36.9 0.0 collective-permute-done.11.refs_3_
  36.9 0.8 %add.33 = (bf16[128,1024]{1,0:T(8,128)(2,1)S(1)}, bf16[128,1024]{1,0:T(8,128)(2,1)}) custom-call(bf16[128,1024]{1,0:T(8,128)(2,1)S(1)} %get-tuple-element.66.refs_0_, bf16[128,1024]{1,0:T(8,128)(2,1)S(1)} %get-tuple-element.71.refs_1_, bf16[128,1024]{1,0:T(8,128)(2,1)S(1)} %collective-permute-done.10.refs_2_, ...), custom_call_target="tpu_custom_call" | custom-call | tf_op jit(solution)/shard_map/add/pallas_call | solution.py:283
  37.6 3.2 %collective-permute-start.12 = (bf16[128,1024]{1,0:T(8,128)(2,1)}, bf16[128,1024]{1,0:T(8,128)(2,1)S(1)}, u32[]{:S(2)}, u32[]{:S(2)}) collective-permute-start(bf16[128,1024]{1,0:T(8,128)(2,1)} %get-tuple-element.73), channel_id=1, source_target_pairs={{0,1},{1,0},{2,3},{3,2},{4,5},{5,4},{6,7},{7,6},{8,9},{9,8},{10,11... | collective-permute-start | bytes 786440 | tf_op jit(solution)/shard_map/ppermute | solution.py:418
  40.8 0.7 %collective-permute-start.13 = (bf16[128,1024]{1,0:T(8,128)(2,1)S(1)}, bf16[128,1024]{1,0:T(8,128)(2,1)S(1)}, u32[]{:S(2)}, u32[]{:S(2)}) collective-permute-start(bf16[128,1024]{1,0:T(8,128)(2,1)S(1)} %get-tuple-element.74), channel_id=1, source_target_pairs={{1,2},{2,1},{5,6},{6,5},{9,10},{10,9},{13,14},{14,13},{17,18},{18,... | collective-permute-start | bytes 786440 | tf_op jit(solution)/shard_map/ppermute | solution.py:418
  41.5 0.0 copy-done.3
  41.5 0.1 copy.21.scale_ref
  41.6 0.0 copy-done.2
  41.6 0.9 %collective-permute-done.14.recv_r = bf16[128,1024]{1,0:T(8,128)(2,1)S(1)} collective-permute-done((bf16[128,1024]{1,0:T(8,128)(2,1)S(1)}, bf16[128,1024]{1,0:T(8,128)(2,1)S(1)}, u32[]{:S(2)}, u32[]{:S(2)}) %collective-permute-start.14) | collective-permute-done | bytes 262176 | tf_op jit(solution)/shard_map/ppermute | solution.py:418
  42.5 0.0 collective-permute-done.15.recv_l
  42.5 0.4 finish.2
  42.9 0.8 %store.2.refs_5_ = f32[128,2048]{1,0:T(8,128)} custom-call(f32[128,1024]{1,0:T(8,128)S(1)} %get-tuple-element.84.value_ref), custom_call_target="tpu_custom_call" | custom-call | bytes 524288 | tf_op jit(solution)/shard_map/store/pallas_call | solution.py:364
  43.7 4.0 %collective-permute-done.12.recv_r = bf16[128,1024]{1,0:T(8,128)(2,1)S(1)} collective-permute-done((bf16[128,1024]{1,0:T(8,128)(2,1)}, bf16[128,1024]{1,0:T(8,128)(2,1)S(1)}, u32[]{:S(2)}, u32[]{:S(2)}) %collective-permute-start.12) | collective-permute-done | bytes 262176 | tf_op jit(solution)/shard_map/ppermute | solution.py:418
  47.8 0.0 collective-permute-done.13.recv_l
  47.8 0.4 finish.3
  48.2 3.6 %collective-permute-start.16 = (f32[8,128]{1,0:T(8,128)S(1)}, f32[8,128]{1,0:T(8,128)S(1)}, u32[]{:S(2)}, u32[]{:S(2)}) collective-permute-start(f32[8,128]{1,0:T(8,128)S(1)} %get-tuple-element.87), channel_id=1, source_target_pairs={{0,2},{1,3},{2,0},{3,1},{4,6},{5,7},{6,4},{7,5},{8,10},{9,11},{10,... | collective-permute-start | bytes 12296 | tf_op jit(solution)/shard_map/ppermute | solution.py:380
  51.9 0.0 collective-permute-start.17
  51.9 1.5 %collective-permute-start.18 = (f32[8,128]{1,0:T(8,128)S(1)}, f32[8,128]{1,0:T(8,128)S(1)}, u32[]{:S(2)}, u32[]{:S(2)}) collective-permute-start(f32[8,128]{1,0:T(8,128)S(1)} %get-tuple-element.87), channel_id=1, source_target_pairs={{0,3},{1,2},{2,1},{3,0},{4,7},{5,6},{6,5},{7,4},{8,11},{9,10},{10,... | collective-permute-start | bytes 12296 | tf_op jit(solution)/shard_map/ppermute | solution.py:380
  53.4 0.8 %store.3 = f32[128,2048]{1,0:T(8,128)} custom-call(f32[128,1024]{1,0:T(8,128)S(1)} %get-tuple-element.85.value_ref, f32[128,2048]{1,0:T(8,128)} %get-tuple-element.86.refs_0_), custom_call_target="tpu_custom_call", output_to_operand_aliasing={{}: (1, {})} | custom-call | bytes 524288 | tf_op jit(solution)/shard_map/store/pallas_call | solution.py:364
  54.2 0.0 collective-permute-done.16
  54.2 1.2 %collective-permute-done.17 = f32[8,128]{1,0:T(8,128)S(1)} collective-permute-done((f32[8,128]{1,0:T(8,128)S(1)}, f32[8,128]{1,0:T(8,128)S(1)}, u32[]{:S(2)}, u32[]{:S(2)}) %collective-permute-start.17) | collective-permute-done | bytes 4128 | tf_op jit(solution)/shard_map/ppermute | solution.py:380
  55.5 1.8 %collective-permute-done.18 = f32[8,128]{1,0:T(8,128)S(1)} collective-permute-done((f32[8,128]{1,0:T(8,128)S(1)}, f32[8,128]{1,0:T(8,128)S(1)}, u32[]{:S(2)}, u32[]{:S(2)}) %collective-permute-start.18) | collective-permute-done | bytes 4128 | tf_op jit(solution)/shard_map/ppermute | solution.py:380
  57.3 0.5 multiply_bitcast_fusion
  (2 shorter events, 0.0 us)
Async XLA Ops:
  0.6 12.8 %copy-start = (bf16[1024,8192]{1,0:T(8,128)(2,1)S(1)}, bf16[1024,8192]{1,0:T(8,128)(2,1)}, u32[]{:S(2)}) copy-start(bf16[1024,8192]{1,0:T(8,128)(2,1)} %w_ref.3) | copy-start | bytes 50331652
  0.6 8.7 %copy-start.1 = (s32[1,8]{1,0:T(1,128)S(1)}, s32[1,8]{1,0:T(1,128)}, u32[]{:S(2)}) copy-start(s32[1,8]{1,0:T(1,128)} %len_ref.3) | copy-start | bytes 100
  2.2 39.3 %copy-start.3 = (bf16[128,16]{0,1:T(8,128)(2,1)S(1)}, bf16[128,16]{0,1:T(8,128)(2,1)}, u32[]{:S(2)}) copy-start(bf16[128,16]{0,1:T(8,128)(2,1)} %param.14) | copy-start | bytes 12292
  2.2 39.4 %copy-start.2 = (bf16[8192]{0:T(1024)(128)(2,1)S(1)}, bf16[8192]{0:T(1024)(128)(2,1)}, u32[]{:S(2)}) copy-start(bf16[8192]{0:T(1024)(128)(2,1)} %param.15) | copy-start | bytes 49156
  2.2 6.0 %collective-permute-start = (bf16[32,1280]{1,0:T(8,128)(2,1)S(1)}, bf16[32,1280]{1,0:T(8,128)(2,1)S(1)}, u32[]{:S(2)}, u32[]{:S(2)}) collective-permute-start(bf16[32,1280]{1,0:T(8,128)(2,1)S(1)} %get-tuple-element.50), channel_id=1, source_target_pairs={{0,8},{4,12},{8,0},{12,4},{1,9},{5,13},{9,1},{13,5},{2,10},{6,14},... | collective-permute-start | bytes 245768 | tf_op jit(solution)/shard_map/ppermute | solution.py:380
  5.3 3.0 %collective-permute-start.1 = (bf16[32,1280]{1,0:T(8,128)(2,1)S(1)}, bf16[32,1280]{1,0:T(8,128)(2,1)S(1)}, u32[]{:S(2)}, u32[]{:S(2)}) collective-permute-start(bf16[32,1280]{1,0:T(8,128)(2,1)S(1)} %get-tuple-element.51), channel_id=1, source_target_pairs={{0,4},{4,0},{8,12},{12,8},{1,5},{5,1},{9,13},{13,9},{2,6},{6,2},{1... | collective-permute-start | bytes 245768 | tf_op jit(solution)/shard_map/ppermute | solution.py:380
  5.3 4.1 %collective-permute-start.2 = (bf16[32,1280]{1,0:T(8,128)(2,1)S(1)}, bf16[32,1280]{1,0:T(8,128)(2,1)S(1)}, u32[]{:S(2)}, u32[]{:S(2)}) collective-permute-start(bf16[32,1280]{1,0:T(8,128)(2,1)S(1)} %get-tuple-element.52), channel_id=1, source_target_pairs={{0,12},{4,8},{8,4},{12,0},{1,13},{5,9},{9,5},{13,1},{2,14},{6,10},... | collective-permute-start | bytes 245768 | tf_op jit(solution)/shard_map/ppermute | solution.py:380
  10.8 9.5 %collective-permute-start.4 = (bf16[128,1024]{1,0:T(8,128)(2,1)S(1)}, bf16[128,1024]{1,0:T(8,128)(2,1)S(1)}, u32[]{:S(2)}, u32[]{:S(2)}) collective-permute-start(bf16[128,1024]{1,0:T(8,128)(2,1)S(1)} %get-tuple-element.58), channel_id=1, source_target_pairs={{0,1},{3,2},{4,5},{7,6},{8,9},{11,10},{12,13},{15,14},{16,17},{19,... | collective-permute-start | bytes 786440 | tf_op jit(solution)/shard_map/ppermute | solution.py:418
  16.4 10.1 %collective-permute-start.3 = (bf16[128,1024]{1,0:T(8,128)(2,1)S(1)}, bf16[128,1024]{1,0:T(8,128)(2,1)S(1)}, u32[]{:S(2)}, u32[]{:S(2)}) collective-permute-start(bf16[128,1024]{1,0:T(8,128)(2,1)S(1)} %get-tuple-element.56.refs_0_), channel_id=1, source_target_pairs={{0,1},{3,2},{4,5},{7,6},{8,9},{11,10},{12,13},{15,14},{16,17},{19,... | collective-permute-start | bytes 786440 | tf_op jit(solution)/shard_map/ppermute | solution.py:418
  18.4 6.1 %collective-permute-start.5 = (bf16[32,2048]{1,0:T(8,128)(2,1)S(1)}, bf16[32,2048]{1,0:T(8,128)(2,1)S(1)}, u32[]{:S(2)}, u32[]{:S(2)}) collective-permute-start(bf16[32,2048]{1,0:T(8,128)(2,1)S(1)} %get-tuple-element.63), channel_id=1, source_target_pairs={{0,4},{4,0},{8,12},{12,8},{1,5},{5,1},{9,13},{13,9},{2,6},{6,2},{1... | collective-permute-start | bytes 393224 | tf_op jit(solution)/shard_map/ppermute | solution.py:380
  18.6 6.6 %collective-permute-start.6 = (bf16[32,2048]{1,0:T(8,128)(2,1)S(1)}, bf16[32,2048]{1,0:T(8,128)(2,1)S(1)}, u32[]{:S(2)}, u32[]{:S(2)}) collective-permute-start(bf16[32,2048]{1,0:T(8,128)(2,1)S(1)} %get-tuple-element.64), channel_id=1, source_target_pairs={{0,8},{4,12},{8,0},{12,4},{1,9},{5,13},{9,1},{13,5},{2,10},{6,14},... | collective-permute-start | bytes 393224 | tf_op jit(solution)/shard_map/ppermute | solution.py:380
  20.0 6.5 %collective-permute-start.7 = (bf16[32,2048]{1,0:T(8,128)(2,1)S(1)}, bf16[32,2048]{1,0:T(8,128)(2,1)S(1)}, u32[]{:S(2)}, u32[]{:S(2)}) collective-permute-start(bf16[32,2048]{1,0:T(8,128)(2,1)S(1)} %get-tuple-element.65), channel_id=1, source_target_pairs={{0,12},{4,8},{8,4},{12,0},{1,13},{5,9},{9,5},{13,1},{2,14},{6,10},... | collective-permute-start | bytes 393224 | tf_op jit(solution)/shard_map/ppermute | solution.py:380
  20.4 10.9 %collective-permute-start.8 = (bf16[128,1024]{1,0:T(8,128)(2,1)S(1)}, bf16[128,1024]{1,0:T(8,128)(2,1)S(1)}, u32[]{:S(2)}, u32[]{:S(2)}) collective-permute-start(bf16[128,1024]{1,0:T(8,128)(2,1)S(1)} %get-tuple-element.67.refs_0_), channel_id=1, source_target_pairs={{0,1},{3,2},{4,5},{7,6},{8,9},{11,10},{12,13},{15,14},{16,17},{19,... | collective-permute-start | bytes 786440 | tf_op jit(solution)/shard_map/ppermute | solution.py:418
  24.5 6.8 %collective-permute-start.9 = (bf16[128,1024]{1,0:T(8,128)(2,1)S(1)}, bf16[128,1024]{1,0:T(8,128)(2,1)S(1)}, u32[]{:S(2)}, u32[]{:S(2)}) collective-permute-start(bf16[128,1024]{1,0:T(8,128)(2,1)S(1)} %get-tuple-element.69), channel_id=1, source_target_pairs={{1,2},{2,1},{5,6},{6,5},{9,10},{10,9},{13,14},{14,13},{17,18},{18,... | collective-permute-start | bytes 786440 | tf_op jit(solution)/shard_map/ppermute | solution.py:418
  26.6 10.2 %collective-permute-start.10 = (bf16[128,1024]{1,0:T(8,128)(2,1)S(1)}, bf16[128,1024]{1,0:T(8,128)(2,1)S(1)}, u32[]{:S(2)}, u32[]{:S(2)}) collective-permute-start(bf16[128,1024]{1,0:T(8,128)(2,1)S(1)} %get-tuple-element.66.refs_0_), channel_id=1, source_target_pairs={{0,1},{3,2},{4,5},{7,6},{8,9},{11,10},{12,13},{15,14},{16,17},{19,... | collective-permute-start | bytes 786440 | tf_op jit(solution)/shard_map/ppermute | solution.py:418
  30.1 6.8 %collective-permute-start.11 = (bf16[128,1024]{1,0:T(8,128)(2,1)S(1)}, bf16[128,1024]{1,0:T(8,128)(2,1)S(1)}, u32[]{:S(2)}, u32[]{:S(2)}) collective-permute-start(bf16[128,1024]{1,0:T(8,128)(2,1)S(1)} %get-tuple-element.72), channel_id=1, source_target_pairs={{1,2},{2,1},{5,6},{6,5},{9,10},{10,9},{13,14},{14,13},{17,18},{18,... | collective-permute-start | bytes 786440 | tf_op jit(solution)/shard_map/ppermute | solution.py:418
  31.4 11.1 %collective-permute-start.14 = (bf16[128,1024]{1,0:T(8,128)(2,1)S(1)}, bf16[128,1024]{1,0:T(8,128)(2,1)S(1)}, u32[]{:S(2)}, u32[]{:S(2)}) collective-permute-start(bf16[128,1024]{1,0:T(8,128)(2,1)S(1)} %get-tuple-element.80), channel_id=1, source_target_pairs={{0,1},{1,0},{2,3},{3,2},{4,5},{5,4},{6,7},{7,6},{8,9},{9,8},{10,11... | collective-permute-start | bytes 786440 | tf_op jit(solution)/shard_map/ppermute | solution.py:418
  33.9 8.6 %collective-permute-start.15 = (bf16[128,1024]{1,0:T(8,128)(2,1)S(1)}, bf16[128,1024]{1,0:T(8,128)(2,1)S(1)}, u32[]{:S(2)}, u32[]{:S(2)}) collective-permute-start(bf16[128,1024]{1,0:T(8,128)(2,1)S(1)} %get-tuple-element.81), channel_id=1, source_target_pairs={{1,2},{2,1},{5,6},{6,5},{9,10},{10,9},{13,14},{14,13},{17,18},{18,... | collective-permute-start | bytes 786440 | tf_op jit(solution)/shard_map/ppermute | solution.py:418
  37.6 10.1 %collective-permute-start.12 = (bf16[128,1024]{1,0:T(8,128)(2,1)}, bf16[128,1024]{1,0:T(8,128)(2,1)S(1)}, u32[]{:S(2)}, u32[]{:S(2)}) collective-permute-start(bf16[128,1024]{1,0:T(8,128)(2,1)} %get-tuple-element.73), channel_id=1, source_target_pairs={{0,1},{1,0},{2,3},{3,2},{4,5},{5,4},{6,7},{7,6},{8,9},{9,8},{10,11... | collective-permute-start | bytes 786440 | tf_op jit(solution)/shard_map/ppermute | solution.py:418
  40.8 7.0 %collective-permute-start.13 = (bf16[128,1024]{1,0:T(8,128)(2,1)S(1)}, bf16[128,1024]{1,0:T(8,128)(2,1)S(1)}, u32[]{:S(2)}, u32[]{:S(2)}) collective-permute-start(bf16[128,1024]{1,0:T(8,128)(2,1)S(1)} %get-tuple-element.74), channel_id=1, source_target_pairs={{1,2},{2,1},{5,6},{6,5},{9,10},{10,9},{13,14},{14,13},{17,18},{18,... | collective-permute-start | bytes 786440 | tf_op jit(solution)/shard_map/ppermute | solution.py:418
  48.2 6.0 %collective-permute-start.16 = (f32[8,128]{1,0:T(8,128)S(1)}, f32[8,128]{1,0:T(8,128)S(1)}, u32[]{:S(2)}, u32[]{:S(2)}) collective-permute-start(f32[8,128]{1,0:T(8,128)S(1)} %get-tuple-element.87), channel_id=1, source_target_pairs={{0,2},{1,3},{2,0},{3,1},{4,6},{5,7},{6,4},{7,5},{8,10},{9,11},{10,... | collective-permute-start | bytes 12296 | tf_op jit(solution)/shard_map/ppermute | solution.py:380
  51.9 3.6 %collective-permute-start.17 = (f32[8,128]{1,0:T(8,128)S(1)}, f32[8,128]{1,0:T(8,128)S(1)}, u32[]{:S(2)}, u32[]{:S(2)}) collective-permute-start(f32[8,128]{1,0:T(8,128)S(1)} %get-tuple-element.87), channel_id=1, source_target_pairs={{0,1},{1,0},{2,3},{3,2},{4,5},{5,4},{6,7},{7,6},{8,9},{9,8},{10,11... | collective-permute-start | bytes 12296 | tf_op jit(solution)/shard_map/ppermute | solution.py:380
  51.9 5.4 %collective-permute-start.18 = (f32[8,128]{1,0:T(8,128)S(1)}, f32[8,128]{1,0:T(8,128)S(1)}, u32[]{:S(2)}, u32[]{:S(2)}) collective-permute-start(f32[8,128]{1,0:T(8,128)S(1)} %get-tuple-element.87), channel_id=1, source_target_pairs={{0,3},{1,2},{2,1},{3,0},{4,7},{5,6},{6,5},{7,4},{8,11},{9,10},{10,... | collective-permute-start | bytes 12296 | tf_op jit(solution)/shard_map/ppermute | solution.py:380

commit v6 on v5

--- a/solution.py
+++ b/solution.py
@@ -101,53 +101,17 @@
             self.copies.append(
                 pltpu.make_async_copy(w_ref.at[rows, pl.ds(start, width)], out.at[rows, :], sems.at[k])
             )
-            self.copies[-1].start()
+
+    def start(self):
+        for copy in self.copies:
+            copy.start()
 
     def wait(self):
         for copy in self.copies:
             copy.wait()
 
 
-def fetch_sems(blocks):
-    return pltpu.SemaphoreType.DMA((max(blocks, 1), FETCHES))
-
-
-def pack_hidden_kernel(n_dp, order, send_ref, h_ref, w_ref, *refs):
-    outs, blocks, (buf, sems) = refs[:n_dp], refs[n_dp:-2], refs[-2:]
-    copies = [Fetch(order, k, w_ref, block, sems.at[k]) for k, block in enumerate(blocks)]
-    me = lax.axis_index("dp")
-    buf[...] = reorder(one_hot_columns(send_ref), h_ref[...])
-    share = outs[0].shape[0]
-    for k, out in enumerate(outs):
-        start = pl.multiple_of((me ^ k) * share, share)
-        out[...] = buf[pl.ds(start, share), :]
-    for copy in copies:
-        copy.wait()
-
-
-def pack_hidden(send_rows, hidden, weight, n_dp, order, cols, blocks):
-    rows, width = hidden.shape
-    depth = weight.shape[0]
-    got = pl.pallas_call(
-        functools.partial(pack_hidden_kernel, n_dp, order),
-        out_shape=[near((rows // n_dp, width))] * n_dp + [near((depth, cols))] * blocks,
-        in_specs=[VMEM] * 2 + [HBM],
-        out_specs=[VMEM] * (n_dp + blocks),
-        scratch_shapes=[pltpu.VMEM((rows, width), BF16), fetch_sems(blocks)],
-        compiler_params=params(4 + 2 * blocks),
-        name="pack_hidden",
-    )(far(send_rows), far(hidden), far(weight))
-    return got[:n_dp], got[n_dp:]
-
-
-def attention(len_ref, pieces, buf, width):
-    n_dp = len(pieces)
-    rows = buf.shape[0]
-    me = lax.axis_index("dp")
-    share = pieces[0].shape[0]
-    for k, piece in zip(arrivals(n_dp), pieces):
-        start = pl.multiple_of((me ^ k) * share, share)
-        buf[pl.ds(start, share), :] = piece[...]
+def allowed_pairs(len_ref, rows):
     row_id = lax.broadcasted_iota(jnp.int32, (rows, rows), 0)
     col_id = lax.broadcasted_iota(jnp.int32, (rows, rows), 1)
     row_seg = jnp.zeros((rows, rows), jnp.int32)
@@ -157,7 +121,57 @@
         end = end + len_ref[0, r]
         row_seg += (row_id >= end).astype(jnp.int32)
         col_seg += (col_id >= end).astype(jnp.int32)
-    allowed = (row_seg == col_seg) & (row_id >= col_id)
+    return (row_seg == col_seg) & (row_id >= col_id)
+
+
+def pack_hidden_kernel(n_dp, order, len_ref, send_ref, h_ref, w_ref, *refs):
+    outs, mask_out, (buf, sems) = refs[:n_dp], refs[n_dp], refs[-2:]
+    block = refs[n_dp + 1] if len(refs) > n_dp + 3 else None
+    if block is not None:
+
+        @pl.when(at_an_end())
+        def _():
+            Fetch(order, 0, w_ref, block, sems).start()
+
+    mask_out[...] = allowed_pairs(len_ref, mask_out.shape[0]).astype(F32)
+    me = lax.axis_index("dp")
+    buf[...] = reorder(one_hot_columns(send_ref), h_ref[...])
+    share = outs[0].shape[0]
+    for k, out in enumerate(outs):
+        start = pl.multiple_of((me ^ k) * share, share)
+        out[...] = buf[pl.ds(start, share), :]
+    if block is not None:
+
+        @pl.when(at_an_end())
+        def _():
+            Fetch(order, 0, w_ref, block, sems).wait()
+
+
+def pack_hidden(lengths, send_rows, hidden, weight, n_dp, order, cols, blocks):
+    rows, width = hidden.shape
+    depth = weight.shape[0]
+    got = pl.pallas_call(
+        functools.partial(pack_hidden_kernel, n_dp, order),
+        out_shape=[near((rows // n_dp, width))] * n_dp
+        + [near((rows, rows), F32)]
+        + [near((depth, cols))] * blocks,
+        in_specs=[SMEM] + [VMEM] * 2 + [HBM],
+        out_specs=[VMEM] * (n_dp + 1 + blocks),
+        scratch_shapes=[pltpu.VMEM((rows, width), BF16), pltpu.SemaphoreType.DMA((FETCHES,))],
+        compiler_params=params(4 + 2 * blocks),
+        name="pack_hidden",
+    )(far(lengths), far(send_rows), far(hidden), far(weight))
+    return got[:n_dp], got[n_dp], got[n_dp + 1 :]
+
+
+def attention(mask_ref, pieces, buf, width):
+    n_dp = len(pieces)
+    rows = buf.shape[0]
+    me = lax.axis_index("dp")
+    share = pieces[0].shape[0]
+    for k, piece in zip(arrivals(n_dp), pieces):
+        start = pl.multiple_of((me ^ k) * share, share)
+        buf[pl.ds(start, share), :] = piece[...]
     heads = width // HD
     keys = buf[:, width : width + HD]
     values = jnp.concatenate(
@@ -167,7 +181,7 @@
     scores = lax.dot_general(
         query, keys, (((1,), (1,)), ((), ())), preferred_element_type=F32
     ) * HD ** (-0.5)
-    scores = jnp.where(allowed[None], scores.reshape(heads, rows, rows), -jnp.inf)
+    scores = jnp.where(mask_ref[...][None] > 0, scores.reshape(heads, rows, rows), -jnp.inf)
     weights = jnp.exp(scores - jnp.max(scores, axis=2, keepdims=True))
     weights = weights.reshape(heads * rows, rows).astype(BF16)
     mixed = jnp.dot(weights, values, preferred_element_type=F32)
@@ -175,9 +189,9 @@
     return jnp.concatenate([context[h * rows : (h + 1) * rows] for h in range(heads)], axis=1)
 
 
-def attend_kernel(len_ref, *refs):
+def attend_kernel(mask_ref, *refs):
     pieces, out, buf = refs[:-2], refs[-2], refs[-1]
-    out[...] = attention(len_ref, pieces, buf, out.shape[1])
+    out[...] = attention(mask_ref, pieces, buf, out.shape[1])
 
 
 def at_an_end():
@@ -185,12 +199,12 @@
     return (i == 0) | (i == 3)
 
 
-def first_kernel(len_ref, *refs):
+def first_kernel(mask_ref, *refs):
     pieces, (w_ref, out, first, buf) = refs[:-4], refs[-4:]
 
     @pl.when(at_an_end())
     def _():
-        context = attention(len_ref, pieces, buf, out.shape[1])
+        context = attention(mask_ref, pieces, buf, out.shape[1])
         out[...] = context
         first[...] = jnp.dot(context, w_ref[...], preferred_element_type=F32).astype(BF16)
 
@@ -203,35 +217,35 @@
     return [held(pieces[k]) for k in arrivals(len(pieces))]
 
 
-def attend(lengths, pieces):
+def attend(mask, pieces):
     share, wide = pieces[0].shape
     rows, width = share * len(pieces), wide - 2 * HD
     return pl.pallas_call(
         attend_kernel,
         out_shape=near((rows, width)),
-        in_specs=[SMEM] + [VMEM] * len(pieces),
+        in_specs=[VMEM] * (1 + len(pieces)),
         out_specs=VMEM,
         scratch_shapes=[pltpu.VMEM((rows, wide), BF16)],
         compiler_params=params(8),
         name="attend",
-    )(lengths, *arrived(pieces))
-
-
-def attend_first(lengths, pieces, block):
+    )(held(mask), *arrived(pieces))
+
+
+def attend_first(mask, pieces, block):
     share, wide = pieces[0].shape
     rows, width = share * len(pieces), wide - 2 * HD
     return pl.pallas_call(
         first_kernel,
         out_shape=[near((rows, width)), near((rows, block.shape[1]))],
-        in_specs=[SMEM] + [VMEM] * (len(pieces) + 1),
+        in_specs=[VMEM] * (len(pieces) + 2),
         out_specs=[VMEM] * 2,
         scratch_shapes=[pltpu.VMEM((rows, wide), BF16)],
         compiler_params=params(8),
         name="attend_first",
-    )(lengths, *arrived(pieces), held(block))
-
-
-def project_kernel(n_dp, order, len_ref, ctx_ref, w_ref, *refs):
+    )(held(mask), *arrived(pieces), held(block))
+
+
+def project_kernel(n_dp, order, mask_ref, ctx_ref, w_ref, *refs):
     pieces, outs, (context, buf) = refs[:n_dp], refs[n_dp:-2], refs[-2:]
     end = at_an_end()
 
@@ -241,7 +255,7 @@
 
     @pl.when(jnp.logical_not(end))
     def _():
-        context[...] = attention(len_ref, pieces, buf, context.shape[1])
+        context[...] = attention(mask_ref, pieces, buf, context.shape[1])
 
     for k, out in enumerate(outs):
         width = out.shape[1]
@@ -250,7 +264,7 @@
         out[...] = term.astype(out.dtype)
 
 
-def project(lengths, pieces, context, weight, order, cols, kept):
+def project(mask, pieces, context, weight, order, cols, kept):
     rows, depth = context.shape
     wide = pieces[0].shape[1]
     count = weight.shape[1] // cols
@@ -259,7 +273,7 @@
         out_shape=[
             near((rows, cols), F32 if place >= count - kept else BF16) for place in range(count)
         ],
-        in_specs=[SMEM] + [VMEM] * (2 + len(pieces)),
+        in_specs=[VMEM] * (3 + len(pieces)),
         out_specs=[VMEM] * count,
         scratch_shapes=[pltpu.VMEM((rows, depth), BF16), pltpu.VMEM((rows, wide), BF16)],
         compiler_params=params(8),
@@ -269,7 +283,7 @@
             transcendentals=0,
         ),
         name="project",
-    )(lengths, held(context), held(weight), *arrived(pieces))
+    )(held(mask), held(context), held(weight), *arrived(pieces))
 
 
 def add_kernel(count, *refs):
@@ -389,7 +403,7 @@
     while done < n:
         radix = min(4, n // done)
         got = [values] + [swap(values, axis, n, k * done) for k in range(1, radix)]
-        values = got[0] + got[1] if radix == 2 else (got[2] + got[0]) + (got[1] + got[3])
+        values = got[0] + got[1] if radix == 2 else (got[3] + got[0]) + (got[2] + got[1])
         done *= radix
     return values
 
@@ -442,17 +456,17 @@
     packed = pack_qkv(send_rows, queries, keys_values, n_dp)
     *packed, hidden_in = together(*packed, hidden_in)
     moved = exchange(packed, "dp", n_dp)
-    packed_hidden, w_early = pack_hidden(
-        send_rows, hidden_in, out_weight, n_dp, order, cols, 1 if n == 4 else 0
+    packed_hidden, mask, w_early = pack_hidden(
+        lengths, send_rows, hidden_in, out_weight, n_dp, order, cols, 1 if n == 4 else 0
     )
     hidden = exchange(packed_hidden, "dp", n_dp)
     if n == 4:
-        context, first = attend_first(lengths, moved, w_early[0])
-        blocks = project(lengths, moved, context, out_weight, order, cols, chunks)
+        context, first = attend_first(mask, moved, w_early[0])
+        blocks = project(mask, moved, context, out_weight, order, cols, chunks)
         terms, own = blocks[:-chunks], blocks[-chunks:]
         recv, hidden[1:] = chain_scatter(first, terms, hidden[1:])
     else:
-        context = attend(lengths, moved)
+        context = attend(mask, moved)
         partial_term = jnp.dot(context, out_weight, preferred_element_type=F32).astype(BF16)
         summed = lax.psum_scatter(partial_term, "tensor", scatter_dimension=1, tiled=True)
         zero = jnp.zeros((hidden_in.shape[0], cols), BF16)

time: 58.1 us -> 56 us (0.964)
  Pallas kernels: 12.3 us -> 11.2 us
  waiting for transfers between devices: 13.1 us -> 12 us
    ppermute x9, waiting for transfers between devices: 5.49 us -> 4.08 us  [swap(): return lax.ppermute(piece, axis, [(i, i ^ bits) for i in range(n)])]
    ppermute x10, starting transfers between devices: 20.5 us -> 21.5 us  [chain_scatter(): move = lambda value, perm: lax.ppermute(value, 'tensor', perm)]
    ppermute x9, starting transfers between devices: 10.3 us -> 9.59 us  [swap(): return lax.ppermute(piece, axis, [(i, i ^ bits) for i in range(n)])]
    pallas_call x1, Pallas kernels: 2.99 us -> 2.39 us  [project(): pl.pallas_call(functools.partial(project_kernel, len(pieces), order), out...]
  transfers between devices with their start and end apart: 19 -> 19, of which waited for: 8 -> 10; matrix products, arithmetic and copies ran while one was open for 0% -> 0% of each run, Pallas kernels for 15% -> 15%
where the time goes in v6:
time: 56 us; the launch traced here: 55.8 us
  starting transfers between devices  31 us (55%)
  waiting for transfers between devices  12 us (21%)
  Pallas kernels  11.2 us (20%)
  between operations  0.86 us (2%)
    ppermute x10, starting transfers between devices, chain_scatter(): move = lambda value, perm: lax.ppermute(value, 'tensor', perm)  21.5 us
    ppermute x9, starting transfers between devices, swap(): return lax.ppermute(piece, axis, [(i, i ^ bits) for i in range(n)])  9.59 us
    ppermute x10, waiting for transfers between devices, chain_scatter(): move = lambda value, perm: lax.ppermute(value, 'tensor', perm)  7.9 us
    ppermute x9, waiting for transfers between devices, swap(): return lax.ppermute(piece, axis, [(i, i ^ bits) for i in range(n)])  4.08 us
    pallas_call x1, Pallas kernels, pack_hidden(): pl.pallas_call(functools.partial(pack_hidden_kernel, n_dp, order), out_sh...  2.87 us
    pallas_call x1, Pallas kernels, project(): pl.pallas_call(functools.partial(project_kernel, len(pieces), order), out...  2.39 us
    pallas_call x2, Pallas kernels, store(): pl.pallas_call(functools.partial(store_kernel, part), out_shape=jax.Shape...  1.61 us
    pallas_call x1, Pallas kernels, pack_qkv(): pl.pallas_call(functools.partial(pack_qkv_kernel, width // HD), out_shape...  1.56 us
  transfers between devices with their start and end apart: 19, of which 10 were waited for; matrix products, arithmetic and copies ran while one was open for 0% of the time, Pallas kernels for 15%

profile of v6, /device:TPU:0, one launch (start us, length us, event | category | flops | bytes accessed | tf_op | source)
XLA Modules:
  0.0 55.8 jit_solution(17744369309970343893)
XLA Ops:
  0.6 0.0 copy-start
  0.6 1.6 %pack_qkv.1 = (bf16[32,1280]{1,0:T(8,128)(2,1)S(1)}, bf16[32,1280]{1,0:T(8,128)(2,1)S(1)}, bf16[32,1280]{1,0:T(8,128)(2,1)S(1)}, bf16[32,1280]{1,0:T(8,128)(2,1)S(1)}) custom-call(s32[1,128]{1,0:T(1,128)} %send_ref.3, bf16[128,1024]{1,0:T(8,128)(2,1)} %q_ref.1, bf16[128,2,512]{2,1,0:T(2,128)(2,1)} %kv_ref.1), custom_call_target="tpu_custom_call" | custom-call | tf_op jit(solution)/shard_map/pack_qkv/pallas_call | solution.py:79
  2.2 0.0 copy-start.2
  2.2 0.0 copy-start.1
  2.2 3.0 %collective-permute-start = (bf16[32,1280]{1,0:T(8,128)(2,1)S(1)}, bf16[32,1280]{1,0:T(8,128)(2,1)S(1)}, u32[]{:S(2)}, u32[]{:S(2)}) collective-permute-start(bf16[32,1280]{1,0:T(8,128)(2,1)S(1)} %get-tuple-element.53), channel_id=1, source_target_pairs={{0,8},{4,12},{8,0},{12,4},{1,9},{5,13},{9,1},{13,5},{2,10},{6,14},... | collective-permute-start | bytes 245768 | tf_op jit(solution)/shard_map/ppermute | solution.py:394
  5.2 0.0 collective-permute-start.1
  5.2 0.2 collective-permute-start.2
  5.4 2.9 %pack_hidden.1 = (bf16[32,2048]{1,0:T(8,128)(2,1)S(1)}, bf16[32,2048]{1,0:T(8,128)(2,1)S(1)}, bf16[32,2048]{1,0:T(8,128)(2,1)S(1)}, bf16[32,2048]{1,0:T(8,128)(2...) custom-call(s32[1,8]{1,0:T(1,128)} %len_ref.1, s32[1,128]{1,0:T(1,128)} %send_ref.3, ...), custom_call_target="tpu_custom_call" | custom-call | tf_op jit(solution)/shard_map/pack_hidden/pallas_call | solution.py:153
  8.3 0.0 collective-permute-done.refs_1_
  8.3 0.0 collective-permute-done.1.refs_2_
  8.3 1.0 %collective-permute-done.2.refs_3_ = bf16[32,1280]{1,0:T(8,128)(2,1)S(1)} collective-permute-done((bf16[32,1280]{1,0:T(8,128)(2,1)S(1)}, bf16[32,1280]{1,0:T(8,128)(2,1)S(1)}, u32[]{:S(2)}, u32[]{:S(2)}) %collective-permute-start.2) | collective-permute-done | bytes 81952 | tf_op jit(solution)/shard_map/ppermute | solution.py:394
  9.3 0.9 %attend_first.1 = (bf16[128,1024]{1,0:T(8,128)(2,1)S(1)}, bf16[128,1024]{1,0:T(8,128)(2,1)S(1)}) custom-call(f32[128,128]{1,0:T(8,128)S(1)} %get-tuple-element.51.mask_ref, bf16[32,1280]{1,0:T(8,128)(2,1)S(1)} %get-tuple-element.52.refs_0_, bf16[32,1280]{1,0:T(8,128)(2,1)S(1)} %collective-permute-done.refs_1_, ...), custom_call_target="tpu_custom_call" | custom-call | tf_op jit(solution)/shard_map/attend_first/pallas_call | solution.py:237
  10.3 2.6 %collective-permute-start.4 = (bf16[128,1024]{1,0:T(8,128)(2,1)S(1)}, bf16[128,1024]{1,0:T(8,128)(2,1)S(1)}, u32[]{:S(2)}, u32[]{:S(2)}) collective-permute-start(bf16[128,1024]{1,0:T(8,128)(2,1)S(1)} %get-tuple-element.60), channel_id=1, source_target_pairs={{0,1},{3,2},{4,5},{7,6},{8,9},{11,10},{12,13},{15,14},{16,17},{19,... | collective-permute-start | bytes 786440 | tf_op jit(solution)/shard_map/ppermute | solution.py:432
  12.8 0.0 copy-done
  12.8 2.4 %project.1 = (bf16[128,1024]{1,0:T(8,128)(2,1)S(1)}, bf16[128,1024]{1,0:T(8,128)(2,1)S(1)}, bf16[128,1024]{1,0:T(8,128)(2,1)S(1)}, bf16[128,1024]{1,0:T(8,128)(2...) custom-call(f32[128,128]{1,0:T(8,128)S(1)} %get-tuple-element.51.mas, ...), custom_call_target="tpu_custom_call" | custom-call | flops 2147483648 | bytes 16777216 | tf_op jit(solution)/shard_map/project/pallas_call | solution.py:271
  15.2 1.9 %collective-permute-start.3 = (bf16[128,1024]{1,0:T(8,128)(2,1)S(1)}, bf16[128,1024]{1,0:T(8,128)(2,1)S(1)}, u32[]{:S(2)}, u32[]{:S(2)}) collective-permute-start(bf16[128,1024]{1,0:T(8,128)(2,1)S(1)} %get-tuple-element.58.refs_0_), channel_id=1, source_target_pairs={{0,1},{3,2},{4,5},{7,6},{8,9},{11,10},{12,13},{15,14},{16,17},{19,... | collective-permute-start | bytes 786440 | tf_op jit(solution)/shard_map/ppermute | solution.py:432
  17.2 0.3 collective-permute-start.5
  17.4 1.4 %collective-permute-start.6 = (bf16[32,2048]{1,0:T(8,128)(2,1)S(1)}, bf16[32,2048]{1,0:T(8,128)(2,1)S(1)}, u32[]{:S(2)}, u32[]{:S(2)}) collective-permute-start(bf16[32,2048]{1,0:T(8,128)(2,1)S(1)} %get-tuple-element.66), channel_id=1, source_target_pairs={{0,8},{4,12},{8,0},{12,4},{1,9},{5,13},{9,1},{13,5},{2,10},{6,14},... | collective-permute-start | bytes 393224 | tf_op jit(solution)/shard_map/ppermute | solution.py:394
  18.8 0.3 collective-permute-start.7
  19.1 0.3 collective-permute-done.4.refs_1_
  19.4 0.1 add.30
  19.5 4.4 %collective-permute-start.8 = (bf16[128,1024]{1,0:T(8,128)(2,1)S(1)}, bf16[128,1024]{1,0:T(8,128)(2,1)S(1)}, u32[]{:S(2)}, u32[]{:S(2)}) collective-permute-start(bf16[128,1024]{1,0:T(8,128)(2,1)S(1)} %get-tuple-element.69.refs_0_), channel_id=1, source_target_pairs={{0,1},{3,2},{4,5},{7,6},{8,9},{11,10},{12,13},{15,14},{16,17},{19,... | collective-permute-start | bytes 786440 | tf_op jit(solution)/shard_map/ppermute | solution.py:432
  23.9 0.0 collective-permute-done.5.refs_4_
  23.9 0.7 %collective-permute-start.9 = (bf16[128,1024]{1,0:T(8,128)(2,1)S(1)}, bf16[128,1024]{1,0:T(8,128)(2,1)S(1)}, u32[]{:S(2)}, u32[]{:S(2)}) collective-permute-start(bf16[128,1024]{1,0:T(8,128)(2,1)S(1)} %get-tuple-element.71), channel_id=1, source_target_pairs={{1,2},{2,1},{5,6},{6,5},{9,10},{10,9},{13,14},{14,13},{17,18},{18,... | collective-permute-start | bytes 786440 | tf_op jit(solution)/shard_map/ppermute | solution.py:432
  24.6 0.0 collective-permute-done.6.refs_5_
  24.6 0.7 %collective-permute-done.7.refs_6_ = bf16[32,2048]{1,0:T(8,128)(2,1)S(1)} collective-permute-done((bf16[32,2048]{1,0:T(8,128)(2,1)S(1)}, bf16[32,2048]{1,0:T(8,128)(2,1)S(1)}, u32[]{:S(2)}, u32[]{:S(2)}) %collective-permute-start.7) | collective-permute-done | bytes 131104 | tf_op jit(solution)/shard_map/ppermute | solution.py:394
  25.3 0.0 collective-permute-done.3.refs_1_
  25.3 0.1 add.31
  25.4 4.1 %collective-permute-start.10 = (bf16[128,1024]{1,0:T(8,128)(2,1)S(1)}, bf16[128,1024]{1,0:T(8,128)(2,1)S(1)}, u32[]{:S(2)}, u32[]{:S(2)}) collective-permute-start(bf16[128,1024]{1,0:T(8,128)(2,1)S(1)} %get-tuple-element.68.refs_0_), channel_id=1, source_target_pairs={{0,1},{3,2},{4,5},{7,6},{8,9},{11,10},{12,13},{15,14},{16,17},{19,... | collective-permute-start | bytes 786440 | tf_op jit(solution)/shard_map/ppermute | solution.py:432
  29.5 0.7 %collective-permute-start.11 = (bf16[128,1024]{1,0:T(8,128)(2,1)S(1)}, bf16[128,1024]{1,0:T(8,128)(2,1)S(1)}, u32[]{:S(2)}, u32[]{:S(2)}) collective-permute-start(bf16[128,1024]{1,0:T(8,128)(2,1)S(1)} %get-tuple-element.74), channel_id=1, source_target_pairs={{1,2},{2,1},{5,6},{6,5},{9,10},{10,9},{13,14},{14,13},{17,18},{18,... | collective-permute-start | bytes 786440 | tf_op jit(solution)/shard_map/ppermute | solution.py:432
  30.2 0.5 collective-permute-done.8.refs_2_
  30.7 0.0 collective-permute-done.9.refs_3_
  30.7 0.1 add.32
  30.8 2.5 %collective-permute-start.14 = (bf16[128,1024]{1,0:T(8,128)(2,1)S(1)}, bf16[128,1024]{1,0:T(8,128)(2,1)S(1)}, u32[]{:S(2)}, u32[]{:S(2)}) collective-permute-start(bf16[128,1024]{1,0:T(8,128)(2,1)S(1)} %get-tuple-element.82), channel_id=1, source_target_pairs={{0,1},{1,0},{2,3},{3,2},{4,5},{5,4},{6,7},{7,6},{8,9},{9,8},{10,11... | collective-permute-start | bytes 786440 | tf_op jit(solution)/shard_map/ppermute | solution.py:432
  33.3 0.7 %collective-permute-start.15 = (bf16[128,1024]{1,0:T(8,128)(2,1)S(1)}, bf16[128,1024]{1,0:T(8,128)(2,1)S(1)}, u32[]{:S(2)}, u32[]{:S(2)}) collective-permute-start(bf16[128,1024]{1,0:T(8,128)(2,1)S(1)} %get-tuple-element.83), channel_id=1, source_target_pairs={{1,2},{2,1},{5,6},{6,5},{9,10},{10,9},{13,14},{14,13},{17,18},{18,... | collective-permute-start | bytes 786440 | tf_op jit(solution)/shard_map/ppermute | solution.py:432
  34.0 2.3 %collective-permute-done.10.refs_2_ = bf16[128,1024]{1,0:T(8,128)(2,1)S(1)} collective-permute-done((bf16[128,1024]{1,0:T(8,128)(2,1)S(1)}, bf16[128,1024]{1,0:T(8,128)(2,1)S(1)}, u32[]{:S(2)}, u32[]{:S(2)}) %collective-permute-start.10) | collective-permute-done | bytes 262176 | tf_op jit(solution)/shard_map/ppermute | solution.py:432
  36.3 0.0 collective-permute-done.11.refs_3_
  36.3 0.8 %add.33 = (bf16[128,1024]{1,0:T(8,128)(2,1)S(1)}, bf16[128,1024]{1,0:T(8,128)(2,1)}) custom-call(bf16[128,1024]{1,0:T(8,128)(2,1)S(1)} %get-tuple-element.68.refs_0_, bf16[128,1024]{1,0:T(8,128)(2,1)S(1)} %get-tuple-element.73.refs_1_, bf16[128,1024]{1,0:T(8,128)(2,1)S(1)} %collective-permute-done.10.refs_2_, ...), custom_call_target="tpu_custom_call" | custom-call | tf_op jit(solution)/shard_map/add/pallas_call | solution.py:297
  37.0 3.2 %collective-permute-start.12 = (bf16[128,1024]{1,0:T(8,128)(2,1)}, bf16[128,1024]{1,0:T(8,128)(2,1)S(1)}, u32[]{:S(2)}, u32[]{:S(2)}) collective-permute-start(bf16[128,1024]{1,0:T(8,128)(2,1)} %get-tuple-element.75), channel_id=1, source_target_pairs={{0,1},{1,0},{2,3},{3,2},{4,5},{5,4},{6,7},{7,6},{8,9},{9,8},{10,11... | collective-permute-start | bytes 786440 | tf_op jit(solution)/shard_map/ppermute | solution.py:432
  40.3 0.7 %collective-permute-start.13 = (bf16[128,1024]{1,0:T(8,128)(2,1)S(1)}, bf16[128,1024]{1,0:T(8,128)(2,1)S(1)}, u32[]{:S(2)}, u32[]{:S(2)}) collective-permute-start(bf16[128,1024]{1,0:T(8,128)(2,1)S(1)} %get-tuple-element.76), channel_id=1, source_target_pairs={{1,2},{2,1},{5,6},{6,5},{9,10},{10,9},{13,14},{14,13},{17,18},{18,... | collective-permute-start | bytes 786440 | tf_op jit(solution)/shard_map/ppermute | solution.py:432
  41.0 0.0 copy-done.2
  41.0 0.1 copy.21.scale_ref
  41.1 0.0 copy-done.1
  41.1 0.8 %collective-permute-done.14.recv_r = bf16[128,1024]{1,0:T(8,128)(2,1)S(1)} collective-permute-done((bf16[128,1024]{1,0:T(8,128)(2,1)S(1)}, bf16[128,1024]{1,0:T(8,128)(2,1)S(1)}, u32[]{:S(2)}, u32[]{:S(2)}) %collective-permute-start.14) | collective-permute-done | bytes 262176 | tf_op jit(solution)/shard_map/ppermute | solution.py:432
  41.9 0.0 collective-permute-done.15.recv_l
  41.9 0.4 finish.2
  42.3 0.8 %store.2.refs_5_ = f32[128,2048]{1,0:T(8,128)} custom-call(f32[128,1024]{1,0:T(8,128)S(1)} %get-tuple-element.86.value_ref), custom_call_target="tpu_custom_call" | custom-call | bytes 524288 | tf_op jit(solution)/shard_map/store/pallas_call | solution.py:378
  43.1 4.1 %collective-permute-done.12.recv_r = bf16[128,1024]{1,0:T(8,128)(2,1)S(1)} collective-permute-done((bf16[128,1024]{1,0:T(8,128)(2,1)}, bf16[128,1024]{1,0:T(8,128)(2,1)S(1)}, u32[]{:S(2)}, u32[]{:S(2)}) %collective-permute-start.12) | collective-permute-done | bytes 262176 | tf_op jit(solution)/shard_map/ppermute | solution.py:432
  47.2 0.0 collective-permute-done.13.recv_l
  47.2 0.4 finish.3
  47.6 2.7 %collective-permute-start.16 = (f32[8,128]{1,0:T(8,128)S(1)}, f32[8,128]{1,0:T(8,128)S(1)}, u32[]{:S(2)}, u32[]{:S(2)}) collective-permute-start(f32[8,128]{1,0:T(8,128)S(1)} %get-tuple-element.89), channel_id=1, source_target_pairs={{0,3},{1,2},{2,1},{3,0},{4,7},{5,6},{6,5},{7,4},{8,11},{9,10},{10,... | collective-permute-start | bytes 12296 | tf_op jit(solution)/shard_map/ppermute | solution.py:394
  50.3 1.3 %collective-permute-start.17 = (f32[8,128]{1,0:T(8,128)S(1)}, f32[8,128]{1,0:T(8,128)S(1)}, u32[]{:S(2)}, u32[]{:S(2)}) collective-permute-start(f32[8,128]{1,0:T(8,128)S(1)} %get-tuple-element.89), channel_id=1, source_target_pairs={{0,2},{1,3},{2,0},{3,1},{4,6},{5,7},{6,4},{7,5},{8,10},{9,11},{10,... | collective-permute-start | bytes 12296 | tf_op jit(solution)/shard_map/ppermute | solution.py:394
  51.6 0.5 collective-permute-start.18
  52.1 0.8 %store.3 = f32[128,2048]{1,0:T(8,128)} custom-call(f32[128,1024]{1,0:T(8,128)S(1)} %get-tuple-element.87.value_ref, f32[128,2048]{1,0:T(8,128)} %get-tuple-element.88.refs_0_), custom_call_target="tpu_custom_call", output_to_operand_aliasing={{}: (1, {})} | custom-call | bytes 524288 | tf_op jit(solution)/shard_map/store/pallas_call | solution.py:378
  52.9 0.2 collective-permute-done.16
  53.1 1.7 %collective-permute-done.17 = f32[8,128]{1,0:T(8,128)S(1)} collective-permute-done((f32[8,128]{1,0:T(8,128)S(1)}, f32[8,128]{1,0:T(8,128)S(1)}, u32[]{:S(2)}, u32[]{:S(2)}) %collective-permute-start.17) | collective-permute-done | bytes 4128 | tf_op jit(solution)/shard_map/ppermute | solution.py:394
  54.8 0.4 collective-permute-done.18
  55.2 0.5 multiply_bitcast_fusion
  (2 shorter events, 0.0 us)
Async XLA Ops:
  0.6 12.2 %copy-start = (bf16[1024,8192]{1,0:T(8,128)(2,1)S(1)}, bf16[1024,8192]{1,0:T(8,128)(2,1)}, u32[]{:S(2)}) copy-start(bf16[1024,8192]{1,0:T(8,128)(2,1)} %w_ref.3) | copy-start | bytes 50331652
  2.2 38.8 %copy-start.2 = (bf16[128,16]{0,1:T(8,128)(2,1)S(1)}, bf16[128,16]{0,1:T(8,128)(2,1)}, u32[]{:S(2)}) copy-start(bf16[128,16]{0,1:T(8,128)(2,1)} %param.14) | copy-start | bytes 12292
  2.2 38.9 %copy-start.1 = (bf16[8192]{0:T(1024)(128)(2,1)S(1)}, bf16[8192]{0:T(1024)(128)(2,1)}, u32[]{:S(2)}) copy-start(bf16[8192]{0:T(1024)(128)(2,1)} %param.15) | copy-start | bytes 49156
  2.2 6.1 %collective-permute-start = (bf16[32,1280]{1,0:T(8,128)(2,1)S(1)}, bf16[32,1280]{1,0:T(8,128)(2,1)S(1)}, u32[]{:S(2)}, u32[]{:S(2)}) collective-permute-start(bf16[32,1280]{1,0:T(8,128)(2,1)S(1)} %get-tuple-element.53), channel_id=1, source_target_pairs={{0,8},{4,12},{8,0},{12,4},{1,9},{5,13},{9,1},{13,5},{2,10},{6,14},... | collective-permute-start | bytes 245768 | tf_op jit(solution)/shard_map/ppermute | solution.py:394
  5.2 3.1 %collective-permute-start.1 = (bf16[32,1280]{1,0:T(8,128)(2,1)S(1)}, bf16[32,1280]{1,0:T(8,128)(2,1)S(1)}, u32[]{:S(2)}, u32[]{:S(2)}) collective-permute-start(bf16[32,1280]{1,0:T(8,128)(2,1)S(1)} %get-tuple-element.54), channel_id=1, source_target_pairs={{0,4},{4,0},{8,12},{12,8},{1,5},{5,1},{9,13},{13,9},{2,6},{6,2},{1... | collective-permute-start | bytes 245768 | tf_op jit(solution)/shard_map/ppermute | solution.py:394
  5.2 4.1 %collective-permute-start.2 = (bf16[32,1280]{1,0:T(8,128)(2,1)S(1)}, bf16[32,1280]{1,0:T(8,128)(2,1)S(1)}, u32[]{:S(2)}, u32[]{:S(2)}) collective-permute-start(bf16[32,1280]{1,0:T(8,128)(2,1)S(1)} %get-tuple-element.55), channel_id=1, source_target_pairs={{0,12},{4,8},{8,4},{12,0},{1,13},{5,9},{9,5},{13,1},{2,14},{6,10},... | collective-permute-start | bytes 245768 | tf_op jit(solution)/shard_map/ppermute | solution.py:394
  10.3 9.2 %collective-permute-start.4 = (bf16[128,1024]{1,0:T(8,128)(2,1)S(1)}, bf16[128,1024]{1,0:T(8,128)(2,1)S(1)}, u32[]{:S(2)}, u32[]{:S(2)}) collective-permute-start(bf16[128,1024]{1,0:T(8,128)(2,1)S(1)} %get-tuple-element.60), channel_id=1, source_target_pairs={{0,1},{3,2},{4,5},{7,6},{8,9},{11,10},{12,13},{15,14},{16,17},{19,... | collective-permute-start | bytes 786440 | tf_op jit(solution)/shard_map/ppermute | solution.py:432
  15.2 10.1 %collective-permute-start.3 = (bf16[128,1024]{1,0:T(8,128)(2,1)S(1)}, bf16[128,1024]{1,0:T(8,128)(2,1)S(1)}, u32[]{:S(2)}, u32[]{:S(2)}) collective-permute-start(bf16[128,1024]{1,0:T(8,128)(2,1)S(1)} %get-tuple-element.58.refs_0_), channel_id=1, source_target_pairs={{0,1},{3,2},{4,5},{7,6},{8,9},{11,10},{12,13},{15,14},{16,17},{19,... | collective-permute-start | bytes 786440 | tf_op jit(solution)/shard_map/ppermute | solution.py:432
  17.2 6.7 %collective-permute-start.5 = (bf16[32,2048]{1,0:T(8,128)(2,1)S(1)}, bf16[32,2048]{1,0:T(8,128)(2,1)S(1)}, u32[]{:S(2)}, u32[]{:S(2)}) collective-permute-start(bf16[32,2048]{1,0:T(8,128)(2,1)S(1)} %get-tuple-element.65), channel_id=1, source_target_pairs={{0,4},{4,0},{8,12},{12,8},{1,5},{5,1},{9,13},{13,9},{2,6},{6,2},{1... | collective-permute-start | bytes 393224 | tf_op jit(solution)/shard_map/ppermute | solution.py:394
  17.4 7.2 %collective-permute-start.6 = (bf16[32,2048]{1,0:T(8,128)(2,1)S(1)}, bf16[32,2048]{1,0:T(8,128)(2,1)S(1)}, u32[]{:S(2)}, u32[]{:S(2)}) collective-permute-start(bf16[32,2048]{1,0:T(8,128)(2,1)S(1)} %get-tuple-element.66), channel_id=1, source_target_pairs={{0,8},{4,12},{8,0},{12,4},{1,9},{5,13},{9,1},{13,5},{2,10},{6,14},... | collective-permute-start | bytes 393224 | tf_op jit(solution)/shard_map/ppermute | solution.py:394
  18.8 6.5 %collective-permute-start.7 = (bf16[32,2048]{1,0:T(8,128)(2,1)S(1)}, bf16[32,2048]{1,0:T(8,128)(2,1)S(1)}, u32[]{:S(2)}, u32[]{:S(2)}) collective-permute-start(bf16[32,2048]{1,0:T(8,128)(2,1)S(1)} %get-tuple-element.67), channel_id=1, source_target_pairs={{0,12},{4,8},{8,4},{12,0},{1,13},{5,9},{9,5},{13,1},{2,14},{6,10},... | collective-permute-start | bytes 393224 | tf_op jit(solution)/shard_map/ppermute | solution.py:394
  19.5 11.2 %collective-permute-start.8 = (bf16[128,1024]{1,0:T(8,128)(2,1)S(1)}, bf16[128,1024]{1,0:T(8,128)(2,1)S(1)}, u32[]{:S(2)}, u32[]{:S(2)}) collective-permute-start(bf16[128,1024]{1,0:T(8,128)(2,1)S(1)} %get-tuple-element.69.refs_0_), channel_id=1, source_target_pairs={{0,1},{3,2},{4,5},{7,6},{8,9},{11,10},{12,13},{15,14},{16,17},{19,... | collective-permute-start | bytes 786440 | tf_op jit(solution)/shard_map/ppermute | solution.py:432
  23.9 6.8 %collective-permute-start.9 = (bf16[128,1024]{1,0:T(8,128)(2,1)S(1)}, bf16[128,1024]{1,0:T(8,128)(2,1)S(1)}, u32[]{:S(2)}, u32[]{:S(2)}) collective-permute-start(bf16[128,1024]{1,0:T(8,128)(2,1)S(1)} %get-tuple-element.71), channel_id=1, source_target_pairs={{1,2},{2,1},{5,6},{6,5},{9,10},{10,9},{13,14},{14,13},{17,18},{18,... | collective-permute-start | bytes 786440 | tf_op jit(solution)/shard_map/ppermute | solution.py:432
  25.4 10.9 %collective-permute-start.10 = (bf16[128,1024]{1,0:T(8,128)(2,1)S(1)}, bf16[128,1024]{1,0:T(8,128)(2,1)S(1)}, u32[]{:S(2)}, u32[]{:S(2)}) collective-permute-start(bf16[128,1024]{1,0:T(8,128)(2,1)S(1)} %get-tuple-element.68.refs_0_), channel_id=1, source_target_pairs={{0,1},{3,2},{4,5},{7,6},{8,9},{11,10},{12,13},{15,14},{16,17},{19,... | collective-permute-start | bytes 786440 | tf_op jit(solution)/shard_map/ppermute | solution.py:432
  29.5 6.8 %collective-permute-start.11 = (bf16[128,1024]{1,0:T(8,128)(2,1)S(1)}, bf16[128,1024]{1,0:T(8,128)(2,1)S(1)}, u32[]{:S(2)}, u32[]{:S(2)}) collective-permute-start(bf16[128,1024]{1,0:T(8,128)(2,1)S(1)} %get-tuple-element.74), channel_id=1, source_target_pairs={{1,2},{2,1},{5,6},{6,5},{9,10},{10,9},{13,14},{14,13},{17,18},{18,... | collective-permute-start | bytes 786440 | tf_op jit(solution)/shard_map/ppermute | solution.py:432
  30.8 11.1 %collective-permute-start.14 = (bf16[128,1024]{1,0:T(8,128)(2,1)S(1)}, bf16[128,1024]{1,0:T(8,128)(2,1)S(1)}, u32[]{:S(2)}, u32[]{:S(2)}) collective-permute-start(bf16[128,1024]{1,0:T(8,128)(2,1)S(1)} %get-tuple-element.82), channel_id=1, source_target_pairs={{0,1},{1,0},{2,3},{3,2},{4,5},{5,4},{6,7},{7,6},{8,9},{9,8},{10,11... | collective-permute-start | bytes 786440 | tf_op jit(solution)/shard_map/ppermute | solution.py:432
  33.3 8.6 %collective-permute-start.15 = (bf16[128,1024]{1,0:T(8,128)(2,1)S(1)}, bf16[128,1024]{1,0:T(8,128)(2,1)S(1)}, u32[]{:S(2)}, u32[]{:S(2)}) collective-permute-start(bf16[128,1024]{1,0:T(8,128)(2,1)S(1)} %get-tuple-element.83), channel_id=1, source_target_pairs={{1,2},{2,1},{5,6},{6,5},{9,10},{10,9},{13,14},{14,13},{17,18},{18,... | collective-permute-start | bytes 786440 | tf_op jit(solution)/shard_map/ppermute | solution.py:432
  37.0 10.1 %collective-permute-start.12 = (bf16[128,1024]{1,0:T(8,128)(2,1)}, bf16[128,1024]{1,0:T(8,128)(2,1)S(1)}, u32[]{:S(2)}, u32[]{:S(2)}) collective-permute-start(bf16[128,1024]{1,0:T(8,128)(2,1)} %get-tuple-element.75), channel_id=1, source_target_pairs={{0,1},{1,0},{2,3},{3,2},{4,5},{5,4},{6,7},{7,6},{8,9},{9,8},{10,11... | collective-permute-start | bytes 786440 | tf_op jit(solution)/shard_map/ppermute | solution.py:432
  40.3 6.9 %collective-permute-start.13 = (bf16[128,1024]{1,0:T(8,128)(2,1)S(1)}, bf16[128,1024]{1,0:T(8,128)(2,1)S(1)}, u32[]{:S(2)}, u32[]{:S(2)}) collective-permute-start(bf16[128,1024]{1,0:T(8,128)(2,1)S(1)} %get-tuple-element.76), channel_id=1, source_target_pairs={{1,2},{2,1},{5,6},{6,5},{9,10},{10,9},{13,14},{14,13},{17,18},{18,... | collective-permute-start | bytes 786440 | tf_op jit(solution)/shard_map/ppermute | solution.py:432
  47.6 5.5 %collective-permute-start.16 = (f32[8,128]{1,0:T(8,128)S(1)}, f32[8,128]{1,0:T(8,128)S(1)}, u32[]{:S(2)}, u32[]{:S(2)}) collective-permute-start(f32[8,128]{1,0:T(8,128)S(1)} %get-tuple-element.89), channel_id=1, source_target_pairs={{0,3},{1,2},{2,1},{3,0},{4,7},{5,6},{6,5},{7,4},{8,11},{9,10},{10,... | collective-permute-start | bytes 12296 | tf_op jit(solution)/shard_map/ppermute | solution.py:394
  50.3 4.5 %collective-permute-start.17 = (f32[8,128]{1,0:T(8,128)S(1)}, f32[8,128]{1,0:T(8,128)S(1)}, u32[]{:S(2)}, u32[]{:S(2)}) collective-permute-start(f32[8,128]{1,0:T(8,128)S(1)} %get-tuple-element.89), channel_id=1, source_target_pairs={{0,2},{1,3},{2,0},{3,1},{4,6},{5,7},{6,4},{7,5},{8,10},{9,11},{10,... | collective-permute-start | bytes 12296 | tf_op jit(solution)/shard_map/ppermute | solution.py:394
  51.6 3.6 %collective-permute-start.18 = (f32[8,128]{1,0:T(8,128)S(1)}, f32[8,128]{1,0:T(8,128)S(1)}, u32[]{:S(2)}, u32[]{:S(2)}) collective-permute-start(f32[8,128]{1,0:T(8,128)S(1)} %get-tuple-element.89), channel_id=1, source_target_pairs={{0,1},{1,0},{2,3},{3,2},{4,5},{5,4},{6,7},{7,6},{8,9},{9,8},{10,11... | collective-permute-start | bytes 12296 | tf_op jit(solution)/shard_map/ppermute | solution.py:394
